TPU v7x, 32 devices: a whole 2x2x4 slice. The times are simulated.
32 devices in a mesh: head: 4 (over z), seq: 8 (over y, x, core).
Axes of the slice: x: 2, y: 2, z: 4, core: 2. Of those that a mesh axis runs over, the one named last changes fastest.
Arguments:
- inputs: bfloat16 [2048, 2048], P('seq', 'head'), may hold values from -6 to 6
- cotangent: bfloat16 [2048, 2048], P('seq', 'head'), may hold values from -6 to 6
- owners: int32 [261], replicated, may hold values from 0 to 7, as said below
- master: float32 [352, 262144], P('seq', 'head'), may hold values from -16 to 16
- moment_one: float32 [352, 262144], P('seq', 'head')
- moment_two: float32 [352, 262144], P('seq', 'head'), as said below
Outputs:
- block_out: bfloat16 [2048, 2048], P('seq', 'head')
- input_grad: float32 [2048, 2048], P('seq', 'head')
- grad_slots: float32 [352, 262144], P('seq', 'head')
- master_new: float32 [352, 262144], P('seq', 'head')
- moment_one_new: float32 [352, 262144], P('seq', 'head')
- moment_two_new: float32 [352, 262144], P('seq', 'head')
- weights_low: bfloat16 [352, 262144], P('seq', 'head')
Inputs may be any that keep to these rules, and one draw needn't show every extreme that they name: owners[p] is the index along seq of the device that keeps block p of every head shard; no index appears more than 44 times and some index exactly 44 times. `moment_two`: every entry is positive.
All inputs are finite; a program needn't handle non-finite values.
Results may differ from a plain program's by a relative error of at most 0.019.
Values may be sent and summed in bfloat16 or wider, within the bound.
No kernel may reach another device: no remote copies, remote signals or barrier semaphores. Data moves between devices by JAX's collectives and lax.ppermute only.
A program may use at most 1.1875 GiB of HBM per device.

v0:
```python
import jax
import jax.numpy as jnp
import numpy as np
from jax import lax
from jax.experimental import pallas as pl
from jax.experimental.pallas import tpu as pltpu
from jax.sharding import PartitionSpec as P

D = 2048
HEADS = 16
DK = 128
DV = 256
FF = 5632
KCONV = 4
STEP = 5


EXACT_ARITHMETIC = lax.Precision.HIGHEST
NORM_EPSILON = 1e-06
UNIT_EPSILON = 1e-06
HEAD_EPSILON = 1e-05
ADAM_EPSILON = 1e-08
BETA_ONE = 0.5
BETA_TWO = 0.5
WEIGHT_DECAY = 0.1
PAD_RATE = 0.1


def shifted(block, axis, distance):
    devices = range(lax.axis_size(axis))
    route = [(i - distance, i) for i in devices if i - distance in devices]
    return lax.ppermute(block, axis, route)


def shard_layout(local_heads, head_parts):
    return [
        ("wq", D, local_heads * DK, 0.02),
        ("wk", D, local_heads * DK, 0.02),
        ("wv", D, local_heads * DV, 0.02),
        ("wg", D, local_heads * DV, 0.02),
        ("wo", local_heads * DV, D, 0.015),
        ("wgate", D, FF // head_parts, 0.02),
        ("wup", D, FF // head_parts, 0.02),
        ("wdown", FF // head_parts, D, 0.012),
        ("cq", KCONV, local_heads * DK, 0.4),
        ("ck", KCONV, local_heads * DK, 0.4),
        ("cv", KCONV, local_heads * DV, 0.4),
        ("wab", D, 2 * local_heads, 0.04),
        ("alog", 1, local_heads, 0.5),
        ("dtbias", 1, local_heads, 0.5),
        ("gainone", 1, D // head_parts, 0.1),
        ("gaintwo", 1, D // head_parts, 0.1),
        ("wnorm", 1, DV // head_parts, 0.1),
    ]


def piece_table(owners, seq_parts, capacity):
    piece_count = owners.shape[0]
    devices = jnp.arange(seq_parts, dtype=jnp.int32)
    onehot = (owners[:, None] == devices[None, :]).astype(jnp.int32)
    before = jnp.cumsum(onehot, axis=0) - onehot
    rank_within = jnp.sum(before * onehot, axis=1)
    slot_of_piece = owners * capacity + rank_within
    matches = slot_of_piece[None, :] == jnp.arange(seq_parts * capacity, dtype=jnp.int32)[:, None]
    present = jnp.any(matches, axis=1)
    piece_of_slot = jnp.sum(
        matches.astype(jnp.int32) * jnp.arange(piece_count, dtype=jnp.int32)[None, :], axis=1
    )
    return (slot_of_piece, piece_of_slot, present)


def unpack(flat_weights, segments_list):
    by_name = {}
    offset_now = 0
    for seg_name, row_count, col_count, seg_rate in segments_list:
        by_name[seg_name] = flat_weights[offset_now : offset_now + row_count * col_count].reshape(
            row_count, col_count
        )
        offset_now += row_count * col_count
    return (by_name, offset_now)


def rate_parts(segments_list, piece_count, piece_size):
    piece_rates = np.full(piece_count, PAD_RATE, np.float32)
    small_rates = np.full(piece_size, PAD_RATE, np.float32)
    offset_now = 0
    big_total = (piece_count - 1) * piece_size
    for seg_name, row_count, col_count, seg_rate in segments_list:
        seg_size = row_count * col_count
        if offset_now < big_total:
            piece_rates[offset_now // piece_size : (offset_now + seg_size) // piece_size] = seg_rate
        else:
            small_rates[offset_now - big_total : offset_now - big_total + seg_size] = seg_rate
        offset_now += seg_size
    return (piece_rates, small_rates)


HEADS_A_STEP = 1


def product(left, right, left_axis, right_axis, exact=False):
    def dot(a, b):
        return lax.dot_general(
            a,
            b,
            (((left_axis,), (right_axis,)), ((), ())),
            preferred_element_type=jnp.float32,
        )

    left_low, right_low = left.astype(jnp.bfloat16), right.astype(jnp.bfloat16)
    if not exact:
        return dot(left_low, right_low)
    left_rest = (left - left_low.astype(jnp.float32)).astype(jnp.bfloat16)
    right_rest = (right - right_low.astype(jnp.float32)).astype(jnp.bfloat16)
    return dot(left_low, right_low) + (dot(left_low, right_rest) + dot(left_rest, right_low))


def take_lane(wide, lane):
    lanes = lax.broadcasted_iota(jnp.int32, wide.shape, 1)
    return jnp.sum(jnp.where(lanes == lane, wide, 0.0), axis=1, keepdims=True)


def put_lane(column, lane):
    lanes = lax.broadcasted_iota(jnp.int32, (column.shape[0], 128), 1)
    return jnp.where(lanes == lane, column, 0.0)


def to_row(column, diagonal):
    return jnp.sum(jnp.where(diagonal, column, 0.0), axis=0, keepdims=True)


def convolved(extended, taps_ref, columns):
    row_count = extended.shape[0] - RIM
    first = RIM - (KCONV - 1)
    running = taps_ref[0:1, columns] * extended[first : first + row_count, columns]
    for tap in range(1, KCONV):
        running = running + taps_ref[tap : tap + 1, columns] * extended[
            first + tap : first + tap + row_count, columns
        ]
    return running


def decay_terms(head, local_heads, decay_ref, scalars_ref):
    row_count = decay_ref.shape[0]
    shape = (row_count, row_count)
    row_ids = lax.broadcasted_iota(jnp.int32, shape, 0)
    column_ids = lax.broadcasted_iota(jnp.int32, shape, 1)
    decay_in = take_lane(decay_ref[...], head) + take_lane(scalars_ref[1:2, :], head)
    rate = -jnp.exp(take_lane(scalars_ref[0:1, :], head))
    soft = jnp.maximum(decay_in, 0.0) + jnp.log1p(jnp.exp(-jnp.abs(decay_in)))
    logs = rate * soft
    beta = jax.nn.sigmoid(take_lane(decay_ref[...], head + local_heads))
    diagonal = row_ids == column_ids
    logs_row = to_row(logs, diagonal)
    upto = row_ids >= column_ids
    sums = jnp.sum(jnp.where(upto, logs_row, 0.0), axis=1, keepdims=True)
    sums_row = to_row(sums, diagonal)
    within = jnp.exp(jnp.where(upto, sums - sums_row, -1e30))
    return decay_in, rate, logs, beta, sums, within, row_ids, column_ids


def unit_rows(rows):
    scale = lax.rsqrt(jnp.sum(rows * rows, axis=-1, keepdims=True) + UNIT_EPSILON)
    return rows * scale, scale


def mixer_specs(local_heads, row_count):
    def spec(rows, width, first):
        width *= HEADS_A_STEP
        return pl.BlockSpec((rows, width), lambda h, first=first // width: (0, first + h))

    def query(rows):
        return spec(rows, DK, 0)

    def key(rows):
        return spec(rows, DK, local_heads * DV)

    def value(rows):
        return spec(rows, DV, 0)

    whole = pl.BlockSpec((row_count, 128), lambda h: (0, 0))
    scalars = pl.BlockSpec((8, 128), lambda h: (0, 0))
    return query, key, value, whole, scalars


def per_head(*shape):
    return pl.BlockSpec((HEADS_A_STEP,) + shape, lambda h: (h,) + (0,) * len(shape))


def head_columns(sub):
    return slice(DK * sub, DK * sub + DK), slice(DV * sub, DV * sub + DV)


def mixer_local(local_heads, value_key, taps, decay_proj, scalars):
    row_count = value_key.shape[0] - RIM
    query, key, value, whole, scalar_spec = mixer_specs(local_heads, row_count)

    def kernel(
        pv, pk, tv, tk, decay_ref, scalars_ref, solve_ref, fresh_ref, wy_ref, handoff_ref
    ):
        for sub in range(HEADS_A_STEP):
            head = pl.program_id(0) * HEADS_A_STEP + sub
            narrow, wide = head_columns(sub)
            key_rows = unit_rows(jax.nn.silu(convolved(pk, tk, narrow)))[0]
            values = jax.nn.silu(convolved(pv, tv, wide))
            decay_in, rate, logs, beta, sums, within, row_ids, column_ids = decay_terms(
                head, local_heads, decay_ref, scalars_ref
            )
            gram = product(key_rows, key_rows, 1, 1, True)
            system = jnp.where(row_ids > column_ids, beta * gram * within, 0.0)
            unit = jnp.where(row_ids == column_ids, 1.0, 0.0)
            solve = unit
            size = 1
            while size < row_count:
                lower = (row_ids // (2 * size) == column_ids // (2 * size)) & (
                    row_ids // size != column_ids // size
                )
                part = jnp.where(lower, system, 0.0)
                if size == 1:
                    solve = solve - part
                else:
                    solve = solve - product(solve, product(part, solve, 1, 0), 1, 0)
                size *= 2
            remainder = (unit - solve) - product(system, solve, 1, 0, True)
            solve = solve + product(solve, remainder, 1, 0)
            grown = jnp.exp(sums)
            fresh = product(solve, beta * values, 1, 0, True)
            wy_keys = product(solve, (beta * grown) * key_rows, 1, 0, True)
            last = sums[row_count - 1 : row_count, :]
            tail_keys = jnp.exp(last - sums) * key_rows
            eye = lax.broadcasted_iota(jnp.int32, (DK, DK), 0) == lax.broadcasted_iota(
                jnp.int32, (DK, DK), 1
            )
            solve_ref[sub] = solve
            fresh_ref[sub] = fresh
            wy_ref[sub] = wy_keys
            handoff_ref[sub, :, :DK] = (
                jnp.where(eye, jnp.exp(last), 0.0) - product(tail_keys, wy_keys, 0, 0)
            ).astype(jnp.bfloat16)
            handoff_ref[sub, :, DK:] = product(tail_keys, fresh, 0, 0).astype(jnp.bfloat16)

    def out(*shape, kind=jnp.float32):
        return jax.ShapeDtypeStruct((local_heads,) + shape, kind)

    return pl.pallas_call(
        kernel,
        grid=(local_heads // HEADS_A_STEP,),
        in_specs=[
            value(RIM + row_count), key(RIM + row_count), value(8), key(8), whole, scalar_spec,
        ],
        out_specs=[
            per_head(row_count, row_count),
            per_head(row_count, DV),
            per_head(row_count, DK),
            per_head(DK, DK + DV),
        ],
        out_shape=[
            out(row_count, row_count),
            out(row_count, DV),
            out(row_count, DK),
            out(DK, DK + DV, kind=jnp.bfloat16),
        ],
        compiler_params=params(),
    )(value_key, value_key, taps, taps, decay_proj, scalars)


def mixer_reach(local_heads, query_gate, value_key, query_taps, taps, decay_proj, scalars, fresh, wy_keys):
    row_count = value_key.shape[0] - RIM
    query, key, value, whole, scalar_spec = mixer_specs(local_heads, row_count)

    def kernel(pq, pk, tq, tk, decay_ref, scalars_ref, fresh_ref, wy_ref, reach_ref, zero_ref):
        for sub in range(HEADS_A_STEP):
            head = pl.program_id(0) * HEADS_A_STEP + sub
            narrow, wide = head_columns(sub)
            queries = unit_rows(jax.nn.silu(convolved(pq, tq, narrow)))[0] * DK ** (-0.5)
            key_rows = unit_rows(jax.nn.silu(convolved(pk, tk, narrow)))[0]
            decay_in, rate, logs, beta, sums, within, row_ids, column_ids = decay_terms(
                head, local_heads, decay_ref, scalars_ref
            )
            attention = product(queries, key_rows, 1, 1) * within
            reach_ref[sub] = jnp.exp(sums) * queries - product(attention, wy_ref[sub], 1, 0)
            zero_ref[sub] = product(attention, fresh_ref[sub], 1, 0)

    return pl.pallas_call(
        kernel,
        grid=(local_heads // HEADS_A_STEP,),
        in_specs=[
            query(RIM + row_count), key(RIM + row_count), query(8), key(8), whole, scalar_spec,
            per_head(row_count, DV),
            per_head(row_count, DK),
        ],
        out_specs=[per_head(row_count, DK), per_head(row_count, DV)],
        out_shape=[
            jax.ShapeDtypeStruct((local_heads, row_count, DK), jnp.float32),
            jax.ShapeDtypeStruct((local_heads, row_count, DV), jnp.float32),
        ],
        compiler_params=params(),
    )(query_gate, value_key, query_taps, taps, decay_proj, scalars, fresh, wy_keys)


def advance_state(block, state, back):
    moved = product(block[:, :DK].astype(jnp.float32), state, 0 if back else 1, 0)
    return moved, block[:, DK:].astype(jnp.float32)


def chain_all(local_heads, my_index, handoffs, inputs, back):
    devices = handoffs.shape[0]

    def kernel(index_ref, handoffs_ref, inputs_ref, state_ref):
        state_ref[...] = jnp.zeros_like(state_ref)

        def advance(step, carry):
            j = devices - 1 - step if back else step
            for h in range(local_heads):
                moved, added = advance_state(handoffs_ref[j, h], state_ref[h], back)
                if back:
                    added = inputs_ref[j, h].astype(jnp.float32)
                state_ref[h] = moved + added
            return carry

        count = devices - 1 - index_ref[0] if back else index_ref[0]
        lax.fori_loop(0, count, advance, 0)

    vmem = pl.BlockSpec(memory_space=pltpu.VMEM)
    return pl.pallas_call(
        kernel,
        in_specs=[pl.BlockSpec(memory_space=pltpu.SMEM), vmem, vmem],
        out_specs=vmem,
        out_shape=jax.ShapeDtypeStruct((local_heads, DK, DV), jnp.float32),
        compiler_params=params(),
    )(my_index, handoffs, inputs)


def join_cores(local_heads, my_index, mine, theirs, inputs):
    half = local_heads // 2

    def kernel(index_ref, mine_ref, theirs_ref, *refs):
        out_ref = refs[-1]
        core = lax.rem(index_ref[0], 2)
        for i in range(half):
            h = core * half + i
            own, other = mine_ref[h], theirs_ref[h]
            first = jnp.where(core == 0, own, other)
            second = jnp.where(core == 0, other, own)
            if inputs:
                own, other = refs[0][h], refs[1][h]
                early = jnp.where(core == 0, own, other).astype(jnp.float32)
                late = jnp.where(core == 0, other, own).astype(jnp.float32)
                out_ref[i] = (advance_state(first, late, True)[0] + early).astype(jnp.bfloat16)
                continue
            moved, added = advance_state(second, first.astype(jnp.float32), False)
            out_ref[i, :, :DK] = moved[:, :DK].astype(jnp.bfloat16)
            out_ref[i, :, DK:] = (moved[:, DK:] + added).astype(jnp.bfloat16)

    vmem = pl.BlockSpec(memory_space=pltpu.VMEM)
    return pl.pallas_call(
        kernel,
        in_specs=[pl.BlockSpec(memory_space=pltpu.SMEM)] + [vmem] * (2 + len(inputs)),
        out_specs=vmem,
        out_shape=jax.ShapeDtypeStruct((half, DK, DV if inputs else DK + DV), jnp.bfloat16),
        compiler_params=params(),
    )(my_index, mine, theirs, *inputs)


def chain_chips(local_heads, my_index, theirs, chips, their_input, chip_inputs):
    half = local_heads // 2
    masks = len(chips) // 2
    back = their_input is not None
    flat = [theirs, *chips] + ([their_input, *chip_inputs] if back else [])

    def kernel(index_ref, *refs):
        state_ref = refs[-1]
        state_ref[...] = jnp.zeros_like(state_ref)
        core, chip = lax.rem(index_ref[0], 2), index_ref[0] // 2
        offset = 1 + len(chips)

        def update(h, block, extra):
            moved, added = advance_state(block, state_ref[h], back)
            state_ref[h] = moved + (extra.astype(jnp.float32) if back else added)

        order = range(masks, 0, -1) if back else range(masks)
        for other in order:
            for mask in range(1, masks + 1):
                here = (other ^ chip) == mask

                @pl.when(here & ((other > chip) if back else (other < chip)))
                def _():
                    for h in range(local_heads):
                        mine = core == h // half
                        pair = [refs[1 + 2 * (mask - 1) + i][h % half] for i in range(2)]
                        extra = None
                        if back:
                            extra = [
                                refs[offset + 1 + 2 * (mask - 1) + i][h % half] for i in range(2)
                            ]
                            extra = jnp.where(mine, *extra)
                        update(h, jnp.where(mine, *pair), extra)

        @pl.when(core == (0 if back else 1))
        def _():
            for h in range(local_heads):
                update(h, refs[0][h], refs[offset][h] if back else None)

    vmem = pl.BlockSpec(memory_space=pltpu.VMEM)
    return pl.pallas_call(
        kernel,
        in_specs=[pl.BlockSpec(memory_space=pltpu.SMEM)] + [vmem] * len(flat),
        out_specs=vmem,
        out_shape=jax.ShapeDtypeStruct((local_heads, DK, DV), jnp.float32),
        compiler_params=params(),
    )(my_index, *flat)


def moved_by(array, mask):
    return lax.ppermute(array, "seq", [(i, i ^ mask) for i in range(lax.axis_size("seq"))])


def pass_chips(block, beside):
    arrived = [moved_by(block, mask) for mask in (2, 4, 6)]
    arrived, beside = lax.optimization_barrier((arrived, beside))
    return [array for part in arrived for array in (part, moved_by(part, 1))], beside


def entering(local_heads, my_index, handoff, beside):
    if lax.axis_size("seq") != 8:
        handoffs = lax.all_gather(handoff, "seq", axis=0, tiled=False)
        return chain_all(local_heads, my_index, handoffs, handoffs, False), handoffs, beside
    theirs = moved_by(handoff, 1)
    chips, beside = pass_chips(join_cores(local_heads, my_index, handoff, theirs, []), beside)
    state = chain_chips(local_heads, my_index, theirs, chips, None, [])
    return state, (handoff, theirs, chips), beside


def leaving(local_heads, my_index, d_entering, kept, beside):
    if lax.axis_size("seq") != 8:
        inputs = lax.all_gather(d_entering, "seq", axis=0, tiled=False)
        return chain_all(local_heads, my_index, kept, inputs, True), beside
    handoff, theirs, chips = kept
    their_input = moved_by(d_entering, 1)
    joined = join_cores(local_heads, my_index, handoff, theirs, [d_entering, their_input])
    inputs, beside = pass_chips(joined, beside)
    return chain_chips(local_heads, my_index, theirs, chips, their_input, inputs), beside


def mixer_out(local_heads, entering_state, reach, zero_out, query_gate, norm_gain):
    row_count = query_gate.shape[0] - RIM
    gate_first = local_heads * DK

    def kernel(state_ref, reach_ref, zero_ref, gate_ref, norm_ref, out_ref, gated_ref):
        for h in range(local_heads):
            columns = slice(DV * h, DV * h + DV)
            out = zero_ref[h] + product(reach_ref[h], state_ref[h], 1, 0)
            normed = out * lax.rsqrt(jnp.mean(out * out, axis=-1, keepdims=True) + HEAD_EPSILON)
            out_ref[:, columns] = out
            gate = gate_ref[RIM:, gate_first + DV * h : gate_first + DV * h + DV]
            gated_ref[:, columns] = (normed * norm_ref[...] * jax.nn.silu(gate)).astype(
                jnp.bfloat16
            )

    vmem = pl.BlockSpec(memory_space=pltpu.VMEM)
    width = local_heads * DV
    return pl.pallas_call(
        kernel,
        in_specs=[vmem] * 5,
        out_specs=[vmem, vmem],
        out_shape=[
            jax.ShapeDtypeStruct((row_count, width), jnp.float32),
            jax.ShapeDtypeStruct((row_count, width), jnp.bfloat16),
        ],
        compiler_params=params(),
    )(entering_state, reach, zero_out, query_gate, norm_gain)


def mixer_gate_back(local_heads, d_gated, recurred, query_gate, norm_gain, reach):
    row_count = query_gate.shape[0] - RIM
    gate_first = local_heads * DK // DV

    def kernel(d_gated_ref, out_ref, gate_ref, norm_ref, reach_ref, d_out_ref, d_gate_ref, d_norm_ref, d_state_ref):
        out, gate, norm_row, d_gated_now = (
            out_ref[...], gate_ref[RIM:, :], norm_ref[...], d_gated_ref[...]
        )
        scale = lax.rsqrt(jnp.mean(out * out, axis=-1, keepdims=True) + HEAD_EPSILON)
        normed = out * scale
        logistic = jax.nn.sigmoid(gate)
        silu = gate * logistic
        d_norm = jnp.sum(d_gated_now * normed * silu, axis=0, keepdims=True)

        @pl.when(pl.program_id(0) == 0)
        def _():
            d_norm_ref[...] = jnp.zeros_like(d_norm_ref)

        d_norm_ref[0:1, :] = d_norm_ref[0:1, :] + d_norm
        d_gate_ref[...] = (
            d_gated_now * normed * norm_row * logistic * (1.0 + gate * (1.0 - logistic))
        ).astype(jnp.bfloat16)
        d_normed = d_gated_now * norm_row * silu
        d_out = scale * d_normed - (scale * scale * scale) * out * jnp.mean(
            d_normed * out, axis=-1, keepdims=True
        )
        d_out_ref[...] = d_out
        d_state_ref[0] = product(reach_ref[0], d_out, 0, 0).astype(jnp.bfloat16)

    width = local_heads * DV
    block = pl.BlockSpec((row_count, DV), lambda h: (0, h))
    return pl.pallas_call(
        kernel,
        grid=(local_heads,),
        in_specs=[
            block,
            block,
            pl.BlockSpec((RIM + row_count, DV), lambda h: (0, gate_first + h)),
            pl.BlockSpec((1, DV), lambda h: (0, 0)),
            pl.BlockSpec((1, row_count, DK), lambda h: (h, 0, 0)),
        ],
        out_specs=[
            block,
            block,
            pl.BlockSpec((8, DV), lambda h: (0, 0)),
            pl.BlockSpec((1, DK, DV), lambda h: (h, 0, 0)),
        ],
        out_shape=[
            jax.ShapeDtypeStruct((row_count, width), jnp.float32),
            jax.ShapeDtypeStruct((row_count, width), jnp.bfloat16),
            jax.ShapeDtypeStruct((8, DV), jnp.float32),
            jax.ShapeDtypeStruct((local_heads, DK, DV), jnp.bfloat16),
        ],
        compiler_params=params(),
    )(d_gated, recurred, query_gate, norm_gain, reach)


def conv_back(
    d_pre, extended, taps_ref, padded, d_block_ref, d_tail_ref, d_rim_ref, d_taps_ref, columns
):
    row_count = d_pre.shape[0]
    first = RIM - (KCONV - 1)
    padded[0:8, :] = jnp.zeros((8, d_pre.shape[1]), jnp.float32)
    padded[8 : 8 + row_count, :] = d_pre
    padded[8 + row_count : 16 + row_count, :] = jnp.zeros((8, d_pre.shape[1]), jnp.float32)
    total = None
    d_taps_ref[:, columns] = jnp.zeros((8, d_pre.shape[1]), jnp.float32)
    for tap in range(KCONV):
        start = KCONV - 1 - tap
        term = taps_ref[tap : tap + 1, columns] * padded[start : start + row_count + 8, :]
        total = term if total is None else total + term
        d_taps_ref[tap : tap + 1, columns] = jnp.sum(
            d_pre * extended[first + tap : first + tap + row_count, columns], axis=0, keepdims=True
        )
    d_rim_ref[:, columns] = total[0:8, :]
    d_block_ref[:, columns] = total[8:, :].astype(jnp.bfloat16)
    d_tail_ref[:, columns] = total[row_count:, :]


def mixer_back(
    local_heads, query_gate, value_key, query_taps, taps, decay_proj, scalars,
    solve, fresh, wy_keys, entering_state, d_recurred, d_leaving,
):
    row_count = value_key.shape[0] - RIM
    query, key, value, whole, scalar_spec = mixer_specs(local_heads, row_count)

    def kernel(
        pq, pk, pv, tq, tk, tv, decay_ref, scalars_ref,
        solve_ref, fresh_ref, wy_ref, enter_ref, d_out_ref, d_leave_ref,
        dq_ref, dk_ref, dv_ref, tail_q, tail_k, tail_v, rim_q, rim_k, rim_v,
        taps_q, taps_k, taps_v, d_decay_ref, d_scalars_ref,
        pad_q, pad_k, pad_v,
    ):
        @pl.when(pl.program_id(0) == 0)
        def _():
            d_decay_ref[...] = jnp.zeros_like(d_decay_ref)
            d_scalars_ref[...] = jnp.zeros_like(d_scalars_ref)

        for sub in range(HEADS_A_STEP):
            head = pl.program_id(0) * HEADS_A_STEP + sub
            narrow, wide = head_columns(sub)
            pre_q = convolved(pq, tq, narrow)
            pre_k = convolved(pk, tk, narrow)
            pre_v = convolved(pv, tv, wide)
            conv_q, conv_k = jax.nn.silu(pre_q), jax.nn.silu(pre_k)
            unit_q, scale_q = unit_rows(conv_q)
            queries = unit_q * DK ** (-0.5)
            key_rows, scale_k = unit_rows(conv_k)
            values = jax.nn.silu(pre_v)
            decay_in, rate, logs, beta, sums, within, row_ids, column_ids = decay_terms(
                head, local_heads, decay_ref, scalars_ref
            )
            strict = row_ids > column_ids
            grown = jnp.exp(sums)
            last = sums[row_count - 1 : row_count, :]
            tail = jnp.exp(last - sums)
            tail_keys = tail * key_rows
            gram = product(key_rows, key_rows, 1, 1, True)
            scores = jnp.where(strict, gram * within, 0.0)
            attention = product(queries, key_rows, 1, 1) * within
            enter, d_out, d_leave = enter_ref[sub], d_out_ref[:, wide], d_leave_ref[sub]
            update = fresh_ref[sub] - product(wy_ref[sub], enter, 1, 0)
            d_update = product(attention, d_out, 0, 0) + product(tail_keys, d_leave, 1, 0)
            d_right = product(solve_ref[sub], d_update, 0, 0, True)
            d_attention = product(d_out, update, 1, 1) * within
            d_system = -product(d_right, update, 1, 1)
            out_state = product(d_out, enter, 1, 1)
            right_state = product(d_right, enter, 1, 1)
            leave_update = product(update, d_leave, 1, 1)
            remainder = values - grown * product(key_rows, enter, 1, 0)
            d_values = beta * d_right
            d_beta = jnp.sum(d_right * remainder, axis=1, keepdims=True) + jnp.sum(
                d_system * scores, axis=1, keepdims=True
            )
            pair = beta * (d_system * scores)
            d_gram = jnp.where(strict, beta * d_system * within, 0.0)
            d_queries = grown * out_state + product(d_attention, key_rows, 1, 0)
            d_keys = (
                product(d_attention, queries, 0, 0)
                + product(d_gram, key_rows, 1, 0)
                + product(d_gram, key_rows, 0, 0)
                + tail * leave_update
                - (beta * grown) * right_state
            )
            both = pair + d_attention * product(queries, key_rows, 1, 1)
            tail_rows = jnp.sum(tail_keys * leave_update, axis=1, keepdims=True)
            diagonal = row_ids == column_ids
            columns = jnp.sum(both, axis=0, keepdims=True)
            d_sums = (
                jnp.sum(both, axis=1, keepdims=True)
                - jnp.sum(jnp.where(diagonal, columns, 0.0), axis=1, keepdims=True)
                + jnp.sum(out_state * (grown * queries), axis=1, keepdims=True)
                - jnp.sum(right_state * ((beta * grown) * key_rows), axis=1, keepdims=True)
                - tail_rows
            )
            d_last = jnp.exp(last) * jnp.sum(
                jnp.sum(d_leave * enter, axis=1, keepdims=True), axis=0, keepdims=True
            ) + jnp.sum(tail_rows, axis=0, keepdims=True)
            d_logs = d_last + jnp.sum(
                jnp.where(row_ids <= column_ids, to_row(d_sums, diagonal), 0.0), axis=1, keepdims=True
            )
            d_decay_in = d_logs * rate * jax.nn.sigmoid(decay_in)
            d_beta_in = d_beta * beta * (1.0 - beta)
            d_decay_ref[...] = (
                d_decay_ref[...]
                + put_lane(d_decay_in, head)
                + put_lane(d_beta_in, head + local_heads)
            )
            d_rate = jnp.sum(d_logs * logs, axis=0, keepdims=True)
            d_bias = jnp.sum(d_decay_in, axis=0, keepdims=True)
            d_scalars_ref[0:1, :] = d_scalars_ref[0:1, :] + put_lane(d_rate, head)
            d_scalars_ref[1:2, :] = d_scalars_ref[1:2, :] + put_lane(d_bias, head)

            def unit_back(d_unit, unit, scale):
                return scale * (d_unit - unit * jnp.sum(unit * d_unit, axis=1, keepdims=True))

            def silu_back(d_act, pre):
                logistic = jax.nn.sigmoid(pre)
                return d_act * logistic * (1.0 + pre * (1.0 - logistic))

            d_pre_q = silu_back(unit_back(d_queries * DK ** (-0.5), unit_q, scale_q), pre_q)
            conv_back(d_pre_q, pq, tq, pad_q.at[sub], dq_ref, tail_q, rim_q, taps_q, narrow)
            d_pre_k = silu_back(unit_back(d_keys, key_rows, scale_k), pre_k)
            conv_back(d_pre_k, pk, tk, pad_k.at[sub], dk_ref, tail_k, rim_k, taps_k, narrow)
            conv_back(
                silu_back(d_values, pre_v), pv, tv, pad_v.at[sub],
                dv_ref, tail_v, rim_v, taps_v, wide,
            )

    def blocks(rows):
        return [
            pl.BlockSpec((rows, HEADS_A_STEP * width), lambda h: (0, h)) for width in (DK, DK, DV)
        ]

    def shapes(rows, kind):
        return [
            jax.ShapeDtypeStruct((rows, local_heads * width), kind) for width in (DK, DK, DV)
        ]

    outs = pl.pallas_call(
        kernel,
        grid=(local_heads // HEADS_A_STEP,),
        in_specs=[each(RIM + row_count) for each in (query, key, value)]
        + [each(8) for each in (query, key, value)]
        + [
            whole,
            scalar_spec,
            per_head(row_count, row_count),
            per_head(row_count, DV),
            per_head(row_count, DK),
            per_head(DK, DV),
            pl.BlockSpec((row_count, HEADS_A_STEP * DV), lambda h: (0, h)),
            per_head(DK, DV),
        ],
        out_specs=blocks(row_count) + blocks(8) * 3 + [whole, scalar_spec],
        out_shape=shapes(row_count, jnp.bfloat16)
        + shapes(8, jnp.float32) * 3
        + [
            jax.ShapeDtypeStruct((row_count, 128), jnp.float32),
            jax.ShapeDtypeStruct((8, 128), jnp.float32),
        ],
        scratch_shapes=[
            pltpu.VMEM((HEADS_A_STEP, row_count + 16, DK), jnp.float32),
            pltpu.VMEM((HEADS_A_STEP, row_count + 16, DK), jnp.float32),
            pltpu.VMEM((HEADS_A_STEP, row_count + 16, DV), jnp.float32),
        ],
        compiler_params=params(),
    )(
        query_gate, value_key, value_key, query_taps, taps, taps, decay_proj, scalars,
        solve, fresh, wy_keys, entering_state, d_recurred, d_leaving,
    )
    joined = [
        (outs[3 * i], jnp.concatenate([outs[3 * i + 2], outs[3 * i + 1]], axis=1))
        for i in range(4)
    ]
    return (*joined, outs[12], outs[13])


LANES = 128
CHUNK = 32768
TILE = 16
CAPACITY_UNIT = 44
FIRST_GATHER = 24
FIRST_REDUCE = 16
SECOND_REDUCE = 20
SECOND_GATHER = 16
RIM = 16
TABLE = 1 << 16
VMEM_LIMIT = 48 * 1024 * 1024


def params(**kwargs):
    return pltpu.CompilerParams(vmem_limit_bytes=VMEM_LIMIT, **kwargs)


def piece_kinds(segments_list, piece_count, piece_size):
    kinds = np.ones(piece_count, np.int32)
    offset_now = 0
    for seg_name, row_count, col_count, seg_rate in segments_list:
        if offset_now >= (piece_count - 1) * piece_size:
            break
        tiles = col_count // LANES
        if tiles in (2, 4, 8, 16):
            first = offset_now // piece_size
            kinds[first : first + row_count * col_count // piece_size] = tiles
        offset_now += row_count * col_count
    return kinds


def pack_blocks(master, slot_kinds, kinds_used, first_slot, slot_count):
    piece_size = master.shape[1]
    chunks = piece_size // CHUNK
    rows = CHUNK // LANES
    first_block = first_slot // 8
    slot_blocks = pl.cdiv(slot_count, 8)

    def kernel(kinds_ref, master_ref, out_ref, scratch):
        first = (first_block + pl.program_id(0)) * 8
        for j in range(rows):
            scratch[8 * j : 8 * j + 8, :] = master_ref[:, LANES * j : LANES * j + LANES]
        for s in range(8):
            kind_now = kinds_ref[first + s]
            for kind in kinds_used:

                @pl.when(kind_now == kind)
                def _():
                    for tile in range(rows // TILE):
                        row_tile, column = divmod(tile, kind)
                        start = (row_tile * TILE * kind + column) * 8 + s
                        out_ref[s, TILE * tile : TILE * tile + TILE, :] = scratch[
                            pl.ds(start, TILE, stride=8 * kind), :
                        ].astype(jnp.bfloat16)

    return pl.pallas_call(
        kernel,
        grid_spec=pltpu.PrefetchScalarGridSpec(
            num_scalar_prefetch=1,
            grid=(slot_blocks, chunks),
            in_specs=[pl.BlockSpec((8, CHUNK), lambda i, j, kinds: (first_block + i, j))],
            out_specs=pl.BlockSpec((8, rows, LANES), lambda i, j, kinds: (i, j, 0)),
            scratch_shapes=[pltpu.VMEM((8 * rows, LANES), jnp.float32)],
        ),
        out_shape=jax.ShapeDtypeStruct((slot_count, piece_size // LANES, LANES), jnp.bfloat16),
        compiler_params=params(),
    )(slot_kinds, master)


def reserve(shape, kind):
    def kernel(out_ref):
        pass

    return pl.pallas_call(
        kernel,
        out_specs=pl.BlockSpec(memory_space=pl.ANY),
        out_shape=jax.ShapeDtypeStruct(shape, kind),
        compiler_params=params(),
    )()


def assemble(tables, matrices, step_rows, rows_in=None):
    piece_rows = tables[0].shape[1]
    plans = []
    first_block, first_column = 0, 0
    for positions, col_count in matrices:
        tiles = col_count // LANES
        blocks = step_rows * tiles // piece_rows
        plans.append((first_block, first_column, tiles, blocks))
        first_block += blocks
        first_column += col_count
    blocks_a_step, width = first_block, first_column
    steps = matrices[0][0].shape[0] // plans[0][3]
    order = jnp.concatenate(
        [
            positions.reshape(steps, plan[3])
            for (positions, col_count), plan in zip(matrices, plans)
        ],
        axis=1,
    ).reshape(-1)
    uneven = [plan for plan in plans if piece_rows * plan[3] != step_rows * plan[2] or plan[2] not in (2, 4, 8, 16)]
    multiply = rows_in is not None

    def kernel(order_ref, *refs):
        if multiply:
            rows_ref, refs = refs[0], refs[1:]
        table_refs, refs = refs[: len(tables)], refs[len(tables) :]
        out_ref, refs = refs[0], refs[1:]
        if multiply:
            product_ref, refs = refs[0], refs[1:]
        buffer, sem, scratch = refs
        g = pl.program_id(0)
        slot = lax.rem(g, 2)

        def start(step, which):
            def one(j, carry):
                position = order_ref[step * blocks_a_step + j]
                for number, table_ref in enumerate(table_refs):

                    @pl.when(position // TABLE == number)
                    def _():
                        pltpu.make_async_copy(
                            table_ref.at[lax.rem(position, TABLE)],
                            buffer.at[which, j],
                            sem.at[which],
                        ).start()

                return carry

            lax.fori_loop(0, blocks_a_step, one, 0)

        @pl.when(g == 0)
        def _():
            start(0, 0)

        @pl.when(g + 1 < steps)
        def _():
            start(g + 1, 1 - slot)

        pltpu.make_async_copy(buffer.at[slot], buffer.at[slot], sem.at[slot]).wait()
        for plan in plans:
            first, left, tiles, blocks = plan
            if plan in uneven:
                for j in range(blocks):
                    scratch[piece_rows * j : piece_rows * j + piece_rows, :] = buffer[
                        slot, first + j
                    ].astype(jnp.float32)
                for c in range(tiles):
                    out_ref[:, left + LANES * c : left + LANES * c + LANES] = scratch[
                        pl.ds(c, step_rows, stride=tiles), :
                    ].astype(jnp.bfloat16)
                continue
            for j in range(blocks):
                for tile in range(piece_rows // TILE):
                    row_tile, column = divmod(tile, tiles)
                    row = piece_rows // tiles * j + TILE * row_tile
                    column = left + LANES * column
                    out_ref[row : row + TILE, column : column + LANES] = buffer[
                        slot, first + j, TILE * tile : TILE * tile + TILE, :
                    ]
        if multiply:
            part = jnp.dot(rows_ref[...], out_ref[...], preferred_element_type=jnp.float32)

            @pl.when(g == 0)
            def _():
                product_ref[...] = part

            @pl.when(g > 0)
            def _():
                product_ref[...] = product_ref[...] + part

    anywhere = pl.BlockSpec(memory_space=pl.ANY)
    in_specs = [anywhere for table in tables]
    operands = list(tables)
    out_specs = [pl.BlockSpec((step_rows, width), lambda g, order: (g, 0))]
    out_shape = [jax.ShapeDtypeStruct((steps * step_rows, width), jnp.bfloat16)]
    if multiply:
        row_count = rows_in.shape[0]
        in_specs.insert(0, pl.BlockSpec((row_count, step_rows), lambda g, order: (0, g)))
        operands.insert(0, rows_in)
        out_specs.append(pl.BlockSpec((row_count, width), lambda g, order: (0, 0)))
        out_shape.append(jax.ShapeDtypeStruct((row_count, width), jnp.float32))
    scratch_rows = max([plan[3] * piece_rows for plan in uneven], default=8)
    return pl.pallas_call(
        kernel,
        grid_spec=pltpu.PrefetchScalarGridSpec(
            num_scalar_prefetch=1,
            grid=(steps,),
            in_specs=in_specs,
            out_specs=out_specs,
            scratch_shapes=[
                pltpu.VMEM((2, blocks_a_step, piece_rows, LANES), jnp.bfloat16),
                pltpu.SemaphoreType.DMA((2,)),
                pltpu.VMEM((scratch_rows, LANES), jnp.float32),
            ],
        ),
        out_shape=out_shape,
        cost_estimate=pl.CostEstimate(
            flops=2 * steps * step_rows * width * (rows_in.shape[0] if multiply else 0),
            bytes_accessed=4 * steps * step_rows * width,
            transcendentals=0,
        ),
        compiler_params=params(),
    )(order, *operands)


def spread_products(my_part, parts, pairs):
    row_count = pairs[0][0][0].shape[0]
    total = pairs[0][1].shape[0 if pairs[0][2] else 1]
    width = total // parts

    def kernel(part_ref, *refs):
        ins, outs = list(refs[:-parts]), refs[-parts:]
        for m in range(parts):
            first = pl.multiple_of((part_ref[0] ^ m) * width, width)
            result, place = None, 0
            for lefts, right, transposed in pairs:
                left_refs, right_ref = ins[place : place + len(lefts)], ins[place + len(lefts)]
                place += len(lefts) + 1
                depth = 0
                for left_ref in left_refs:
                    inner = slice(depth, depth + left_ref.shape[1])
                    depth += left_ref.shape[1]
                    if transposed:
                        block, axis = right_ref[pl.ds(first, width), inner], 1
                    else:
                        block, axis = right_ref[inner, pl.ds(first, width)], 0
                    part = lax.dot_general(
                        left_ref[...],
                        block,
                        (((1,), (axis,)), ((), ())),
                        preferred_element_type=jnp.float32,
                    )
                    result = part if result is None else result + part
            outs[m][...] = result.astype(jnp.bfloat16)

    vmem = pl.BlockSpec(memory_space=pltpu.VMEM)
    flat = [array for lefts, right, transposed in pairs for array in (*lefts, right)]
    return pl.pallas_call(
        kernel,
        in_specs=[pl.BlockSpec(memory_space=pltpu.SMEM)] + [vmem] * len(flat),
        out_specs=[vmem] * parts,
        out_shape=[jax.ShapeDtypeStruct((row_count, width), jnp.bfloat16)] * parts,
        cost_estimate=pl.CostEstimate(
            flops=2 * row_count * sum(pair[1].size for pair in pairs),
            bytes_accessed=2 * sum(pair[1].size for pair in pairs),
            transcendentals=0,
        ),
        compiler_params=params(),
    )(my_part, *flat)


def exchange(blocks, axis):
    devices = lax.axis_size(axis)
    return [blocks[0]] + [
        lax.ppermute(blocks[m], axis, [(i, i ^ m) for i in range(devices)])
        for m in range(1, devices)
    ]


def total_of(blocks):
    total = blocks[0].astype(jnp.float32)
    for block in blocks[1:]:
        total = total + block.astype(jnp.float32)
    return total


def sum_over(block, axis):
    return total_of(exchange([block] * lax.axis_size(axis), axis))


def in_order(blocks, my_part, axis):
    stacked = jnp.stack(blocks)
    return jnp.concatenate(
        [
            lax.dynamic_index_in_dim(stacked, my_part ^ j, 0, keepdims=False)
            for j in range(len(blocks))
        ],
        axis=axis,
    )


def gather_states(block):
    devices = lax.axis_size("seq")
    if devices != 8:
        return lax.all_gather(block, "seq", axis=0, tiled=False), jnp.zeros((1,), jnp.int32)

    def moved(array, mask):
        return lax.ppermute(array, "seq", [(i, i ^ mask) for i in range(devices)])

    chips = [block] + [moved(block, mask) for mask in (2, 4, 6)]
    pairs = [(chip, moved(chip, 1)) for chip in chips]
    rows = jnp.stack([array for pair in pairs for array in pair])
    return rows, lax.axis_index("seq").astype(jnp.int32).reshape(1)


def weight_grad_blocks(left_t, right, right_block, col_count, positions, tables, blocks_a_step):
    row_total, depth = left_t.shape
    tiles = col_count // LANES
    piece_rows = 512
    even = tiles in (2, 4, 8, 16)
    step_rows = blocks_a_step * piece_rows // tiles
    steps = row_total // step_rows

    def kernel(positions_ref, left_ref, right_ref, *refs):
        table_refs = refs[len(tables) : 2 * len(tables)]
        product, staged, sem = refs[2 * len(tables) :]
        g = pl.program_id(0)
        slot = lax.rem(g, 2)

        def settle(which):
            pltpu.make_async_copy(staged.at[which], staged.at[which], sem.at[which]).wait()

        @pl.when(g >= 2)
        def _():
            settle(slot)

        left = left_ref[...]
        if even:
            product[...] = jnp.dot(left, right_ref[...], preferred_element_type=jnp.float32)
            for tile in range(step_rows // TILE * tiles):
                row_tile, column = divmod(tile, tiles)
                block, row = divmod(TILE * tile, piece_rows)
                staged[slot, block, row : row + TILE, :] = product[
                    TILE * row_tile : TILE * row_tile + TILE, LANES * column : LANES * column + LANES
                ].astype(jnp.bfloat16)
        else:
            for c in range(0, tiles, 2):
                width = min(2, tiles - c)
                part = jnp.dot(
                    left,
                    right_ref[:, LANES * c : LANES * (c + width)],
                    preferred_element_type=jnp.float32,
                )
                for w in range(width):
                    product[pl.ds(c + w, step_rows, stride=tiles), :] = part[
                        :, LANES * w : LANES * w + LANES
                    ]
            for block in range(blocks_a_step):
                staged[slot, block] = product[
                    piece_rows * block : piece_rows * block + piece_rows, :
                ].astype(jnp.bfloat16)
        for block in range(blocks_a_step):
            position = positions_ref[g * blocks_a_step + block]

            for number, table_ref in enumerate(table_refs):

                @pl.when(position // TABLE == number)
                def _():
                    pltpu.make_async_copy(
                        staged.at[slot, block],
                        table_ref.at[lax.rem(position, TABLE)],
                        sem.at[slot],
                    ).start()

        @pl.when(g == steps - 1)
        def _():
            settle(slot)
            if steps > 1:
                settle(1 - slot)

    anywhere = pl.BlockSpec(memory_space=pl.ANY)
    in_specs = [
        pl.BlockSpec((step_rows, depth), lambda g, positions: (g, 0)),
        pl.BlockSpec((depth, col_count), lambda g, positions: (0, right_block)),
    ] + [anywhere for table in tables]
    product_shape = (step_rows, col_count) if even else (step_rows * tiles, LANES)
    return pl.pallas_call(
        kernel,
        grid_spec=pltpu.PrefetchScalarGridSpec(
            num_scalar_prefetch=1,
            grid=(steps,),
            in_specs=in_specs,
            out_specs=[anywhere for table in tables],
            scratch_shapes=[
                pltpu.VMEM(product_shape, jnp.float32),
                pltpu.VMEM((2, blocks_a_step, piece_rows, LANES), jnp.bfloat16),
                pltpu.SemaphoreType.DMA((2,)),
            ],
        ),
        out_shape=[jax.ShapeDtypeStruct(table.shape, table.dtype) for table in tables],
        input_output_aliases={3 + i: i for i in range(len(tables))},
        cost_estimate=pl.CostEstimate(
            flops=2 * row_total * depth * col_count,
            bytes_accessed=2 * row_total * col_count,
            transcendentals=0,
        ),
        compiler_params=params(),
    )(positions, left_t, right, *tables)


def optimizer_update(
    sources, slot_sources, slot_rows, slot_kinds, kinds_used, slot_masks, small_rates,
    master, moment_one, moment_two, block_range, most_blocks, earlier,
):
    capacity, piece_size = master.shape
    chunks = piece_size // CHUNK
    rows = CHUNK // LANES
    last_block = pl.cdiv(capacity, 8) - 1
    steps = most_blocks * chunks

    def place(step, first, end):
        now = jnp.minimum(step, jnp.maximum((end - first) * chunks - 1, 0))
        return jnp.minimum(first + now // chunks, last_block), lax.rem(now, chunks)

    def kernel(range_ref, kinds_ref, sources_ref, rows_ref, *refs):
        source_refs, refs = refs[: len(sources)], refs[len(sources) :]
        masks_ref, small_ref, master_ref, one_ref, two_ref = refs[:5]
        refs = refs[5 + len(earlier) :]
        grad_out, master_out, one_out, two_out, low_out, scratch, buffer, sem = refs
        step = pl.program_id(0)
        count = jnp.maximum((range_ref[1] - range_ref[0]) * chunks, 1)
        first = place(step, range_ref[0], range_ref[1])[0] * 8
        slot = lax.rem(step, 2)

        def start(step, which):
            block, chunk = place(step, range_ref[0], range_ref[1])
            for s in range(8):
                for i, source_ref in enumerate(source_refs):

                    @pl.when(sources_ref[block * 8 + s] == i)
                    def _():
                        pltpu.make_async_copy(
                            source_ref.at[
                                rows_ref[block * 8 + s],
                                pl.ds(pl.multiple_of(chunk * rows, rows), rows),
                            ],
                            buffer.at[which, s],
                            sem.at[which],
                        ).start()

                @pl.when(sources_ref[block * 8 + s] >= len(sources))
                def _():
                    pltpu.make_async_copy(
                        source_refs[0].at[0, pl.ds(0, rows)], buffer.at[which, s], sem.at[which]
                    ).start()

        @pl.when(step == 0)
        def _():
            start(0, 0)

        @pl.when(step + 1 < count)
        def _():
            start(step + 1, 1 - slot)

        @pl.when(step < count)
        def _():
            pltpu.make_async_copy(buffer.at[slot], buffer.at[slot], sem.at[slot]).wait()
            for s in range(8):
                kind_now = kinds_ref[first + s]
                for kind in kinds_used:

                    @pl.when(kind_now == kind)
                    def _():
                        for tile in range(rows // TILE):
                            row_tile, column = divmod(tile, kind)
                            start_row = (row_tile * TILE * kind + column) * 8 + s
                            scratch[pl.ds(start_row, TILE, stride=8 * kind), :] = buffer[
                                slot, s, TILE * tile : TILE * tile + TILE, :
                            ].astype(jnp.float32)

            present = masks_ref[0] > 0.5
            is_small = masks_ref[1] > 0.5
            rate_rows = masks_ref[2]
            for j in range(rows):
                lanes = slice(LANES * j, LANES * j + LANES)
                grad = jnp.where(present, scratch[8 * j : 8 * j + 8, :], 0.0)
                rate = jnp.where(is_small, small_ref[:, lanes], rate_rows)
                master_now = master_ref[:, lanes]
                one_new = BETA_ONE * one_ref[:, lanes] + (1.0 - BETA_ONE) * grad
                two_new = BETA_TWO * two_ref[:, lanes] + (1.0 - BETA_TWO) * grad * grad
                first_hat = one_new / (1.0 - BETA_ONE**STEP)
                second_hat = two_new / (1.0 - BETA_TWO**STEP)
                master_new = master_now - rate * (
                    first_hat / (jnp.sqrt(second_hat) + ADAM_EPSILON) + WEIGHT_DECAY * master_now
                )
                grad_out[:, lanes] = grad
                master_out[:, lanes] = master_new
                one_out[:, lanes] = one_new
                two_out[:, lanes] = two_new
                low_out[:, lanes] = master_new.astype(jnp.bfloat16)

    state_spec = pl.BlockSpec((8, CHUNK), lambda t, ends, *tables: place(t, ends[0], ends[1]))
    anywhere = pl.BlockSpec(memory_space=pl.ANY)
    wide = jax.ShapeDtypeStruct((capacity, piece_size), jnp.float32)
    operands = [*sources, slot_masks, small_rates, master, moment_one, moment_two, *earlier]
    return pl.pallas_call(
        kernel,
        grid_spec=pltpu.PrefetchScalarGridSpec(
            num_scalar_prefetch=4,
            grid=(steps,),
            in_specs=[pl.BlockSpec(memory_space=pltpu.HBM) for source in sources]
            + [
                pl.BlockSpec((3, 8, LANES), lambda t, ends, *tables: (0, place(t, ends[0], ends[1])[0], 0)),
                pl.BlockSpec((1, CHUNK), lambda t, ends, *tables: (0, place(t, ends[0], ends[1])[1])),
                state_spec,
                state_spec,
                state_spec,
            ]
            + [anywhere for array in earlier],
            out_specs=[state_spec] * 5,
            scratch_shapes=[
                pltpu.VMEM((8 * rows, LANES), jnp.float32),
                pltpu.VMEM((2, 8, rows, LANES), jnp.bfloat16),
                pltpu.SemaphoreType.DMA((2,)),
            ],
        ),
        out_shape=[wide] * 4 + [jax.ShapeDtypeStruct((capacity, piece_size), jnp.bfloat16)],
        input_output_aliases={
            4 + len(operands) - len(earlier) + i: i for i in range(len(earlier))
        },
        cost_estimate=pl.CostEstimate(
            flops=20 * most_blocks * 8 * piece_size,
            bytes_accessed=16 * most_blocks * 8 * piece_size,
            transcendentals=2 * most_blocks * 8 * piece_size,
        ),
        compiler_params=params(),
    )(block_range, slot_kinds, slot_sources, slot_rows, *operands)


def weight_grad(left, right):
    return jnp.einsum("td,tc->dc", left, right, preferred_element_type=jnp.float32)


def back_product(grad_rows, weight):
    return jnp.dot(grad_rows, weight.T, preferred_element_type=jnp.float32)


def gather_rest(packed, first, trips, most, extra_step):
    devices = lax.axis_size("seq")
    rows = devices * extra_step
    room = reserve((most * rows,) + packed.shape[1:], packed.dtype)

    def more(trip, table):
        part = lax.dynamic_slice_in_dim(packed, first + trip * extra_step, extra_step)
        if devices != 8:
            part = lax.all_gather(part, "seq", axis=0, tiled=True)
            return lax.dynamic_update_slice_in_dim(table, part, trip * rows, axis=0)
        me = lax.axis_index("seq").astype(jnp.int32)
        chips = [part] + [moved_by(part, mask) for mask in (2, 4, 6)]
        for mask, chip in zip((0, 2, 4, 6), chips):
            for core, block in ((0, chip), (1, moved_by(chip, 1))):
                place = trip * rows + (me ^ (mask + core)) * extra_step
                table = lax.dynamic_update_slice_in_dim(table, block, place, axis=0)
        return table

    return lax.fori_loop(0, trips, more, room)


def reduce_rest(rest, trips, most, extra_step):
    devices = lax.axis_size("seq")
    rows = devices * extra_step
    room = reserve((most * extra_step,) + rest.shape[1:], rest.dtype)

    def more(trip, table):
        part = lax.dynamic_slice_in_dim(rest, trip * rows, rows)
        part = lax.psum_scatter(part, "seq", scatter_dimension=0, tiled=True)
        return lax.dynamic_update_slice_in_dim(table, part, trip * extra_step, axis=0)

    return lax.fori_loop(0, trips, more, room)


def on_device(inputs, cotangent, owners, master, moment_one, moment_two):
    head_parts = lax.axis_size("head")
    seq_parts = lax.axis_size("seq")
    local_heads = HEADS // head_parts
    capacity, piece_size = master.shape
    piece_count = owners.shape[0]
    row_count = inputs.shape[0]
    rim_width = KCONV - 1
    segments_list = shard_layout(local_heads, head_parts)
    columns = {name: c for name, r, c, rate in segments_list}
    counts = {name: r * c // piece_size for name, r, c, rate in segments_list[:8]}
    firsts = dict(zip(counts, np.cumsum([0] + list(counts.values())).tolist()))
    mixer_count = firsts["wgate"]
    big_count = piece_count - 1
    my_head = lax.axis_index("head").astype(jnp.int32)
    my_index = lax.axis_index("seq").astype(jnp.int32)
    my_head_row, my_index_row = my_head.reshape(1), my_index.reshape(1)

    onehot = (owners[:, None] == jnp.arange(seq_parts, dtype=jnp.int32)[None, :]).astype(jnp.int32)
    ranks = jnp.sum((jnp.cumsum(onehot, axis=0) - onehot) * onehot, axis=1)
    mixer_held = jnp.sum(onehot[:mixer_count], axis=0)
    mlp_held = jnp.sum(onehot[mixer_count:big_count], axis=0)
    padded = capacity + -capacity % 8
    small_rank = ranks[big_count]
    big_owners, big_ranks = owners[:big_count], ranks[:big_count]

    def rest_row(over, owner):
        return over // extra_step * (seq_parts * extra_step) + owner * extra_step + over % extra_step

    early = -(-capacity * FIRST_GATHER // (8 * CAPACITY_UNIT)) * 8
    late = capacity - early
    late_room = min(late, -(-capacity * SECOND_GATHER // CAPACITY_UNIT))
    extra_step = 2 if late % 2 == 0 else 1
    most_gather = -(-late // extra_step)
    trips_gather = jnp.maximum(-(-(jnp.max(mixer_held) - early) // extra_step), 0)
    early_row = big_owners * early + big_ranks
    mixer_fetch = jnp.where(
        big_ranks < early, early_row, TABLE + rest_row(big_ranks - early, big_owners)
    )
    neighbours = np.arange(seq_parts) ^ 1
    late_held = jnp.maximum(mixer_held + mlp_held - early, 0)
    late_spare = jnp.maximum(late_room - late_held[neighbours], 0)
    late_over = jnp.maximum(late_held - late_room, 0)
    trips_late = -(-jnp.max(jnp.maximum(late_over - late_spare, 0)) // extra_step)
    spare_there = jnp.sum(onehot[:big_count] * late_spare[None, :], axis=1)
    past = big_ranks - early - late_room
    rest_trip = (past - spare_there) // extra_step
    rest_start = late_room + spare_there + rest_trip * extra_step
    rest_start = jnp.minimum(rest_start, late - extra_step)
    mlp_fetch = jnp.where(
        big_ranks < early,
        TABLE + early_row,
        jnp.where(
            past < 0,
            big_owners * late_room + big_ranks - early,
            jnp.where(
                past < spare_there,
                (big_owners ^ 1) * late_room + late_room - spare_there + past,
                2 * TABLE
                + rest_trip * (seq_parts * extra_step)
                + big_owners * extra_step
                + big_ranks - early - rest_start,
            ),
        ),
    )
    first_room = -(-capacity * FIRST_REDUCE // CAPACITY_UNIT)
    second_room = -(-capacity * SECOND_REDUCE // CAPACITY_UNIT)
    most_reduce = -(-(capacity - second_room) // extra_step)
    second_held = mixer_held + jnp.maximum(mlp_held - first_room, 0)
    second_there = jnp.sum(onehot[:big_count] * second_held[None, :], axis=1)
    spill_plan, spill_taken = [], jnp.zeros_like(second_held)
    hosted = jnp.zeros_like(second_held)
    over_held = jnp.maximum(second_held - second_room, 0)
    for mask, most in (((1, 6), (2, 4), (4, 4), (6, 4)) if seq_parts == 8 else ((1, 4),)):
        most = min(most, second_room)
        partner = np.arange(seq_parts) ^ mask
        free = jnp.maximum(second_room - second_held - hosted, 0)[partner]
        take = jnp.minimum(jnp.minimum(over_held - spill_taken, most - hosted[partner]), free)
        take = jnp.maximum(take, 0)
        first_row = second_room - hosted[partner] - take
        spill_plan.append((mask, most, spill_taken, take, first_row))
        spill_taken = spill_taken + take
        hosted = hosted + take[partner]
    trips_reduce = -(-jnp.max(over_held - spill_taken) // extra_step)

    def of_owner(values):
        return jnp.sum(onehot[:big_count] * values[None, :], axis=1)

    second_over = big_ranks - second_room
    second_spot = jnp.where(
        second_over < 0,
        TABLE + big_owners * second_room + big_ranks,
        2 * TABLE + rest_row(second_over - of_owner(spill_taken), big_owners),
    )
    for mask, most, before, take, first_row in spill_plan:
        inside = second_over - of_owner(before)
        second_spot = jnp.where(
            (inside >= 0) & (inside < of_owner(take)),
            TABLE + (big_owners ^ mask) * second_room + of_owner(first_row) + inside,
            second_spot,
        )
    store = jnp.where(
        big_ranks >= second_there,
        big_owners * first_room + big_ranks - second_there,
        second_spot,
    )
    small_owner = owners[big_count]

    def spots(table, name):
        return table[firsts[name] : firsts[name] + counts[name]]

    my_mixer = mixer_held[my_index]
    my_mlp = mlp_held[my_index]
    my_count = my_mixer + my_mlp
    slot_ids = jnp.arange(padded, dtype=jnp.int32)
    mine = owners == my_index
    matches = (mine[None, :] & (ranks[None, :] == slot_ids[:, None])).astype(jnp.int32)
    kind_table = piece_kinds(segments_list, piece_count, piece_size)
    piece_rates, small_rates = rate_parts(segments_list, piece_count, piece_size)
    present = jnp.sum(matches, axis=1)
    slot_kinds = 1 + jnp.sum(matches * jnp.asarray(kind_table - 1)[None, :], axis=1)
    slot_rates = PAD_RATE + jnp.sum(
        matches.astype(jnp.float32) * jnp.asarray(piece_rates - np.float32(PAD_RATE))[None, :], axis=1
    )
    is_small = matches[:, big_count]
    kinds_used = sorted(set(kind_table.tolist()) | {1})
    my_held = second_held[my_index]
    in_first = slot_ids >= my_held
    my_over = slot_ids - second_room
    rest_source = 3 + len(spill_plan)
    slot_sources = jnp.where(my_over < 0, 2, rest_source)
    slot_rows = jnp.where(my_over < 0, slot_ids, my_over - spill_taken[my_index])
    for number, (mask, most, before, take, first_row) in enumerate(spill_plan):
        inside = my_over - before[my_index]
        here = (inside >= 0) & (inside < take[my_index])
        slot_sources = jnp.where(here, 3 + number, slot_sources)
        slot_rows = jnp.where(
            here, first_row[my_index] + inside - (second_room - most), slot_rows
        )
    slot_sources = jnp.where(in_first, 0, slot_sources)
    slot_rows = jnp.where(in_first, slot_ids - my_held, slot_rows)
    slot_sources = jnp.where(present > 0, jnp.where(is_small > 0, 1, slot_sources), 0)
    slot_rows = jnp.where(is_small > 0, 0, slot_rows)
    slot_rows = jnp.where(present > 0, slot_rows, 0)
    slot_masks = jnp.stack([present.astype(jnp.float32), is_small.astype(jnp.float32), slot_rates])
    slot_masks = jnp.broadcast_to(slot_masks[:, :, None], slot_masks.shape + (LANES,))
    all_blocks = padded // 8
    plain_blocks = second_room // 8
    from_first = jnp.clip((my_held + 7) // 8, plain_blocks, all_blocks).astype(jnp.int32)
    ranges = [
        jnp.stack([from_first, jnp.int32(all_blocks)]),
        jnp.array([0, plain_blocks], jnp.int32),
        jnp.stack([jnp.int32(plain_blocks), jnp.maximum(from_first, plain_blocks + 1)]),
    ]

    small_rows = -(-sum(r * c for name, r, c, rate in segments_list[8:]) // (TILE * LANES)) * TILE
    gain_width = D // head_parts
    norm_width = DV // head_parts
    gain_first = sum(r * c for name, r, c, rate in segments_list[8:14])
    my_small = lax.dynamic_slice(master, (small_rank, 0), (1, small_rows * LANES))
    my_small = my_small.astype(jnp.bfloat16)
    gains = my_small[:, gain_first : gain_first + 2 * gain_width + norm_width]
    gains = in_order(exchange([gains] * head_parts, "head"), my_head, 0)
    gains = jnp.concatenate(
        [
            gains[:, :gain_width].reshape(1, D),
            gains[:, gain_width : 2 * gain_width].reshape(1, D),
            gains[:, 2 * gain_width :].reshape(1, DV),
        ],
        axis=1,
    )
    rows_of_piece = piece_size // LANES
    small_width = small_rows * LANES
    small_part = jnp.concatenate([my_small, gains], axis=1).reshape(-1, LANES)
    small_table, small_base = gather_states(small_part)
    input_blocks = exchange([inputs] * head_parts, "head")
    early_part = pack_blocks(master, slot_kinds, kinds_used, 0, early)
    early_table = lax.all_gather(early_part, "seq", axis=0, tiled=True)
    late_part = pack_blocks(master, slot_kinds, kinds_used, early, late)
    late_send = late_part[:late_room]
    if late_room < late:
        guests = lax.ppermute(
            late_part[late_room:], "seq", [(i, i ^ 1) for i in range(seq_parts)]
        )
        late_send = lax.dynamic_update_slice_in_dim(
            late_part, guests, late_held[my_index], axis=0
        )[:late_room]
    back_blocks = exchange([cotangent] * head_parts, "head")
    rows_full = in_order(input_blocks, my_head, 1)
    back_full = in_order(back_blocks, my_head, 1)
    small_flat = lax.dynamic_index_in_dim(
        small_table, small_owner ^ small_base[0], axis=0, keepdims=False
    ).reshape(-1)
    by_name, small_used = unpack(small_flat, segments_list[8:])
    gains = small_flat[small_width:].astype(jnp.float32)[None, :]
    gain_one, gain_two, norm_row = gains[:, :D], gains[:, D : 2 * D], gains[:, 2 * D :]
    gain_one_mine = by_name["gainone"].astype(jnp.float32)
    gain_two_mine = by_name["gaintwo"].astype(jnp.float32)

    rows_wide = rows_full.astype(jnp.float32)
    scale_one = lax.rsqrt(jnp.mean(rows_wide * rows_wide, axis=-1, keepdims=True) + NORM_EPSILON)
    normed = (rows_wide * scale_one * gain_one).astype(jnp.bfloat16)
    normed_ext = jnp.concatenate([shifted(normed[row_count - RIM :], "seq", 1), normed], axis=0)

    decay_weight = jnp.pad(by_name["wab"], ((0, 0), (0, LANES - 2 * local_heads)))
    decay_proj = jnp.dot(normed, decay_weight, preferred_element_type=jnp.float32)
    taps = jnp.concatenate([by_name["cv"], by_name["ck"]], axis=1)
    taps = jnp.pad(taps.astype(jnp.float32), ((0, 8 - KCONV), (0, 0)))
    query_taps = jnp.pad(by_name["cq"].astype(jnp.float32), ((0, 8 - KCONV), (0, 0)))
    scalars = jnp.pad(
        jnp.concatenate([by_name["alog"], by_name["dtbias"]], axis=0).astype(jnp.float32),
        ((0, 6), (0, LANES - local_heads)),
    )

    beside = (
        trips_gather, late_part, late_send, normed, normed_ext, scale_one, decay_proj, decay_weight, taps, query_taps, scalars,
        back_full, mixer_fetch, mlp_fetch, store, gain_two, norm_row,
        slot_sources, slot_rows, slot_masks, ranges, trips_late, trips_reduce,
    )
    early_table, beside = lax.optimization_barrier((early_table, beside))
    (
        trips_now, late_part, late_send, normed, normed_ext, scale_one, decay_proj, decay_weight, taps, query_taps, scalars,
        back_full, mixer_fetch, mlp_fetch, store, gain_two, norm_row,
        slot_sources, slot_rows, slot_masks, ranges, trips_late, trips_reduce,
    ) = beside
    mixer_rest = gather_rest(late_part, 0, trips_now, most_gather, extra_step)
    late_table = lax.all_gather(late_send, "seq", axis=0, tiled=True)

    value_key_weights, value_key = assemble(
        [early_table, mixer_rest],
        [(spots(mixer_fetch, name), columns[name]) for name in ("wv", "wk")],
        512,
        normed_ext,
    )
    solve, fresh, wy_keys, handoff = mixer_local(
        local_heads, value_key, taps, decay_proj, scalars
    )
    query_gate_weights, query_gate = assemble(
        [early_table, mixer_rest],
        [(spots(mixer_fetch, name), columns[name]) for name in ("wq", "wg")],
        512,
        normed_ext,
    )
    reach, zero_out = mixer_reach(
        local_heads, query_gate, value_key, query_taps, taps, decay_proj, scalars, fresh, wy_keys
    )
    (out_weights,) = assemble(
        [early_table, mixer_rest], [(spots(mixer_fetch, "wo"), columns["wo"])], 256
    )
    entering_state, kept_states, beside = entering(
        local_heads,
        my_index_row,
        handoff,
        (query_gate_weights, query_gate, reach, zero_out, out_weights),
    )
    query_gate_weights, query_gate, reach, zero_out, out_weights = beside
    recurred, gated_low = mixer_out(
        local_heads, entering_state, reach, zero_out, query_gate, norm_row
    )
    mixed_parts = exchange(
        spread_products(my_head_row, head_parts, [((gated_low,), out_weights, False)]), "head"
    )
    mixed = total_of(mixed_parts)
    inputs_wide = inputs.astype(jnp.float32)
    residual = inputs_wide + mixed
    resid_low = residual.astype(jnp.bfloat16)

    resid_blocks = exchange([resid_low] * head_parts, "head")
    trips_now, late_table = lax.optimization_barrier((trips_late, late_table))
    late_rest = gather_rest(
        late_part, late_room + late_spare[my_index], trips_now, most_gather, extra_step
    )
    mlp_tables = [late_table, early_table, late_rest]
    (down_weights,) = assemble(
        mlp_tables, [(spots(mlp_fetch, "wdown"), columns["wdown"])], 352
    )
    (mlp_weights,) = assemble(
        mlp_tables,
        [(spots(mlp_fetch, name), columns[name]) for name in ("wgate", "wup")],
        512,
    )
    resid_blocks, down_weights, mlp_weights = lax.optimization_barrier(
        (resid_blocks, down_weights, mlp_weights)
    )
    resid_full = in_order(resid_blocks, my_head, 1).astype(jnp.float32)
    scale_two = lax.rsqrt(jnp.mean(resid_full * resid_full, axis=-1, keepdims=True) + NORM_EPSILON)
    hidden_in = (resid_full * scale_two * gain_two).astype(jnp.bfloat16)
    gate_up = jnp.dot(hidden_in, mlp_weights, preferred_element_type=jnp.float32)
    hidden_width = columns["wgate"]
    gate_mlp, up_mlp = gate_up[:, :hidden_width], gate_up[:, hidden_width:]
    logistic_output_multiplier = jax.nn.sigmoid(gate_mlp)
    silu_gate = gate_mlp * logistic_output_multiplier
    hidden = (silu_gate * up_mlp).astype(jnp.bfloat16)
    mlp_blocks = spread_products(my_head_row, head_parts, [((hidden,), down_weights, False)])
    d_hidden = back_product(back_full, down_weights)
    d_gate_mlp = (
        d_hidden
        * up_mlp
        * logistic_output_multiplier
        * (1.0 + gate_mlp * (1.0 - logistic_output_multiplier))
    ).astype(jnp.bfloat16)
    d_up_mlp = (d_hidden * silu_gate).astype(jnp.bfloat16)
    def store_grad(tables, name, left_t, right, right_block, blocks_a_step):
        return weight_grad_blocks(
            left_t, right, right_block, columns[name], spots(store, name), tables, blocks_a_step
        )

    grad_tables = [
        reserve((rows, rows_of_piece, LANES), jnp.bfloat16)
        for rows in (
            seq_parts * first_room,
            seq_parts * second_room,
            most_reduce * seq_parts * extra_step,
        )
    ]
    grad_tables = store_grad(grad_tables, "wdown", hidden.T, back_full, 0, 11)
    hidden_in_t = hidden_in.T
    grad_tables = store_grad(grad_tables, "wgate", hidden_in_t, d_gate_mlp, 0, 11)
    grad_tables = store_grad(grad_tables, "wup", hidden_in_t, d_up_mlp, 0, 11)
    grad_tables, d_gate_mlp, d_up_mlp = lax.optimization_barrier(
        (grad_tables, d_gate_mlp, d_up_mlp)
    )
    d_hidden_parts = exchange(
        spread_products(my_head_row, head_parts, [((d_gate_mlp, d_up_mlp), mlp_weights, True)]), "head"
    )
    first_reduced = lax.psum_scatter(grad_tables[0], "seq", scatter_dimension=0, tiled=True)
    grad_tables = grad_tables[1:]
    store = store - TABLE
    d_hidden_mine = total_of(d_hidden_parts)

    resid_mine = resid_low.astype(jnp.float32)
    d_hidden_low = d_hidden_mine.astype(jnp.bfloat16)
    dot_mine = jnp.sum(d_hidden_mine * gain_two_mine * resid_mine, axis=-1)
    d_hidden_blocks = exchange([d_hidden_low] * head_parts, "head")
    dot_two = sum_over(dot_mine.reshape(-1, LANES), "head").reshape(row_count, 1)
    grad_gaintwo = jnp.sum(d_hidden_mine * resid_mine * scale_two, axis=0)
    d_resid = (
        cotangent.astype(jnp.float32)
        + scale_two * d_hidden_mine * gain_two_mine
        - scale_two**3 / D * resid_mine * dot_two
    )
    d_hidden_full = in_order(d_hidden_blocks, my_head, 1).astype(jnp.float32)
    back_mix_full = (
        back_full.astype(jnp.float32)
        + scale_two * d_hidden_full * gain_two
        - scale_two**3 / D * resid_full * dot_two
    ).astype(jnp.bfloat16)

    d_gated = back_product(back_mix_full, out_weights)
    d_recurred, d_gate, norm_grad, d_entering = mixer_gate_back(
        local_heads, d_gated, recurred, query_gate, norm_row, reach
    )
    normed_t = normed.T
    grad_tables = store_grad(grad_tables, "wo", gated_low.T, back_mix_full, 0, 8)
    grad_tables = store_grad(grad_tables, "wg", normed_t, d_gate, 0, 8)
    d_leaving, (grad_tables, mlp_blocks) = leaving(
        local_heads, my_index_row, d_entering, kept_states, (grad_tables, mlp_blocks)
    )
    mlp_parts = exchange(mlp_blocks, "head")
    d_conv, d_tail, d_rim, d_taps, d_decay_wide, d_scalars = mixer_back(
        local_heads,
        query_gate,
        value_key,
        query_taps,
        taps,
        decay_proj,
        scalars,
        solve,
        fresh,
        wy_keys,
        entering_state,
        d_recurred,
        d_leaving,
    )
    d_rims = shifted(tuple(part[8 - rim_width :] for part in d_rim), "seq", -1)

    def with_rim(whole, tail, rim_grad):
        tail = tail + jnp.pad(rim_grad, ((8 - rim_width, 0), (0, 0)))
        return lax.dynamic_update_slice(whole, tail.astype(jnp.bfloat16), (row_count - 8, 0))

    d_query, d_value_key = (
        with_rim(*parts) for parts in zip(d_conv, d_tail, d_rims)
    )
    grad_tables = store_grad(grad_tables, "wv", normed_t, d_value_key, 0, 8)
    grad_tables = store_grad(grad_tables, "wk", normed_t, d_value_key, 2, 4)
    grad_tables = store_grad(grad_tables, "wq", normed_t, d_query, 0, 4)
    second_table, first_reduced, mlp_parts = lax.optimization_barrier(
        (grad_tables[0], first_reduced, mlp_parts)
    )
    block_out = (residual + total_of(mlp_parts)).astype(jnp.bfloat16)
    second_reduced = lax.psum_scatter(second_table, "seq", scatter_dimension=0, tiled=True)
    d_decay = d_decay_wide.astype(jnp.bfloat16)
    grad_wab = weight_grad(normed, d_decay)[:, : 2 * local_heads]
    d_normed_mine = total_of(
        exchange(
            spread_products(
                my_head_row,
                head_parts,
                [
                    ((d_value_key,), value_key_weights, True),
                    ((d_query, d_gate), query_gate_weights, True),
                    ((d_decay,), decay_weight, True),
                ],
            ),
            "head",
        )
    )
    dot_one = jnp.sum(d_normed_mine * gain_one_mine * inputs_wide, axis=-1)
    sums = sum_over(
        jnp.concatenate([dot_one.reshape(-1, LANES), norm_grad[0].reshape(-1, LANES)]), "head"
    )
    dot_one = sums[: row_count // LANES].reshape(row_count, 1)
    grad_wnorm = lax.dynamic_slice_in_dim(
        sums[row_count // LANES :].reshape(-1), my_head * norm_width, norm_width
    )
    grad_gainone = jnp.sum(d_normed_mine * inputs_wide * scale_one, axis=0)
    input_grad = (
        d_resid
        + scale_one * d_normed_mine * gain_one_mine
        - scale_one**3 / D * inputs_wide * dot_one
    )

    small_grads = [
        d_taps[0][:KCONV],
        d_taps[1][:KCONV, local_heads * DV :],
        d_taps[1][:KCONV, : local_heads * DV],
        grad_wab,
        d_scalars[0, :local_heads],
        d_scalars[1, :local_heads],
        grad_gainone,
        grad_gaintwo,
        grad_wnorm,
    ]
    small_block = jnp.concatenate(
        [grad_now.reshape(-1) for grad_now in small_grads]
        + [jnp.zeros((small_rows * LANES - small_used,), jnp.float32)]
    ).reshape(-1, LANES)
    mask = 1
    while mask < seq_parts:
        small_block = small_block + lax.ppermute(
            small_block, "seq", [(i, i ^ mask) for i in range(seq_parts)]
        )
        mask *= 2
    small_block = jnp.pad(
        small_block.astype(jnp.bfloat16), ((0, rows_of_piece - small_rows), (0, 0))
    )[None]

    def update(sources, block_range, most_blocks, earlier):
        return optimizer_update(
            sources,
            slot_sources,
            slot_rows,
            slot_kinds,
            kinds_used,
            slot_masks,
            jnp.asarray(small_rates)[None, :],
            master,
            moment_one,
            moment_two,
            block_range,
            most_blocks,
            earlier,
        )

    done = update([first_reduced, small_block], ranges[0], all_blocks - plain_blocks, [])
    done, second_reduced, input_grad, block_out = lax.optimization_barrier(
        (done, second_reduced, input_grad, block_out)
    )
    spilled = []
    for mask, most, before, take, first_row in spill_plan:
        spilled.append(moved_by(second_reduced[second_room - most :], mask))
    sources = [first_reduced, small_block, second_reduced]
    if plain_blocks:
        done = update(sources, ranges[1], plain_blocks, done)
    done, spilled, rest_grads, trips_now = lax.optimization_barrier(
        (done, spilled, grad_tables[1], trips_reduce)
    )
    rest_reduced = reduce_rest(rest_grads, trips_now, most_reduce, extra_step)
    grad_slots, master_new, moment_new, second_new, weights_low = update(
        sources + spilled + [rest_reduced],
        ranges[2],
        all_blocks - plain_blocks,
        done,
    )
    return (
        block_out,
        input_grad,
        grad_slots,
        master_new,
        moment_new,
        second_new,
        weights_low,
    )


def solution(mesh):
    return jax.shard_map(
        on_device,
        mesh=mesh,
        in_specs=(
            P("seq", "head"),
            P("seq", "head"),
            P(),
            P("seq", "head"),
            P("seq", "head"),
            P("seq", "head"),
        ),
        out_specs=(
            P("seq", "head"),
            P("seq", "head"),
            P("seq", "head"),
            P("seq", "head"),
            P("seq", "head"),
            P("seq", "head"),
            P("seq", "head"),
        ),
        check_vma=False,
    )
```

profile of v0, /device:TPU:0, one launch (start us, length us, event | category | flops | bytes accessed | tf_op | source)
XLA Modules:
  0.0 625.6 jit_solution(16152172969015257530)
XLA Ops:
  11.4 8.8 %shard_map.342 = bf16[24,512,128]{2,1,0:T(8,128)(2,1)} custom-call(s32[48]{0:T(128)S(1)} %broadcast_add_fusion.1.kinds_ref, f32[44,65536]{1,0:T(8,128)} %refs_10_.1), custom_call_target="tpu_custom_call" | custom-call | tf_op jit(solution)/shard_map/pallas_call | solution.py:767
  24.4 4.0 collective-permute-start.19
  50.2 7.1 %shard_map.343 = bf16[20,512,128]{2,1,0:T(8,128)(2,1)S(1)} custom-call(s32[48]{0:T(128)S(1)} %broadcast_add_fusion.1.kinds_ref, f32[44,65536]{1,0:T(8,128)} %refs_10_.1), custom_call_target="tpu_custom_call" | custom-call | tf_op jit(solution)/shard_map/pallas_call | solution.py:767
  63.7 7.4 %compare_select_fusion.4 = (s32[48]{0:T(128)S(1)}, s32[48]{0:T(128)S(1)}, f32[1,48]{1,0:T(1,128)S(1)}) fusion(s32[48]{0:T(128)S(1)} %get-tuple-element.423, s32[]{:T(128)} %bitcast.54, s32[]{:T(128)} %bitcast.53, s32[]{:T(128)} %bitcast.52, s32[]{:T(128)} %bitcast.51, s32[]{:T(128)} %bitcast.50, s32[]{:T(128)} %bitcast.48, s32[]{:T(128)} %bitcast.46, ...), kind=kLoop, calls=%fused_computation.259 | loop fusion | flops 2256 | bytes 1008 | tf_op jit(solution)/shard_map/jit(_where)/select_n | solution.py:1417
  73.9 2.5 collective-permute-start.15
  80.2 2.5 collective-permute-done.22
  82.8 2.5 collective-permute-start.26
  85.6 4.2 collective-permute-done.26
  93.0 3.2 collective-permute-start.31
  98.7 18.1 %collective-permute-done.30 = bf16[256,512]{1,0:T(8,128)(2,1)} collective-permute-done((bf16[256,512]{1,0:T(8,128)(2,1)S(1)}, bf16[256,512]{1,0:T(8,128)(2,1)}, u32[]{:S(2)}, u32[]{:S(2)}) %collective-permute-start.30) | collective-permute-done | bytes 262176 | tf_op jit(solution)/shard_map/ppermute | solution.py:967
  125.6 29.8 %all-gather.3.cloned.1.call-done.refs_1_.refs_0_ = bf16[192,512,128]{2,1,0:T(8,128)(2,1)} async-done(((bf16[24,512,128]{2,1,0:T(8,128)(2,1)}), bf16[192,512,128]{2,1,0:T(8,128)(2,1)}) %all-gather.3.cloned.1.call-update) | async-done | bytes 25165840 | tf_op jit(solution)/shard_map/all_gather | solution.py:1451
  157.2 8.0 %shard_map.345 = (bf16[2048,1536]{1,0:T(8,128)(2,1)}, f32[272,1536]{1,0:T(8,128)S(1)}) custom-call(s32[48]{0:T(128)S(1)} %reshape.464.order_ref, bf16[272,2048]{1,0:T(8,128)(2,1)S(1)} %copy.92.refs_0_, bf16[192,512,128]{2,1,0:T(8,128)(2,1)} %all-gather.3.cloned.1.call-done.refs_1_.refs_0_, bf16[160,512,128]{2,1,0:T(8,128)(2,1)} %get-tuple-element.252.refs_2_.refs_1_), custom_call_target="tpu_custom_call" | custom-call | flops 1711276032 | bytes 12582912 | tf_op jit(solution)/shard_map/pallas_call | solution.py:895
  165.2 17.1 %shard_map.346 = (f32[4,256,256]{2,1,0:T(8,128)S(1)}, f32[4,256,256]{2,1,0:T(8,128)S(1)}, f32[4,256,128]{2,1,0:T(8,128)S(1)}, bf16[4,128,384]{2,1,0:T(8,128)(2,1)S(1)}) custom-call(f32[272,1536]{1,0:T(8,128)S(1)} %get-tuple-element.253.pv.pk, f32[272,1536]{1,0:T(8,128)S(1)} %get-tuple-element.253.pv.pk, f32[8,1536]{1,0:T(8,128)S(1)} %fusion.34.tv.tk, ...), custom_call_target="tpu_custom_call" | custom-call | tf_op jit(solution)/shard_map/pallas_call | solution.py:245
  191.9 3.8 shard_map.350.refs_1_
  195.8 9.3 %shard_map.348 = (bf16[2048,1536]{1,0:T(8,128)(2,1)}, f32[272,1536]{1,0:T(8,128)S(1)}) custom-call(s32[48]{0:T(128)S(1)} %reshape.467.order_ref, bf16[272,2048]{1,0:T(8,128)(2,1)S(1)} %copy.92.refs_0_, bf16[192,512,128]{2,1,0:T(8,128)(2,1)} %all-gather.3.cloned.1.call-done.refs_1_.refs_0_, bf16[160,512,128]{2,1,0:T(8,128)(2,1)} %get-tuple-element.252.refs_2_.refs_1_), custom_call_target="tpu_custom_call" | custom-call | flops 1711276032 | bytes 12582912 | tf_op jit(solution)/shard_map/pallas_call | solution.py:895
  205.2 4.2 shard_map.349
  218.0 2.4 collective-permute-start.40
  222.7 8.0 %collective-permute-done.39 = bf16[256,512]{1,0:T(8,128)(2,1)S(1)} collective-permute-done((bf16[256,512]{1,0:T(8,128)(2,1)S(1)}, bf16[256,512]{1,0:T(8,128)(2,1)S(1)}, u32[]{:S(2)}, u32[]{:S(2)}) %collective-permute-start.39) | collective-permute-done | bytes 262176 | tf_op jit(solution)/shard_map/ppermute | solution.py:967
  230.7 8.6 %collective-permute-done.40 = bf16[256,512]{1,0:T(8,128)(2,1)S(1)} collective-permute-done((bf16[256,512]{1,0:T(8,128)(2,1)S(1)}, bf16[256,512]{1,0:T(8,128)(2,1)S(1)}, u32[]{:S(2)}, u32[]{:S(2)}) %collective-permute-start.40) | collective-permute-done | bytes 262176 | tf_op jit(solution)/shard_map/ppermute | solution.py:967
  239.5 2.5 collective-permute-start.44
  242.0 11.2 %all-gather.5.cloned.1.call-done.refs_0_ = bf16[128,512,128]{2,1,0:T(8,128)(2,1)} async-done(((bf16[16,512,128]{2,1,0:T(8,128)(2,1)}), bf16[128,512,128]{2,1,0:T(8,128)(2,1)}) %all-gather.5.cloned.1.call-update) | async-done | bytes 16777232 | tf_op jit(solution)/shard_map/all_gather | solution.py:1500
  253.6 2.5 collective-permute-start.43
  257.9 4.4 shard_map.355.refs_1_
  262.3 12.0 %shard_map.356.refs_2_ = bf16[2048,2816]{1,0:T(8,128)(2,1)} custom-call(s32[88]{0:T(128)S(1)} %reshape.471.order_ref, bf16[128,512,128]{2,1,0:T(8,128)(2,1)} %all-gather.5.cloned.1.call-done.refs_0_, bf16[192,512,128]{2,1,0:T(8,128)(2,1)} %all-gather.3.cloned.1.call-done.refs_1_.refs_0_, bf16[160,512,128]{2,1,0:T(8,128)(2,1)} %get-tuple-element.285.refs_2_), custom_call_target="tpu_custom_call" | custom-call | bytes 23068672 | tf_op jit(solution)/shard_map/pallas_call | solution.py:895
  278.6 6.8 %fusion.21 = f32[256,2816]{1,0:T(8,128)S(1)} fusion(bf16[2048,2816]{1,0:T(8,128)(2,1)} %shard_map.356.refs_2_, f32[2048]{0:T(1024)S(1)} %bitcast.215, f32[256]{0:T(256)S(1)} %get-tuple-element.539, bf16[256,512]{1,0:T(8,128)(2,1)} %copy-done.62, bf16[256,512]{1,0:T(8,128)(2,1)} %copy-done.64, bf16[256,512]{1,0:T(8,128)(2,1)} %copy-done.66, ...), kind=kOutput, calls=%fused_computation.80 | convolution fusion | flops 2958557184 | bytes 15475712 | tf_op jit(solution)/shard_map/dot_general | solution.py:1561
  285.4 3.7 multiply_convert_fusion.1
  291.8 4.5 shard_map.360
  296.3 4.9 shard_map.361
  301.2 4.8 shard_map.362
  306.3 8.5 %shard_map.363 = (bf16[256,512]{1,0:T(8,128)(2,1)S(1)}, bf16[256,512]{1,0:T(8,128)(2,1)S(1)}, bf16[256,512]{1,0:T(8,128)(2,1)S(1)}, bf16[256,512]{1,0:T(8,128)(2,1)S(1)}) custom-call(s32[1]{0:T(128)} %bitcast.62.part_ref, bf16[256,1408]{1,0:T(8,128)(2,1)S(1)} %copy-done.19, bf16[256,1408]{1,0:T(8,128)(2,1)S(1)} %copy-done.20, ...), custom_call_target="tpu_custom_call" | custom-call | flops 2952790016 | bytes 11534336 | tf_op jit(solution)/shard_map/pallas_call | solution.py:950
  315.1 4.1 collective-permute-start.47
  320.6 6.3 %collective-permute-done.45 = bf16[256,512]{1,0:T(8,128)(2,1)S(1)} collective-permute-done((bf16[256,512]{1,0:T(8,128)(2,1)S(1)}, bf16[256,512]{1,0:T(8,128)(2,1)S(1)}, u32[]{:S(2)}, u32[]{:S(2)}) %collective-permute-start.45) | collective-permute-done | bytes 262176 | tf_op jit(solution)/shard_map/ppermute | solution.py:967
  326.9 9.5 %collective-permute-done.46 = bf16[256,512]{1,0:T(8,128)(2,1)S(1)} collective-permute-done((bf16[256,512]{1,0:T(8,128)(2,1)S(1)}, bf16[256,512]{1,0:T(8,128)(2,1)S(1)}, u32[]{:S(2)}, u32[]{:S(2)}) %collective-permute-start.46) | collective-permute-done | bytes 262176 | tf_op jit(solution)/shard_map/ppermute | solution.py:967
  337.3 4.6 collective-permute-start.52
  341.9 2.4 collective-permute-start.53
  349.0 15.3 %collective-permute-done.49 = bf16[256,512]{1,0:T(8,128)(2,1)S(1)} collective-permute-done((bf16[256,512]{1,0:T(8,128)(2,1)S(1)}, bf16[256,512]{1,0:T(8,128)(2,1)S(1)}, u32[]{:S(2)}, u32[]{:S(2)}) %collective-permute-start.49) | collective-permute-done | bytes 262176 | tf_op jit(solution)/shard_map/ppermute | solution.py:967
  368.8 3.0 shard_map.364
  375.0 4.8 shard_map.368
  381.6 2.7 collective-permute-start.56
  384.8 3.9 shard_map.366
  388.8 4.0 shard_map.367
  393.7 4.9 collective-permute-start.63
  401.0 2.4 shard_map.369.d_leave_ref
  403.5 11.2 %shard_map.370 = (bf16[256,512]{1,0:T(8,128)(2,1)S(1)}, bf16[256,512]{1,0:T(8,128)(2,1)S(1)}, bf16[256,1024]{1,0:T(8,128)(2,1)S(1)}, f32[8,512]{1,0:T(8,128)S(1)...) custom-call(f32[272,1536]{1,0:T(8,128)} %copy-done.3, ...), custom_call_target="tpu_custom_call" | custom-call | tf_op jit(solution)/shard_map/pallas_call | solution.py:673
  419.8 4.0 shard_map.371
  423.8 3.1 shard_map.372
  426.9 3.1 shard_map.373
  432.8 8.4 %shard_map.374 = (bf16[256,512]{1,0:T(8,128)(2,1)S(1)}, bf16[256,512]{1,0:T(8,128)(2,1)S(1)}, bf16[256,512]{1,0:T(8,128)(2,1)S(1)}, bf16[256,512]{1,0:T(8,128)(2,1)S(1)}) custom-call(s32[1]{0:T(128)} %bitcast.62.part_ref, bf16[256,1536]{1,0:T(8,128)(2,1)S(1)} %fusion.32.right_ref.refs_0_, bf16[2048,1536]{1,0:T(8,128)(2,1)} %get-tuple-element.352.refs_1_, ...), custom_call_target="tpu_custom_call" | custom-call | flops 3355443200 | bytes 13107200 | tf_op jit(solution)/shard_map/pallas_call | solution.py:950
  447.1 3.2 collective-permute-done.66
  450.3 2.5 collective-permute-done.67
  452.9 6.5 %collective-permute-done.68 = bf16[256,512]{1,0:T(8,128)(2,1)S(1)} collective-permute-done((bf16[256,512]{1,0:T(8,128)(2,1)S(1)}, bf16[256,512]{1,0:T(8,128)(2,1)S(1)}, u32[]{:S(2)}, u32[]{:S(2)}) %collective-permute-start.68) | collective-permute-done | bytes 262176 | tf_op jit(solution)/shard_map/ppermute | solution.py:967
  459.5 2.4 fusion.19
  462.0 7.5 %collective-permute-start.70 = (f32[4,128]{1,0:T(4,128)S(1)}, f32[4,128]{1,0:T(4,128)S(1)}, u32[]{:S(2)}, u32[]{:S(2)}) collective-permute-start(f32[4,128]{1,0:T(4,128)S(1)} %pad_maximum_fusion.13), channel_id=1, source_target_pairs={{0,16},{8,24},{16,0},{24,8},{1,17},{9,25},{17,1},{25,9},{2,18},{10... | collective-permute-start | bytes 6152 | tf_op jit(solution)/shard_map/ppermute | solution.py:967
  469.5 3.2 collective-permute-start.71
  478.1 2.9 collective-permute-start.73
  481.0 5.9 collective-permute-done.73
  486.9 2.8 collective-permute-start.74
  489.7 2.6 fusion.16
  492.3 3.1 collective-permute-done.74
  495.4 17.1 %shard_map.375 = (f32[44,65536]{1,0:T(8,128)}, f32[44,65536]{1,0:T(8,128)}, f32[44,65536]{1,0:T(8,128)}, f32[44,65536]{1,0:T(8,128)}, bf16[44,65536]{1,0:T(8,128)(2,1)}) custom-call(s32[2]{0:T(128)S(1)} %pad_add_fusion.3.range_ref, s32[48]{0:T(128)S(1)} %copy-done.55, s32[48]{0:T(128)S(1)} %get-tuple-element.243.sources_ref, ...), custom_call_target="tpu_custom_call" | custom-call | flops 41943040 | bytes 33554432 | tf_op jit(solution)/shard_map/pallas_call | solution.py:1198
  512.6 58.9 %reduce-scatter.6.cloned.1.call-done.refs_2_ = bf16[20,512,128]{2,1,0:T(8,128)(2,1)} async-done(((bf16[160,512,128]{2,1,0:T(8,128)(2,1)}), bf16[20,512,128]{2,1,0:T(8,128)(2,1)}) %reduce-scatter.6.cloned.1.call-update) | async-done | bytes 2621456 | tf_op jit(solution)/shard_map/reduce_scatter | solution.py:1664
  580.7 17.3 %shard_map.376 = (f32[44,65536]{1,0:T(8,128)}, f32[44,65536]{1,0:T(8,128)}, f32[44,65536]{1,0:T(8,128)}, f32[44,65536]{1,0:T(8,128)}, bf16[44,65536]{1,0:T(8,128)(2,1)}) custom-call(s32[2]{0:T(128)S(1)} %iota_multiply_fusion.range_ref, s32[48]{0:T(128)S(1)} %copy-done.55, ...), custom_call_target="tpu_custom_call", output_to_operand_aliasing={{0}: (12, {}), {1}: (13, {}), {2}: (14, {}), {3}: (15, {}),... | custom-call | flops 20971520 | bytes 16777216 | tf_op jit(solution)/shard_map/pallas_call | solution.py:1198
  598.0 4.3 collective-permute-done.77.refs_5_
  602.2 16.6 %shard_map.378 = (f32[44,65536]{1,0:T(8,128)}, f32[44,65536]{1,0:T(8,128)}, f32[44,65536]{1,0:T(8,128)}, f32[44,65536]{1,0:T(8,128)}, bf16[44,65536]{1,0:T(8,128)(2,1)}) custom-call(s32[2]{0:T(128)S(1)} %pad_add_fusion.4.range_ref, s32[48]{0:T(128)S(1)} %copy-done.55, ...), custom_call_target="tpu_custom_call", output_to_operand_aliasing={{0}: (17, {}), {1}: (18, {}), {2}: (19, {}), {3}: (20, {}),... | custom-call | flops 41943040 | bytes 33554432 | tf_op jit(solution)/shard_map/pallas_call | solution.py:1198
  (533 shorter events, 127.9 us)
Async XLA Ops:
  7.2 148.3 %all-gather.3.cloned.1.call-start = ((), (), s32[]{:S(2)}) async-start(), calls=%async_computation.3 | async-start | bytes 28311552 | tf_op jit(solution)/shard_map/all_gather | solution.py:1451
  20.3 232.9 %all-gather.5.cloned.1.call-start = ((), (), s32[]{:S(2)}) async-start(), calls=%async_computation.4 | async-start | bytes 18874368 | tf_op jit(solution)/shard_map/all_gather | solution.py:1500
  24.4 52.1 %collective-permute-start.19 = (bf16[1,1088]{1,0:T(2,128)(2,1)S(1)}, bf16[1,1088]{1,0:T(2,128)(2,1)S(1)}, u32[]{:S(2)}, u32[]{:S(2)}) collective-permute-start(bf16[1,1088]{1,0:T(2,128)(2,1)S(1)} %get-tuple-element.500), channel_id=1, source_target_pairs={{0,16},{8,24},{16,0},{24,8},{1,17},{9,25},{17,1},{25,9},{2,18},{10... | collective-permute-start | bytes 6536 | tf_op jit(solution)/shard_map/ppermute | solution.py:967
  28.4 48.1 %collective-permute-start.18 = (bf16[1,1088]{1,0:T(2,128)(2,1)S(1)}, bf16[1,1088]{1,0:T(2,128)(2,1)S(1)}, u32[]{:S(2)}, u32[]{:S(2)}) collective-permute-start(bf16[1,1088]{1,0:T(2,128)(2,1)S(1)} %get-tuple-element.500), channel_id=1, source_target_pairs={{0,8},{8,0},{16,24},{24,16},{1,9},{9,1},{17,25},{25,17},{2,10},{10... | collective-permute-start | bytes 6536 | tf_op jit(solution)/shard_map/ppermute | solution.py:967
  30.0 46.5 %collective-permute-start.20 = (bf16[1,1088]{1,0:T(2,128)(2,1)S(1)}, bf16[1,1088]{1,0:T(2,128)(2,1)S(1)}, u32[]{:S(2)}, u32[]{:S(2)}) collective-permute-start(bf16[1,1088]{1,0:T(2,128)(2,1)S(1)} %get-tuple-element.500), channel_id=1, source_target_pairs={{0,24},{8,16},{16,8},{24,0},{1,25},{9,17},{17,9},{25,1},{2,26},{10... | collective-permute-start | bytes 6536 | tf_op jit(solution)/shard_map/ppermute | solution.py:967
  30.0 63.0 %collective-permute-start.16 = (bf16[256,512]{1,0:T(8,128)(2,1)S(1)}, bf16[256,512]{1,0:T(8,128)(2,1)}, u32[]{:S(2)}, u32[]{:S(2)}) collective-permute-start(bf16[256,512]{1,0:T(8,128)(2,1)S(1)} %copy-done.71), channel_id=1, source_target_pairs={{0,16},{8,24},{16,0},{24,8},{1,17},{9,25},{17,1},{25,9},{2,18},{10... | collective-permute-start | bytes 786440 | tf_op jit(solution)/shard_map/ppermute | solution.py:967
  73.9 22.3 %collective-permute-start.15 = (bf16[256,512]{1,0:T(8,128)(2,1)S(1)}, bf16[256,512]{1,0:T(8,128)(2,1)S(1)}, u32[]{:S(2)}, u32[]{:S(2)}) collective-permute-start(bf16[256,512]{1,0:T(8,128)(2,1)S(1)} %copy-done.71), channel_id=1, source_target_pairs={{0,8},{8,0},{16,24},{24,16},{1,9},{9,1},{17,25},{25,17},{2,10},{10... | collective-permute-start | bytes 786440 | tf_op jit(solution)/shard_map/ppermute | solution.py:967
  77.1 5.6 collective-permute-start.22
  78.8 3.9 collective-permute-start.21
  78.8 6.4 %collective-permute-start.24 = (bf16[242,128]{1,0:T(8,128)(2,1)S(1)}, bf16[242,128]{1,0:T(8,128)(2,1)S(1)}, u32[]{:S(2)}, u32[]{:S(2)}) collective-permute-start(bf16[242,128]{1,0:T(8,128)(2,1)S(1)} %bitcast.212), channel_id=1, source_target_pairs={{0,4},{1,5},{2,6},{3,7},{4,0},{5,1},{6,2},{7,3},{8,12},{9,13},{10,... | collective-permute-start | bytes 185864 | tf_op jit(solution)/shard_map/ppermute | solution.py:1000
  82.8 2.7 collective-permute-start.23
  82.8 7.1 %collective-permute-start.26 = (bf16[242,128]{1,0:T(8,128)(2,1)S(1)}, bf16[242,128]{1,0:T(8,128)(2,1)S(1)}, u32[]{:S(2)}, u32[]{:S(2)}) collective-permute-start(bf16[242,128]{1,0:T(8,128)(2,1)S(1)} %bitcast.213), channel_id=1, source_target_pairs={{0,6},{1,7},{2,4},{3,5},{4,2},{5,3},{6,0},{7,1},{8,14},{9,15},{10,... | collective-permute-start | bytes 185864 | tf_op jit(solution)/shard_map/ppermute | solution.py:1000
  85.3 4.6 collective-permute-start.25
  85.5 11.1 %collective-permute-start.17 = (bf16[256,512]{1,0:T(8,128)(2,1)S(1)}, bf16[256,512]{1,0:T(8,128)(2,1)S(1)}, u32[]{:S(2)}, u32[]{:S(2)}) collective-permute-start(bf16[256,512]{1,0:T(8,128)(2,1)S(1)} %copy-done.71), channel_id=1, source_target_pairs={{0,24},{8,16},{16,8},{24,0},{1,25},{9,17},{17,9},{25,1},{2,26},{10... | collective-permute-start | bytes 786440 | tf_op jit(solution)/shard_map/ppermute | solution.py:967
  89.9 26.9 %collective-permute-start.30 = (bf16[256,512]{1,0:T(8,128)(2,1)S(1)}, bf16[256,512]{1,0:T(8,128)(2,1)}, u32[]{:S(2)}, u32[]{:S(2)}) collective-permute-start(bf16[256,512]{1,0:T(8,128)(2,1)S(1)} %copy-done.74), channel_id=1, source_target_pairs={{0,16},{8,24},{16,0},{24,8},{1,17},{9,25},{17,1},{25,9},{2,18},{10... | collective-permute-start | bytes 786440 | tf_op jit(solution)/shard_map/ppermute | solution.py:967
  93.0 23.8 %collective-permute-start.29 = (bf16[256,512]{1,0:T(8,128)(2,1)S(1)}, bf16[256,512]{1,0:T(8,128)(2,1)}, u32[]{:S(2)}, u32[]{:S(2)}) collective-permute-start(bf16[256,512]{1,0:T(8,128)(2,1)S(1)} %copy-done.74), channel_id=1, source_target_pairs={{0,8},{8,0},{16,24},{24,16},{1,9},{9,1},{17,25},{25,17},{2,10},{10... | collective-permute-start | bytes 786440 | tf_op jit(solution)/shard_map/ppermute | solution.py:967
  93.0 23.7 %collective-permute-start.31 = (bf16[256,512]{1,0:T(8,128)(2,1)S(1)}, bf16[256,512]{1,0:T(8,128)(2,1)}, u32[]{:S(2)}, u32[]{:S(2)}) collective-permute-start(bf16[256,512]{1,0:T(8,128)(2,1)S(1)} %copy-done.74), channel_id=1, source_target_pairs={{0,24},{8,16},{16,8},{24,0},{1,25},{9,17},{17,9},{25,1},{2,26},{10... | collective-permute-start | bytes 786440 | tf_op jit(solution)/shard_map/ppermute | solution.py:967
  96.3 26.7 %collective-permute-start.14 = (bf16[4,512,128]{2,1,0:T(8,128)(2,1)}, bf16[4,512,128]{2,1,0:T(8,128)(2,1)}, u32[]{:S(2)}, u32[]{:S(2)}) collective-permute-start(bf16[4,512,128]{2,1,0:T(8,128)(2,1)} %slice.306), channel_id=1, source_target_pairs={{0,1},{1,0},{2,3},{3,2},{4,5},{5,4},{6,7},{7,6},{8,9},{9,8},{10,11... | collective-permute-start | bytes 1572872 | tf_op jit(solution)/shard_map/ppermute | solution.py:1455
  119.2 2.9 collective-permute-start.28
  155.6 275.9 %reduce-scatter.4.cloned.1.call-start = ((), (), s32[]{:S(2)}) async-start(), calls=%async_computation.5 | async-start | bytes 18874368 | tf_op jit(solution)/shard_map/reduce_scatter | solution.py:1599
  188.3 21.0 %collective-permute-start.35 = (bf16[2,128,384]{2,1,0:T(8,128)(2,1)}, bf16[2,128,384]{2,1,0:T(8,128)(2,1)}, u32[]{:S(2)}, u32[]{:S(2)}) collective-permute-start(bf16[2,128,384]{2,1,0:T(8,128)(2,1)} %shard_map.347), channel_id=1, source_target_pairs={{0,6},{1,7},{2,4},{3,5},{4,2},{5,3},{6,0},{7,1},{8,14},{9,15},{10,... | collective-permute-start | bytes 589832 | tf_op jit(solution)/shard_map/ppermute | solution.py:415
  189.8 19.5 %collective-permute-start.34 = (bf16[2,128,384]{2,1,0:T(8,128)(2,1)}, bf16[2,128,384]{2,1,0:T(8,128)(2,1)}, u32[]{:S(2)}, u32[]{:S(2)}) collective-permute-start(bf16[2,128,384]{2,1,0:T(8,128)(2,1)} %shard_map.347), channel_id=1, source_target_pairs={{0,4},{1,5},{2,6},{3,7},{4,0},{5,1},{6,2},{7,3},{8,12},{9,13},{10,... | collective-permute-start | bytes 589832 | tf_op jit(solution)/shard_map/ppermute | solution.py:415
  190.1 19.2 %collective-permute-start.33 = (bf16[2,128,384]{2,1,0:T(8,128)(2,1)}, bf16[2,128,384]{2,1,0:T(8,128)(2,1)}, u32[]{:S(2)}, u32[]{:S(2)}) collective-permute-start(bf16[2,128,384]{2,1,0:T(8,128)(2,1)} %shard_map.347), channel_id=1, source_target_pairs={{0,2},{1,3},{2,0},{3,1},{4,6},{5,7},{6,4},{7,5},{8,10},{9,11},{10,... | collective-permute-start | bytes 589832 | tf_op jit(solution)/shard_map/ppermute | solution.py:415
  209.4 1.9 collective-permute-start.37
  216.8 13.9 %collective-permute-start.39 = (bf16[256,512]{1,0:T(8,128)(2,1)S(1)}, bf16[256,512]{1,0:T(8,128)(2,1)S(1)}, u32[]{:S(2)}, u32[]{:S(2)}) collective-permute-start(bf16[256,512]{1,0:T(8,128)(2,1)S(1)} %get-tuple-element.277), channel_id=1, source_target_pairs={{0,8},{8,0},{16,24},{24,16},{1,9},{9,1},{17,25},{25,17},{2,10},{10... | collective-permute-start | bytes 786440 | tf_op jit(solution)/shard_map/ppermute | solution.py:967
  218.0 21.3 %collective-permute-start.40 = (bf16[256,512]{1,0:T(8,128)(2,1)S(1)}, bf16[256,512]{1,0:T(8,128)(2,1)S(1)}, u32[]{:S(2)}, u32[]{:S(2)}) collective-permute-start(bf16[256,512]{1,0:T(8,128)(2,1)S(1)} %get-tuple-element.278), channel_id=1, source_target_pairs={{0,16},{8,24},{16,0},{24,8},{1,17},{9,25},{17,1},{25,9},{2,18},{10... | collective-permute-start | bytes 786440 | tf_op jit(solution)/shard_map/ppermute | solution.py:967
  220.4 18.9 %collective-permute-start.41 = (bf16[256,512]{1,0:T(8,128)(2,1)S(1)}, bf16[256,512]{1,0:T(8,128)(2,1)S(1)}, u32[]{:S(2)}, u32[]{:S(2)}) collective-permute-start(bf16[256,512]{1,0:T(8,128)(2,1)S(1)} %get-tuple-element.279), channel_id=1, source_target_pairs={{0,24},{8,16},{16,8},{24,0},{1,25},{9,17},{17,9},{25,1},{2,26},{10... | collective-permute-start | bytes 786440 | tf_op jit(solution)/shard_map/ppermute | solution.py:967
  239.5 34.9 %collective-permute-start.44 = (bf16[256,512]{1,0:T(8,128)(2,1)S(1)}, bf16[256,512]{1,0:T(8,128)(2,1)S(1)}, u32[]{:S(2)}, u32[]{:S(2)}) collective-permute-start(bf16[256,512]{1,0:T(8,128)(2,1)S(1)} %fusion.39), channel_id=1, source_target_pairs={{0,24},{8,16},{16,8},{24,0},{1,25},{9,17},{17,9},{25,1},{2,26},{10... | collective-permute-start | bytes 786440 | tf_op jit(solution)/shard_map/ppermute | solution.py:967
  253.6 20.8 %collective-permute-start.43 = (bf16[256,512]{1,0:T(8,128)(2,1)S(1)}, bf16[256,512]{1,0:T(8,128)(2,1)S(1)}, u32[]{:S(2)}, u32[]{:S(2)}) collective-permute-start(bf16[256,512]{1,0:T(8,128)(2,1)S(1)} %fusion.39), channel_id=1, source_target_pairs={{0,16},{8,24},{16,0},{24,8},{1,17},{9,25},{17,1},{25,9},{2,18},{10... | collective-permute-start | bytes 786440 | tf_op jit(solution)/shard_map/ppermute | solution.py:967
  256.1 18.4 %collective-permute-start.42 = (bf16[256,512]{1,0:T(8,128)(2,1)S(1)}, bf16[256,512]{1,0:T(8,128)(2,1)S(1)}, u32[]{:S(2)}, u32[]{:S(2)}) collective-permute-start(bf16[256,512]{1,0:T(8,128)(2,1)S(1)} %fusion.39), channel_id=1, source_target_pairs={{0,8},{8,0},{16,24},{24,16},{1,9},{9,1},{17,25},{25,17},{2,10},{10... | collective-permute-start | bytes 786440 | tf_op jit(solution)/shard_map/ppermute | solution.py:967
  306.1 265.4 %reduce-scatter.6.cloned.1.call-start = ((), (), s32[]{:S(2)}) async-start(), calls=%async_computation.6 | async-start | bytes 23592960 | tf_op jit(solution)/shard_map/reduce_scatter | solution.py:1664
  314.8 12.1 %collective-permute-start.45 = (bf16[256,512]{1,0:T(8,128)(2,1)S(1)}, bf16[256,512]{1,0:T(8,128)(2,1)S(1)}, u32[]{:S(2)}, u32[]{:S(2)}) collective-permute-start(bf16[256,512]{1,0:T(8,128)(2,1)S(1)} %get-tuple-element.305), channel_id=1, source_target_pairs={{0,8},{8,0},{16,24},{24,16},{1,9},{9,1},{17,25},{25,17},{2,10},{10... | collective-permute-start | bytes 786440 | tf_op jit(solution)/shard_map/ppermute | solution.py:967
  315.0 21.4 %collective-permute-start.46 = (bf16[256,512]{1,0:T(8,128)(2,1)S(1)}, bf16[256,512]{1,0:T(8,128)(2,1)S(1)}, u32[]{:S(2)}, u32[]{:S(2)}) collective-permute-start(bf16[256,512]{1,0:T(8,128)(2,1)S(1)} %get-tuple-element.306), channel_id=1, source_target_pairs={{0,16},{8,24},{16,0},{24,8},{1,17},{9,25},{17,1},{25,9},{2,18},{10... | collective-permute-start | bytes 786440 | tf_op jit(solution)/shard_map/ppermute | solution.py:967
  315.1 21.3 %collective-permute-start.47 = (bf16[256,512]{1,0:T(8,128)(2,1)S(1)}, bf16[256,512]{1,0:T(8,128)(2,1)S(1)}, u32[]{:S(2)}, u32[]{:S(2)}) collective-permute-start(bf16[256,512]{1,0:T(8,128)(2,1)S(1)} %get-tuple-element.307), channel_id=1, source_target_pairs={{0,24},{8,16},{16,8},{24,0},{1,25},{9,17},{17,9},{25,1},{2,26},{10... | collective-permute-start | bytes 786440 | tf_op jit(solution)/shard_map/ppermute | solution.py:967
  337.3 9.3 %collective-permute-start.52 = (f32[2,128]{1,0:T(2,128)S(1)}, f32[2,128]{1,0:T(2,128)S(1)}, u32[]{:S(2)}, u32[]{:S(2)}) collective-permute-start(f32[2,128]{1,0:T(2,128)S(1)} %bitcast.235), channel_id=1, source_target_pairs={{0,16},{8,24},{16,0},{24,8},{1,17},{9,25},{17,1},{25,9},{2,18},{10... | collective-permute-start | bytes 3080 | tf_op jit(solution)/shard_map/ppermute | solution.py:967
  341.9 7.0 %collective-permute-start.53 = (f32[2,128]{1,0:T(2,128)S(1)}, f32[2,128]{1,0:T(2,128)S(1)}, u32[]{:S(2)}, u32[]{:S(2)}) collective-permute-start(f32[2,128]{1,0:T(2,128)S(1)} %bitcast.236), channel_id=1, source_target_pairs={{0,24},{8,16},{16,8},{24,0},{1,25},{9,17},{17,9},{25,1},{2,26},{10... | collective-permute-start | bytes 3080 | tf_op jit(solution)/shard_map/ppermute | solution.py:967
  344.4 4.6 collective-permute-start.51
  344.4 19.8 %collective-permute-start.49 = (bf16[256,512]{1,0:T(8,128)(2,1)S(1)}, bf16[256,512]{1,0:T(8,128)(2,1)S(1)}, u32[]{:S(2)}, u32[]{:S(2)}) collective-permute-start(bf16[256,512]{1,0:T(8,128)(2,1)S(1)} %convert_element_type.217), channel_id=1, source_target_pairs={{0,16},{8,24},{16,0},{24,8},{1,17},{9,25},{17,1},{25,9},{2,18},{10... | collective-permute-start | bytes 786440 | tf_op jit(solution)/shard_map/ppermute | solution.py:967
  346.4 17.8 %collective-permute-start.48 = (bf16[256,512]{1,0:T(8,128)(2,1)S(1)}, bf16[256,512]{1,0:T(8,128)(2,1)S(1)}, u32[]{:S(2)}, u32[]{:S(2)}) collective-permute-start(bf16[256,512]{1,0:T(8,128)(2,1)S(1)} %convert_element_type.217), channel_id=1, source_target_pairs={{0,8},{8,0},{16,24},{24,16},{1,9},{9,1},{17,25},{25,17},{2,10},{10... | collective-permute-start | bytes 786440 | tf_op jit(solution)/shard_map/ppermute | solution.py:967
  346.6 17.7 %collective-permute-start.50 = (bf16[256,512]{1,0:T(8,128)(2,1)S(1)}, bf16[256,512]{1,0:T(8,128)(2,1)S(1)}, u32[]{:S(2)}, u32[]{:S(2)}) collective-permute-start(bf16[256,512]{1,0:T(8,128)(2,1)S(1)} %convert_element_type.217), channel_id=1, source_target_pairs={{0,24},{8,16},{16,8},{24,0},{1,25},{9,17},{17,9},{25,1},{2,26},{10... | collective-permute-start | bytes 786440 | tf_op jit(solution)/shard_map/ppermute | solution.py:967
  372.8 7.1 %collective-permute-start.54 = (bf16[4,128,256]{2,1,0:T(8,128)(2,1)}, bf16[4,128,256]{2,1,0:T(8,128)(2,1)S(1)}, u32[]{:S(2)}, u32[]{:S(2)}) collective-permute-start(bf16[4,128,256]{2,1,0:T(8,128)(2,1)} %get-tuple-element.310.refs_0_), channel_id=1, source_target_pairs={{0,1},{1,0},{2,3},{3,2},{4,5},{5,4},{6,7},{7,6},{8,9},{9,8},{10,11... | collective-permute-start | bytes 786440 | tf_op jit(solution)/shard_map/ppermute | solution.py:415
  381.2 11.7 %collective-permute-start.57 = (bf16[2,128,256]{2,1,0:T(8,128)(2,1)S(1)}, bf16[2,128,256]{2,1,0:T(8,128)(2,1)S(1)}, u32[]{:S(2)}, u32[]{:S(2)}) collective-permute-start(bf16[2,128,256]{2,1,0:T(8,128)(2,1)S(1)} %shard_map.365), channel_id=1, source_target_pairs={{0,6},{1,7},{2,4},{3,5},{4,2},{5,3},{6,0},{7,1},{8,14},{9,15},{10,... | collective-permute-start | bytes 393224 | tf_op jit(solution)/shard_map/ppermute | solution.py:415
  381.6 11.3 %collective-permute-start.56 = (bf16[2,128,256]{2,1,0:T(8,128)(2,1)S(1)}, bf16[2,128,256]{2,1,0:T(8,128)(2,1)S(1)}, u32[]{:S(2)}, u32[]{:S(2)}) collective-permute-start(bf16[2,128,256]{2,1,0:T(8,128)(2,1)S(1)} %shard_map.365), channel_id=1, source_target_pairs={{0,4},{1,5},{2,6},{3,7},{4,0},{5,1},{6,2},{7,3},{8,12},{9,13},{10,... | collective-permute-start | bytes 393224 | tf_op jit(solution)/shard_map/ppermute | solution.py:415
  384.3 8.6 %collective-permute-start.55 = (bf16[2,128,256]{2,1,0:T(8,128)(2,1)S(1)}, bf16[2,128,256]{2,1,0:T(8,128)(2,1)S(1)}, u32[]{:S(2)}, u32[]{:S(2)}) collective-permute-start(bf16[2,128,256]{2,1,0:T(8,128)(2,1)S(1)} %shard_map.365), channel_id=1, source_target_pairs={{0,2},{1,3},{2,0},{3,1},{4,6},{5,7},{6,4},{7,5},{8,10},{9,11},{10,... | collective-permute-start | bytes 393224 | tf_op jit(solution)/shard_map/ppermute | solution.py:415
  392.9 5.7 collective-permute-start.58
  393.0 8.0 %collective-permute-start.59 = (bf16[2,128,256]{2,1,0:T(8,128)(2,1)S(1)}, bf16[2,128,256]{2,1,0:T(8,128)(2,1)S(1)}, u32[]{:S(2)}, u32[]{:S(2)}) collective-permute-start(bf16[2,128,256]{2,1,0:T(8,128)(2,1)S(1)} %collective-permute-done.56.refs_10_), channel_id=1, source_target_pairs={{0,1},{1,0},{2,3},{3,2},{4,5},{5,4},{6,7},{7,6},{8,9},{9,8},{10,11... | collective-permute-start | bytes 393224 | tf_op jit(solution)/shard_map/ppermute | solution.py:415
  393.5 7.5 %collective-permute-start.60 = (bf16[2,128,256]{2,1,0:T(8,128)(2,1)S(1)}, bf16[2,128,256]{2,1,0:T(8,128)(2,1)S(1)}, u32[]{:S(2)}, u32[]{:S(2)}) collective-permute-start(bf16[2,128,256]{2,1,0:T(8,128)(2,1)S(1)} %collective-permute-done.57.refs_12_), channel_id=1, source_target_pairs={{0,1},{1,0},{2,3},{3,2},{4,5},{5,4},{6,7},{7,6},{8,9},{9,8},{10,11... | collective-permute-start | bytes 393224 | tf_op jit(solution)/shard_map/ppermute | solution.py:415
  393.7 36.4 %collective-permute-start.63 = (bf16[256,512]{1,0:T(8,128)(2,1)S(1)}, bf16[256,512]{1,0:T(8,128)(2,1)S(1)}, u32[]{:S(2)}, u32[]{:S(2)}) collective-permute-start(bf16[256,512]{1,0:T(8,128)(2,1)S(1)} %get-tuple-element.343), channel_id=1, source_target_pairs={{0,8},{8,0},{16,24},{24,16},{1,9},{9,1},{17,25},{25,17},{2,10},{10... | collective-permute-start | bytes 786440 | tf_op jit(solution)/shard_map/ppermute | solution.py:967
  398.6 31.4 %collective-permute-start.64 = (bf16[256,512]{1,0:T(8,128)(2,1)S(1)}, bf16[256,512]{1,0:T(8,128)(2,1)S(1)}, u32[]{:S(2)}, u32[]{:S(2)}) collective-permute-start(bf16[256,512]{1,0:T(8,128)(2,1)S(1)} %get-tuple-element.344), channel_id=1, source_target_pairs={{0,16},{8,24},{16,0},{24,8},{1,17},{9,25},{17,1},{25,9},{2,18},{10... | collective-permute-start | bytes 786440 | tf_op jit(solution)/shard_map/ppermute | solution.py:967
  398.6 32.8 %collective-permute-start.65 = (bf16[256,512]{1,0:T(8,128)(2,1)S(1)}, bf16[256,512]{1,0:T(8,128)(2,1)}, u32[]{:S(2)}, u32[]{:S(2)}) collective-permute-start(bf16[256,512]{1,0:T(8,128)(2,1)S(1)} %get-tuple-element.345), channel_id=1, source_target_pairs={{0,24},{8,16},{16,8},{24,0},{1,25},{9,17},{17,9},{25,1},{2,26},{10... | collective-permute-start | bytes 786440 | tf_op jit(solution)/shard_map/ppermute | solution.py:967
  414.8 3.1 collective-permute-start.61
  416.1 3.7 collective-permute-start.62
  441.3 9.1 %collective-permute-start.66 = (bf16[256,512]{1,0:T(8,128)(2,1)S(1)}, bf16[256,512]{1,0:T(8,128)(2,1)S(1)}, u32[]{:S(2)}, u32[]{:S(2)}) collective-permute-start(bf16[256,512]{1,0:T(8,128)(2,1)S(1)} %get-tuple-element.356), channel_id=1, source_target_pairs={{0,8},{8,0},{16,24},{24,16},{1,9},{9,1},{17,25},{25,17},{2,10},{10... | collective-permute-start | bytes 786440 | tf_op jit(solution)/shard_map/ppermute | solution.py:967
  442.4 10.4 %collective-permute-start.67 = (bf16[256,512]{1,0:T(8,128)(2,1)S(1)}, bf16[256,512]{1,0:T(8,128)(2,1)S(1)}, u32[]{:S(2)}, u32[]{:S(2)}) collective-permute-start(bf16[256,512]{1,0:T(8,128)(2,1)S(1)} %get-tuple-element.357), channel_id=1, source_target_pairs={{0,16},{8,24},{16,0},{24,8},{1,17},{9,25},{17,1},{25,9},{2,18},{10... | collective-permute-start | bytes 786440 | tf_op jit(solution)/shard_map/ppermute | solution.py:967
  443.4 15.9 %collective-permute-start.68 = (bf16[256,512]{1,0:T(8,128)(2,1)S(1)}, bf16[256,512]{1,0:T(8,128)(2,1)S(1)}, u32[]{:S(2)}, u32[]{:S(2)}) collective-permute-start(bf16[256,512]{1,0:T(8,128)(2,1)S(1)} %get-tuple-element.358), channel_id=1, source_target_pairs={{0,24},{8,16},{16,8},{24,0},{1,25},{9,17},{17,9},{25,1},{2,26},{10... | collective-permute-start | bytes 786440 | tf_op jit(solution)/shard_map/ppermute | solution.py:967
  462.0 12.5 %collective-permute-start.70 = (f32[4,128]{1,0:T(4,128)S(1)}, f32[4,128]{1,0:T(4,128)S(1)}, u32[]{:S(2)}, u32[]{:S(2)}) collective-permute-start(f32[4,128]{1,0:T(4,128)S(1)} %pad_maximum_fusion.13), channel_id=1, source_target_pairs={{0,16},{8,24},{16,0},{24,8},{1,17},{9,25},{17,1},{25,9},{2,18},{10... | collective-permute-start | bytes 6152 | tf_op jit(solution)/shard_map/ppermute | solution.py:967
  469.5 5.4 collective-permute-start.71
  472.7 3.6 collective-permute-start.69
  478.1 8.8 %collective-permute-start.73 = (f32[208,128]{1,0:T(8,128)S(1)}, f32[208,128]{1,0:T(8,128)S(1)}, u32[]{:S(2)}, u32[]{:S(2)}) collective-permute-start(f32[208,128]{1,0:T(8,128)S(1)} %bitcast_add_fusion), channel_id=1, source_target_pairs={{0,2},{1,3},{2,0},{3,1},{4,6},{5,7},{6,4},{7,5},{8,10},{9,11},{10,... | collective-permute-start | bytes 319496 | tf_op jit(solution)/shard_map/ppermute | solution.py:1713
  486.9 8.4 %collective-permute-start.74 = (f32[208,128]{1,0:T(8,128)S(1)}, f32[208,128]{1,0:T(8,128)S(1)}, u32[]{:S(2)}, u32[]{:S(2)}) collective-permute-start(f32[208,128]{1,0:T(8,128)S(1)} %fusion.103), channel_id=1, source_target_pairs={{0,4},{1,5},{2,6},{3,7},{4,0},{5,1},{6,2},{7,3},{8,12},{9,13},{10,... | collective-permute-start | bytes 319496 | tf_op jit(solution)/shard_map/ppermute | solution.py:1713
  573.6 28.7 %collective-permute-start.75 = (bf16[6,512,128]{2,1,0:T(8,128)(2,1)}, bf16[6,512,128]{2,1,0:T(8,128)(2,1)S(1)}, u32[]{:S(2)}, u32[]{:S(2)}) collective-permute-start(bf16[6,512,128]{2,1,0:T(8,128)(2,1)} %slice.278), channel_id=1, source_target_pairs={{0,1},{1,0},{2,3},{3,2},{4,5},{5,4},{6,7},{7,6},{8,9},{9,8},{10,11... | collective-permute-start | bytes 2359304 | tf_op jit(solution)/shard_map/ppermute | solution.py:415
  575.5 22.5 %collective-permute-start.78 = (bf16[4,512,128]{2,1,0:T(8,128)(2,1)}, bf16[4,512,128]{2,1,0:T(8,128)(2,1)}, u32[]{:S(2)}, u32[]{:S(2)}) collective-permute-start(bf16[4,512,128]{2,1,0:T(8,128)(2,1)} %slice.279), channel_id=1, source_target_pairs={{0,6},{1,7},{2,4},{3,5},{4,2},{5,3},{6,0},{7,1},{8,14},{9,15},{10,... | collective-permute-start | bytes 1572872 | tf_op jit(solution)/shard_map/ppermute | solution.py:415
  576.9 25.3 %collective-permute-start.77 = (bf16[4,512,128]{2,1,0:T(8,128)(2,1)}, bf16[4,512,128]{2,1,0:T(8,128)(2,1)}, u32[]{:S(2)}, u32[]{:S(2)}) collective-permute-start(bf16[4,512,128]{2,1,0:T(8,128)(2,1)} %slice.279), channel_id=1, source_target_pairs={{0,4},{1,5},{2,6},{3,7},{4,0},{5,1},{6,2},{7,3},{8,12},{9,13},{10,... | collective-permute-start | bytes 1572872 | tf_op jit(solution)/shard_map/ppermute | solution.py:415
  578.3 24.0 %collective-permute-start.76 = (bf16[4,512,128]{2,1,0:T(8,128)(2,1)}, bf16[4,512,128]{2,1,0:T(8,128)(2,1)}, u32[]{:S(2)}, u32[]{:S(2)}) collective-permute-start(bf16[4,512,128]{2,1,0:T(8,128)(2,1)} %slice.279), channel_id=1, source_target_pairs={{0,2},{1,3},{2,0},{3,1},{4,6},{5,7},{6,4},{7,5},{8,10},{9,11},{10,... | collective-permute-start | bytes 1572872 | tf_op jit(solution)/shard_map/ppermute | solution.py:415
  (117 other events, 1739.7 us)
Sparse Core Ops, SparseCore 0:
  20.4 134.9 all-gather.2
  157.9 95.1 all-gather.4
  306.2 118.9 reduce-scatter.3
  431.6 139.7 reduce-scatter.5
where the time goes:
time: 629 us; the launch traced here: 626 us
  waiting for transfers between devices  208 us (33%)
  Pallas kernels  202 us (32%)
  starting transfers between devices  91.6 us (15%)
  local copies, waits for them, and re-layouts  53.3 us (8%)
  other arithmetic  30.9 us (5%)
  between operations  25.5 us (4%)
  matrix products  13.7 us (2%)
    ppermute x33, waiting for transfers between devices, exchange(): lax.ppermute(blocks[m], axis, [(i, i ^ m) for i in range(devices)])  80.4 us
    ppermute x33, starting transfers between devices, exchange(): lax.ppermute(blocks[m], axis, [(i, i ^ m) for i in range(devices)])  62.9 us
    reduce_scatter x1, waiting for transfers between devices, on_device(): lax.psum_scatter(second_table, 'seq', scatter_dimension=0, tiled=True)  58.9 us
    pallas_call x3, Pallas kernels, optimizer_update(): pl.pallas_call(kernel, grid_spec=pltpu.PrefetchScalarGridSpec(num_scalar_...  51 us
    pallas_call x5, Pallas kernels, assemble(): pl.pallas_call(kernel, grid_spec=pltpu.PrefetchScalarGridSpec(num_scalar_...  37.6 us
    pallas_call x8, Pallas kernels, weight_grad_blocks(): pl.pallas_call(kernel, grid_spec=pltpu.PrefetchScalarGridSpec(num_scalar_...  32.3 us
    all_gather x1, waiting for transfers between devices, on_device(): early_table = lax.all_gather(early_part, 'seq', axis=0, tiled=True)  29.8 us
    pallas_call x4, Pallas kernels, spread_products(): pl.pallas_call(kernel, in_specs=[pl.BlockSpec(memory_space=pltpu.SMEM)] +...  23 us
  transfers between devices with their start and end apart: 69, of which 29 were waited for; matrix products, arithmetic and copies ran while one was open for 10% of the time, Pallas kernels for 26%

commit v1 on v0

--- a/solution.py
+++ b/solution.py
@@ -961,6 +961,17 @@
     )(my_part, *flat)
 
 
+def stored(array):
+    def kernel(in_ref, out_ref):
+        out_ref[...] = in_ref[...]
+
+    return pl.pallas_call(
+        kernel,
+        out_shape=jax.ShapeDtypeStruct(array.shape, array.dtype),
+        compiler_params=params(),
+    )(array)
+
+
 def exchange(blocks, axis):
     devices = lax.axis_size(axis)
     return [blocks[0]] + [
@@ -1102,9 +1113,9 @@
 
 def optimizer_update(
     sources, slot_sources, slot_rows, slot_kinds, kinds_used, slot_masks, small_rates,
-    master, moment_one, moment_two, block_range, most_blocks, earlier,
+    master, moment_one, moment_two, capacity, block_range, most_blocks, earlier,
 ):
-    capacity, piece_size = master.shape
+    piece_size = master.shape[1]
     chunks = piece_size // CHUNK
     rows = CHUNK // LANES
     last_block = pl.cdiv(capacity, 8) - 1
@@ -1473,7 +1484,9 @@
     rows_wide = rows_full.astype(jnp.float32)
     scale_one = lax.rsqrt(jnp.mean(rows_wide * rows_wide, axis=-1, keepdims=True) + NORM_EPSILON)
     normed = (rows_wide * scale_one * gain_one).astype(jnp.bfloat16)
-    normed_ext = jnp.concatenate([shifted(normed[row_count - RIM :], "seq", 1), normed], axis=0)
+    normed_ext = stored(
+        jnp.concatenate([shifted(normed[row_count - RIM :], "seq", 1), normed], axis=0)
+    )
 
     decay_weight = jnp.pad(by_name["wab"], ((0, 0), (0, LANES - 2 * local_heads)))
     decay_proj = jnp.dot(normed, decay_weight, preferred_element_type=jnp.float32)
@@ -1485,18 +1498,18 @@
         ((0, 6), (0, LANES - local_heads)),
     )
 
+    mixer_rest = gather_rest(late_part, 0, trips_gather, most_gather, extra_step)
     beside = (
-        trips_gather, late_part, late_send, normed, normed_ext, scale_one, decay_proj, decay_weight, taps, query_taps, scalars,
+        mixer_rest, late_part, late_send, normed, normed_ext, scale_one, decay_proj, decay_weight, taps, query_taps, scalars,
         back_full, mixer_fetch, mlp_fetch, store, gain_two, norm_row,
         slot_sources, slot_rows, slot_masks, ranges, trips_late, trips_reduce,
     )
     early_table, beside = lax.optimization_barrier((early_table, beside))
     (
-        trips_now, late_part, late_send, normed, normed_ext, scale_one, decay_proj, decay_weight, taps, query_taps, scalars,
+        mixer_rest, late_part, late_send, normed, normed_ext, scale_one, decay_proj, decay_weight, taps, query_taps, scalars,
         back_full, mixer_fetch, mlp_fetch, store, gain_two, norm_row,
         slot_sources, slot_rows, slot_masks, ranges, trips_late, trips_reduce,
     ) = beside
-    mixer_rest = gather_rest(late_part, 0, trips_now, most_gather, extra_step)
     late_table = lax.all_gather(late_send, "seq", axis=0, tiled=True)
 
     value_key_weights, value_key = assemble(
@@ -1718,7 +1731,7 @@
         small_block.astype(jnp.bfloat16), ((0, rows_of_piece - small_rows), (0, 0))
     )[None]
 
-    def update(sources, block_range, most_blocks, earlier):
+    def update(sources, block_range, most_blocks, states, earlier):
         return optimizer_update(
             sources,
             slot_sources,
@@ -1727,15 +1740,15 @@
             kinds_used,
             slot_masks,
             jnp.asarray(small_rates)[None, :],
-            master,
-            moment_one,
-            moment_two,
+            *states,
+            capacity,
             block_range,
             most_blocks,
             earlier,
         )
 
-    done = update([first_reduced, small_block], ranges[0], all_blocks - plain_blocks, [])
+    states = [master, moment_one, moment_two]
+    done = update([first_reduced, small_block], ranges[0], all_blocks - plain_blocks, states, [])
     done, second_reduced, input_grad, block_out = lax.optimization_barrier(
         (done, second_reduced, input_grad, block_out)
     )
@@ -1744,7 +1757,7 @@
         spilled.append(moved_by(second_reduced[second_room - most :], mask))
     sources = [first_reduced, small_block, second_reduced]
     if plain_blocks:
-        done = update(sources, ranges[1], plain_blocks, done)
+        done = update(sources, ranges[1], plain_blocks, states, done)
     done, spilled, rest_grads, trips_now = lax.optimization_barrier(
         (done, spilled, grad_tables[1], trips_reduce)
     )
@@ -1753,6 +1766,7 @@
         sources + spilled + [rest_reduced],
         ranges[2],
         all_blocks - plain_blocks,
+        states,
         done,
     )
     return (

time: 629 us -> 638 us (1.014)
  starting transfers between devices: 91.6 us -> 116 us
  waiting for transfers between devices: 208 us -> 186 us
  local copies, waits for them, and re-layouts: 53.3 us -> 63.5 us
    all_gather x1, waiting for transfers between devices: 29.8 us -> 0.01 us  [on_device(): early_table = lax.all_gather(early_part, 'seq', axis=0, tiled=True)]
    ppermute x18 -> x25, starting transfers between devices: 12.1 us -> 34.4 us  [moved_by(): lax.ppermute(array, 'seq', [(i, i ^ mask) for i in range(lax.axis_size('s...]
    ppermute x18 -> x25, waiting for transfers between devices: 7.39 us -> 19.3 us  [moved_by(): lax.ppermute(array, 'seq', [(i, i ^ mask) for i in range(lax.axis_size('s...]
    dynamic_update_slice x0 -> x8, local copies, waits for them, and re-layouts: none -> 6.89 us  [more(): table = lax.dynamic_update_slice_in_dim(table, block, place, axis=0)]
    unnamed x241 -> x240, local copies, waits for them, and re-layouts: 15.8 us -> 16.7 us
  transfers between devices with their start and end apart: 69 -> 76, of which waited for: 29 -> 31; matrix products, arithmetic and copies ran while one was open for 10% -> 11% of each run, Pallas kernels for 26% -> 26%
where the time goes in v1:
time: 638 us; the launch traced here: 636 us
  Pallas kernels  201 us (32%)
  waiting for transfers between devices  186 us (29%)
  starting transfers between devices  116 us (18%)
  local copies, waits for them, and re-layouts  63.5 us (10%)
  other arithmetic  30.9 us (5%)
  between operations  25.3 us (4%)
  matrix products  13.7 us (2%)
    ppermute x33, waiting for transfers between devices, exchange(): lax.ppermute(blocks[m], axis, [(i, i ^ m) for i in range(devices)])  81.5 us
    ppermute x33, starting transfers between devices, exchange(): lax.ppermute(blocks[m], axis, [(i, i ^ m) for i in range(devices)])  64.9 us
    reduce_scatter x1, waiting for transfers between devices, on_device(): lax.psum_scatter(second_table, 'seq', scatter_dimension=0, tiled=True)  53.6 us
    pallas_call x3, Pallas kernels, optimizer_update(): pl.pallas_call(kernel, grid_spec=pltpu.PrefetchScalarGridSpec(num_scalar_...  50.3 us
    pallas_call x5, Pallas kernels, assemble(): pl.pallas_call(kernel, grid_spec=pltpu.PrefetchScalarGridSpec(num_scalar_...  37.6 us
    ppermute x25, starting transfers between devices, moved_by(): lax.ppermute(array, 'seq', [(i, i ^ mask) for i in range(lax.axis_size('s...  34.4 us
    pallas_call x8, Pallas kernels, weight_grad_blocks(): pl.pallas_call(kernel, grid_spec=pltpu.PrefetchScalarGridSpec(num_scalar_...  32.2 us
    pallas_call x4, Pallas kernels, spread_products(): pl.pallas_call(kernel, in_specs=[pl.BlockSpec(memory_space=pltpu.SMEM)] +...  22.9 us
  transfers between devices with their start and end apart: 76, of which 31 were waited for; matrix products, arithmetic and copies ran while one was open for 11% of the time, Pallas kernels for 26%

profile of v1, /device:TPU:0, one launch (start us, length us, event | category | flops | bytes accessed | tf_op | source)
XLA Modules:
  0.0 636.5 jit_solution(11594255846673722754)
XLA Ops:
  11.4 8.5 %shard_map.342 = bf16[24,512,128]{2,1,0:T(8,128)(2,1)} custom-call(s32[48]{0:T(128)S(1)} %broadcast_add_fusion.1.kinds_ref, f32[44,65536]{1,0:T(8,128)} %refs_10_.1), custom_call_target="tpu_custom_call" | custom-call | tf_op jit(solution)/shard_map/pallas_call | solution.py:767
  24.0 4.0 collective-permute-start.19
  49.8 7.4 %shard_map.344 = bf16[20,512,128]{2,1,0:T(8,128)(2,1)S(1)} custom-call(s32[48]{0:T(128)S(1)} %broadcast_add_fusion.1.kinds_ref, f32[44,65536]{1,0:T(8,128)} %refs_10_.1), custom_call_target="tpu_custom_call" | custom-call | tf_op jit(solution)/shard_map/pallas_call | solution.py:767
  64.6 7.4 %compare_select_fusion.4 = (s32[48]{0:T(128)S(1)}, s32[48]{0:T(128)S(1)}, f32[1,48]{1,0:T(1,128)S(1)}) fusion(s32[48]{0:T(128)S(1)} %get-tuple-element.423, s32[]{:T(128)} %bitcast.54, s32[]{:T(128)} %bitcast.53, s32[]{:T(128)} %bitcast.52, s32[]{:T(128)} %bitcast.51, s32[]{:T(128)} %bitcast.50, s32[]{:T(128)} %bitcast.48, s32[]{:T(128)} %bitcast.46, ...), kind=kLoop, calls=%fused_computation.259 | loop fusion | flops 2256 | bytes 1008 | tf_op jit(solution)/shard_map/jit(_where)/select_n | solution.py:1428
  74.8 2.5 collective-permute-start.15
  81.2 2.4 collective-permute-done.22
  83.7 2.5 collective-permute-start.26
  86.8 4.0 collective-permute-done.26
  94.0 3.2 collective-permute-start.31
  99.7 18.1 %collective-permute-done.30 = bf16[256,512]{1,0:T(8,128)(2,1)} collective-permute-done((bf16[256,512]{1,0:T(8,128)(2,1)S(1)}, bf16[256,512]{1,0:T(8,128)(2,1)}, u32[]{:S(2)}, u32[]{:S(2)}) %collective-permute-start.30) | collective-permute-done | bytes 262176 | tf_op jit(solution)/shard_map/ppermute | solution.py:978
  126.5 3.1 slice.308
  129.6 39.9 %while.30 = (s32[]{:T(128)}, bf16[160,512,128]{2,1,0:T(8,128)(2,1)}, s32[]{:T(128)}, bf16[20,512,128]{2,1,0:T(8,128)(2,1)}, s32[]{:T(128)}, /*index=5*/s32[]{:T(...) while((s32[]{:T(128)}, ...), condition=%wide.region_7.8_spmd, body=%wide.region_6.7_spmd.sunk | while | flops 56 | bytes 11797571 | solution.py:1269
  131.4 19.3 %collective-permute-start.1 = (bf16[2,512,128]{2,1,0:T(8,128)(2,1)}, bf16[2,512,128]{2,1,0:T(8,128)(2,1)S(1)}, u32[]{:S(2)}, u32[]{:S(2)}) collective-permute-start(bf16[2,512,128]{2,1,0:T(8,128)(2,1)} %get-tuple-element.630), channel_id=1, source_target_pairs={{0,2},{1,3},{2,0},{3,1},{4,6},{5,7},{6,4},{7,5},{8,10},{9,11},{10,... | collective-permute-start | bytes 786440 | tf_op jit(solution)/shard_map/while/body/ppermute | solution.py:415
  150.7 2.7 collective-permute-start.5
  153.4 6.0 collective-permute-done.1
  159.4 3.7 collective-permute-done.5
  170.6 8.0 %shard_map.346 = (bf16[2048,1536]{1,0:T(8,128)(2,1)}, f32[272,1536]{1,0:T(8,128)S(1)}) custom-call(s32[48]{0:T(128)S(1)} %reshape.464.order_ref, bf16[272,2048]{1,0:T(8,128)(2,1)S(1)} %shard_map.345.refs_0_, bf16[192,512,128]{2,1,0:T(8,128)(2,1)} %all-gather.3.cloned.1.call-done.refs_1_.refs_0_, bf16[160,512,128]{2,1,0:T(8,128)(2,1)} %get-tuple-element.251.refs_2_.refs_1_), custom_call_target="tpu_custom_call" | custom-call | flops 1711276032 | bytes 12582912 | tf_op jit(solution)/shard_map/pallas_call | solution.py:895
  178.6 17.1 %shard_map.347 = (f32[4,256,256]{2,1,0:T(8,128)S(1)}, f32[4,256,256]{2,1,0:T(8,128)S(1)}, f32[4,256,128]{2,1,0:T(8,128)S(1)}, bf16[4,128,384]{2,1,0:T(8,128)(2,1)S(1)}) custom-call(f32[272,1536]{1,0:T(8,128)S(1)} %get-tuple-element.252.pv.pk, f32[272,1536]{1,0:T(8,128)S(1)} %get-tuple-element.252.pv.pk, f32[8,1536]{1,0:T(8,128)S(1)} %fusion.34.tv.tk, ...), custom_call_target="tpu_custom_call" | custom-call | tf_op jit(solution)/shard_map/pallas_call | solution.py:245
  205.5 3.8 shard_map.351.refs_1_
  209.4 9.3 %shard_map.349 = (bf16[2048,1536]{1,0:T(8,128)(2,1)}, f32[272,1536]{1,0:T(8,128)S(1)}) custom-call(s32[48]{0:T(128)S(1)} %reshape.467.order_ref, bf16[272,2048]{1,0:T(8,128)(2,1)S(1)} %shard_map.345.refs_0_, bf16[192,512,128]{2,1,0:T(8,128)(2,1)} %all-gather.3.cloned.1.call-done.refs_1_.refs_0_, bf16[160,512,128]{2,1,0:T(8,128)(2,1)} %get-tuple-element.251.refs_2_.refs_1_), custom_call_target="tpu_custom_call" | custom-call | flops 1711276032 | bytes 12582912 | tf_op jit(solution)/shard_map/pallas_call | solution.py:895
  218.7 4.2 shard_map.350
  231.2 5.4 collective-permute-start.39
  240.3 6.9 %collective-permute-done.39 = bf16[256,512]{1,0:T(8,128)(2,1)S(1)} collective-permute-done((bf16[256,512]{1,0:T(8,128)(2,1)S(1)}, bf16[256,512]{1,0:T(8,128)(2,1)S(1)}, u32[]{:S(2)}, u32[]{:S(2)}) %collective-permute-start.39) | collective-permute-done | bytes 262176 | tf_op jit(solution)/shard_map/ppermute | solution.py:978
  247.2 10.8 %collective-permute-done.40 = bf16[256,512]{1,0:T(8,128)(2,1)S(1)} collective-permute-done((bf16[256,512]{1,0:T(8,128)(2,1)S(1)}, bf16[256,512]{1,0:T(8,128)(2,1)S(1)}, u32[]{:S(2)}, u32[]{:S(2)}) %collective-permute-start.40) | collective-permute-done | bytes 262176 | tf_op jit(solution)/shard_map/ppermute | solution.py:978
  258.9 10.9 %all-gather.5.cloned.1.call-done.refs_0_ = bf16[128,512,128]{2,1,0:T(8,128)(2,1)} async-done(((bf16[16,512,128]{2,1,0:T(8,128)(2,1)}), bf16[128,512,128]{2,1,0:T(8,128)(2,1)}) %all-gather.5.cloned.1.call-update) | async-done | bytes 16777232 | tf_op jit(solution)/shard_map/all_gather | solution.py:1513
  270.2 2.5 collective-permute-start.43
  274.6 4.4 shard_map.356.refs_1_
  279.0 12.0 %shard_map.357.refs_2_ = bf16[2048,2816]{1,0:T(8,128)(2,1)} custom-call(s32[88]{0:T(128)S(1)} %reshape.471.order_ref, bf16[128,512,128]{2,1,0:T(8,128)(2,1)} %all-gather.5.cloned.1.call-done.refs_0_, bf16[192,512,128]{2,1,0:T(8,128)(2,1)} %all-gather.3.cloned.1.call-done.refs_1_.refs_0_, bf16[160,512,128]{2,1,0:T(8,128)(2,1)} %get-tuple-element.285.refs_2_), custom_call_target="tpu_custom_call" | custom-call | bytes 23068672 | tf_op jit(solution)/shard_map/pallas_call | solution.py:895
  295.2 6.8 %fusion.21 = f32[256,2816]{1,0:T(8,128)S(1)} fusion(bf16[2048,2816]{1,0:T(8,128)(2,1)} %shard_map.357.refs_2_, f32[2048]{0:T(1024)S(1)} %bitcast.215, f32[256]{0:T(256)S(1)} %get-tuple-element.539, bf16[256,512]{1,0:T(8,128)(2,1)} %copy-done.61, bf16[256,512]{1,0:T(8,128)(2,1)} %copy-done.63, bf16[256,512]{1,0:T(8,128)(2,1)} %copy-done.65, ...), kind=kOutput, calls=%fused_computation.80 | convolution fusion | flops 2958557184 | bytes 15475712 | tf_op jit(solution)/shard_map/dot_general | solution.py:1574
  302.1 3.7 multiply_convert_fusion.1
  308.4 4.5 shard_map.361
  312.9 4.9 shard_map.362
  317.8 4.8 shard_map.363
  322.9 8.4 %shard_map.364 = (bf16[256,512]{1,0:T(8,128)(2,1)S(1)}, bf16[256,512]{1,0:T(8,128)(2,1)S(1)}, bf16[256,512]{1,0:T(8,128)(2,1)S(1)}, bf16[256,512]{1,0:T(8,128)(2,1)S(1)}) custom-call(s32[1]{0:T(128)} %bitcast.62.part_ref, bf16[256,1408]{1,0:T(8,128)(2,1)S(1)} %copy-done.19, bf16[256,1408]{1,0:T(8,128)(2,1)S(1)} %copy-done.20, ...), custom_call_target="tpu_custom_call" | custom-call | flops 2952790016 | bytes 11534336 | tf_op jit(solution)/shard_map/pallas_call | solution.py:950
  331.7 4.0 collective-permute-start.47
  337.1 6.4 %collective-permute-done.45 = bf16[256,512]{1,0:T(8,128)(2,1)S(1)} collective-permute-done((bf16[256,512]{1,0:T(8,128)(2,1)S(1)}, bf16[256,512]{1,0:T(8,128)(2,1)S(1)}, u32[]{:S(2)}, u32[]{:S(2)}) %collective-permute-start.45) | collective-permute-done | bytes 262176 | tf_op jit(solution)/shard_map/ppermute | solution.py:978
  343.5 9.3 %collective-permute-done.46 = bf16[256,512]{1,0:T(8,128)(2,1)S(1)} collective-permute-done((bf16[256,512]{1,0:T(8,128)(2,1)S(1)}, bf16[256,512]{1,0:T(8,128)(2,1)S(1)}, u32[]{:S(2)}, u32[]{:S(2)}) %collective-permute-start.46) | collective-permute-done | bytes 262176 | tf_op jit(solution)/shard_map/ppermute | solution.py:978
  353.7 4.8 collective-permute-start.52
  365.5 15.4 %collective-permute-done.49 = bf16[256,512]{1,0:T(8,128)(2,1)S(1)} collective-permute-done((bf16[256,512]{1,0:T(8,128)(2,1)S(1)}, bf16[256,512]{1,0:T(8,128)(2,1)S(1)}, u32[]{:S(2)}, u32[]{:S(2)}) %collective-permute-start.49) | collective-permute-done | bytes 262176 | tf_op jit(solution)/shard_map/ppermute | solution.py:978
  385.5 3.0 shard_map.365
  391.7 4.8 shard_map.369
  398.1 2.8 collective-permute-start.56
  401.4 3.9 shard_map.367
  405.4 3.9 shard_map.368
  410.1 5.1 collective-permute-start.63
  420.1 11.2 %shard_map.371 = (bf16[256,512]{1,0:T(8,128)(2,1)S(1)}, bf16[256,512]{1,0:T(8,128)(2,1)S(1)}, bf16[256,1024]{1,0:T(8,128)(2,1)S(1)}, f32[8,512]{1,0:T(8,128)S(1)...) custom-call(f32[272,1536]{1,0:T(8,128)} %copy-done.3, ...), custom_call_target="tpu_custom_call" | custom-call | tf_op jit(solution)/shard_map/pallas_call | solution.py:673
  436.4 4.0 shard_map.372
  440.4 3.1 shard_map.373
  443.6 3.1 shard_map.374
  449.4 8.4 %shard_map.375 = (bf16[256,512]{1,0:T(8,128)(2,1)S(1)}, bf16[256,512]{1,0:T(8,128)(2,1)S(1)}, bf16[256,512]{1,0:T(8,128)(2,1)S(1)}, bf16[256,512]{1,0:T(8,128)(2,1)S(1)}) custom-call(s32[1]{0:T(128)} %bitcast.62.part_ref, bf16[256,1536]{1,0:T(8,128)(2,1)S(1)} %fusion.32.right_ref.refs_0_, bf16[2048,1536]{1,0:T(8,128)(2,1)} %get-tuple-element.352.refs_1_, ...), custom_call_target="tpu_custom_call" | custom-call | flops 3355443200 | bytes 13107200 | tf_op jit(solution)/shard_map/pallas_call | solution.py:950
  463.7 3.4 collective-permute-done.66
  469.3 6.7 %collective-permute-done.68 = bf16[256,512]{1,0:T(8,128)(2,1)S(1)} collective-permute-done((bf16[256,512]{1,0:T(8,128)(2,1)S(1)}, bf16[256,512]{1,0:T(8,128)(2,1)S(1)}, u32[]{:S(2)}, u32[]{:S(2)}) %collective-permute-start.68) | collective-permute-done | bytes 262176 | tf_op jit(solution)/shard_map/ppermute | solution.py:978
  478.7 7.3 %collective-permute-start.70 = (f32[4,128]{1,0:T(4,128)S(1)}, f32[4,128]{1,0:T(4,128)S(1)}, u32[]{:S(2)}, u32[]{:S(2)}) collective-permute-start(f32[4,128]{1,0:T(4,128)S(1)} %pad_maximum_fusion.13), channel_id=1, source_target_pairs={{0,16},{8,24},{16,0},{24,8},{1,17},{9,25},{17,1},{25,9},{2,18},{10... | collective-permute-start | bytes 6152 | tf_op jit(solution)/shard_map/ppermute | solution.py:978
  486.0 3.3 collective-permute-start.71
  494.7 2.8 collective-permute-start.73
  497.6 5.9 collective-permute-done.73
  503.5 2.9 collective-permute-start.74
  506.4 2.6 fusion.16
  509.0 3.1 collective-permute-done.74
  512.1 22.5 %shard_map.376 = (f32[44,65536]{1,0:T(8,128)}, f32[44,65536]{1,0:T(8,128)}, f32[44,65536]{1,0:T(8,128)}, f32[44,65536]{1,0:T(8,128)}, bf16[44,65536]{1,0:T(8,128)(2,1)}) custom-call(s32[2]{0:T(128)S(1)} %pad_add_fusion.3.range_ref, s32[48]{0:T(128)S(1)} %copy-done.55, s32[48]{0:T(128)S(1)} %get-tuple-element.244.sources_ref, ...), custom_call_target="tpu_custom_call" | custom-call | flops 41943040 | bytes 33554432 | tf_op jit(solution)/shard_map/pallas_call | solution.py:1209
  534.6 53.6 %reduce-scatter.6.cloned.1.call-done.refs_2_ = bf16[20,512,128]{2,1,0:T(8,128)(2,1)} async-done(((bf16[160,512,128]{2,1,0:T(8,128)(2,1)}), bf16[20,512,128]{2,1,0:T(8,128)(2,1)}) %reduce-scatter.6.cloned.1.call-update) | async-done | bytes 2621456 | tf_op jit(solution)/shard_map/reduce_scatter | solution.py:1677
  597.4 17.1 %shard_map.377 = (f32[44,65536]{1,0:T(8,128)}, f32[44,65536]{1,0:T(8,128)}, f32[44,65536]{1,0:T(8,128)}, f32[44,65536]{1,0:T(8,128)}, bf16[44,65536]{1,0:T(8,128)(2,1)}) custom-call(s32[2]{0:T(128)S(1)} %iota_multiply_fusion.range_ref, s32[48]{0:T(128)S(1)} %copy-done.55, ...), custom_call_target="tpu_custom_call", output_to_operand_aliasing={{0}: (12, {}), {1}: (13, {}), {2}: (14, {}), {3}: (15, {}),... | custom-call | flops 20971520 | bytes 16777216 | tf_op jit(solution)/shard_map/pallas_call | solution.py:1209
  614.5 4.4 collective-permute-done.77.refs_5_
  619.0 10.7 %shard_map.379 = (f32[44,65536]{1,0:T(8,128)}, f32[44,65536]{1,0:T(8,128)}, f32[44,65536]{1,0:T(8,128)}, f32[44,65536]{1,0:T(8,128)}, bf16[44,65536]{1,0:T(8,128)(2,1)}) custom-call(s32[2]{0:T(128)S(1)} %pad_add_fusion.4.range_ref, s32[48]{0:T(128)S(1)} %copy-done.55, ...), custom_call_target="tpu_custom_call", output_to_operand_aliasing={{0}: (17, {}), {1}: (18, {}), {2}: (19, {}), {3}: (20, {}),... | custom-call | flops 41943040 | bytes 33554432 | tf_op jit(solution)/shard_map/pallas_call | solution.py:1209
  (555 shorter events, 148.1 us)
Async XLA Ops:
  7.2 162.4 %all-gather.3.cloned.1.call-start = ((), (), s32[]{:S(2)}) async-start(), calls=%async_computation.3 | async-start | bytes 28311552 | tf_op jit(solution)/shard_map/all_gather | solution.py:1462
  19.9 249.8 %all-gather.5.cloned.1.call-start = ((), (), s32[]{:S(2)}) async-start(), calls=%async_computation.4 | async-start | bytes 18874368 | tf_op jit(solution)/shard_map/all_gather | solution.py:1513
  24.0 53.4 %collective-permute-start.19 = (bf16[1,1088]{1,0:T(2,128)(2,1)S(1)}, bf16[1,1088]{1,0:T(2,128)(2,1)S(1)}, u32[]{:S(2)}, u32[]{:S(2)}) collective-permute-start(bf16[1,1088]{1,0:T(2,128)(2,1)S(1)} %get-tuple-element.500), channel_id=1, source_target_pairs={{0,16},{8,24},{16,0},{24,8},{1,17},{9,25},{17,1},{25,9},{2,18},{10... | collective-permute-start | bytes 6536 | tf_op jit(solution)/shard_map/ppermute | solution.py:978
  28.1 49.3 %collective-permute-start.18 = (bf16[1,1088]{1,0:T(2,128)(2,1)S(1)}, bf16[1,1088]{1,0:T(2,128)(2,1)S(1)}, u32[]{:S(2)}, u32[]{:S(2)}) collective-permute-start(bf16[1,1088]{1,0:T(2,128)(2,1)S(1)} %get-tuple-element.500), channel_id=1, source_target_pairs={{0,8},{8,0},{16,24},{24,16},{1,9},{9,1},{17,25},{25,17},{2,10},{10... | collective-permute-start | bytes 6536 | tf_op jit(solution)/shard_map/ppermute | solution.py:978
  29.6 47.8 %collective-permute-start.20 = (bf16[1,1088]{1,0:T(2,128)(2,1)S(1)}, bf16[1,1088]{1,0:T(2,128)(2,1)S(1)}, u32[]{:S(2)}, u32[]{:S(2)}) collective-permute-start(bf16[1,1088]{1,0:T(2,128)(2,1)S(1)} %get-tuple-element.500), channel_id=1, source_target_pairs={{0,24},{8,16},{16,8},{24,0},{1,25},{9,17},{17,9},{25,1},{2,26},{10... | collective-permute-start | bytes 6536 | tf_op jit(solution)/shard_map/ppermute | solution.py:978
  29.6 64.3 %collective-permute-start.16 = (bf16[256,512]{1,0:T(8,128)(2,1)S(1)}, bf16[256,512]{1,0:T(8,128)(2,1)}, u32[]{:S(2)}, u32[]{:S(2)}) collective-permute-start(bf16[256,512]{1,0:T(8,128)(2,1)S(1)} %copy-done.70), channel_id=1, source_target_pairs={{0,16},{8,24},{16,0},{24,8},{1,17},{9,25},{17,1},{25,9},{2,18},{10... | collective-permute-start | bytes 786440 | tf_op jit(solution)/shard_map/ppermute | solution.py:978
  74.8 22.3 %collective-permute-start.15 = (bf16[256,512]{1,0:T(8,128)(2,1)S(1)}, bf16[256,512]{1,0:T(8,128)(2,1)S(1)}, u32[]{:S(2)}, u32[]{:S(2)}) collective-permute-start(bf16[256,512]{1,0:T(8,128)(2,1)S(1)} %copy-done.70), channel_id=1, source_target_pairs={{0,8},{8,0},{16,24},{24,16},{1,9},{9,1},{17,25},{25,17},{2,10},{10... | collective-permute-start | bytes 786440 | tf_op jit(solution)/shard_map/ppermute | solution.py:978
  78.0 5.6 collective-permute-start.22
  79.8 3.9 collective-permute-start.21
  79.8 6.5 %collective-permute-start.24 = (bf16[242,128]{1,0:T(8,128)(2,1)S(1)}, bf16[242,128]{1,0:T(8,128)(2,1)S(1)}, u32[]{:S(2)}, u32[]{:S(2)}) collective-permute-start(bf16[242,128]{1,0:T(8,128)(2,1)S(1)} %bitcast.212), channel_id=1, source_target_pairs={{0,4},{1,5},{2,6},{3,7},{4,0},{5,1},{6,2},{7,3},{8,12},{9,13},{10,... | collective-permute-start | bytes 185864 | tf_op jit(solution)/shard_map/ppermute | solution.py:1011
  83.7 7.1 %collective-permute-start.26 = (bf16[242,128]{1,0:T(8,128)(2,1)S(1)}, bf16[242,128]{1,0:T(8,128)(2,1)S(1)}, u32[]{:S(2)}, u32[]{:S(2)}) collective-permute-start(bf16[242,128]{1,0:T(8,128)(2,1)S(1)} %bitcast.213), channel_id=1, source_target_pairs={{0,6},{1,7},{2,4},{3,5},{4,2},{5,3},{6,0},{7,1},{8,14},{9,15},{10,... | collective-permute-start | bytes 185864 | tf_op jit(solution)/shard_map/ppermute | solution.py:1011
  86.3 4.5 collective-permute-start.25
  86.5 11.1 %collective-permute-start.17 = (bf16[256,512]{1,0:T(8,128)(2,1)S(1)}, bf16[256,512]{1,0:T(8,128)(2,1)S(1)}, u32[]{:S(2)}, u32[]{:S(2)}) collective-permute-start(bf16[256,512]{1,0:T(8,128)(2,1)S(1)} %copy-done.70), channel_id=1, source_target_pairs={{0,24},{8,16},{16,8},{24,0},{1,25},{9,17},{17,9},{25,1},{2,26},{10... | collective-permute-start | bytes 786440 | tf_op jit(solution)/shard_map/ppermute | solution.py:978
  90.8 27.0 %collective-permute-start.30 = (bf16[256,512]{1,0:T(8,128)(2,1)S(1)}, bf16[256,512]{1,0:T(8,128)(2,1)}, u32[]{:S(2)}, u32[]{:S(2)}) collective-permute-start(bf16[256,512]{1,0:T(8,128)(2,1)S(1)} %copy-done.73), channel_id=1, source_target_pairs={{0,16},{8,24},{16,0},{24,8},{1,17},{9,25},{17,1},{25,9},{2,18},{10... | collective-permute-start | bytes 786440 | tf_op jit(solution)/shard_map/ppermute | solution.py:978
  93.9 23.9 %collective-permute-start.29 = (bf16[256,512]{1,0:T(8,128)(2,1)S(1)}, bf16[256,512]{1,0:T(8,128)(2,1)}, u32[]{:S(2)}, u32[]{:S(2)}) collective-permute-start(bf16[256,512]{1,0:T(8,128)(2,1)S(1)} %copy-done.73), channel_id=1, source_target_pairs={{0,8},{8,0},{16,24},{24,16},{1,9},{9,1},{17,25},{25,17},{2,10},{10... | collective-permute-start | bytes 786440 | tf_op jit(solution)/shard_map/ppermute | solution.py:978
  94.0 23.8 %collective-permute-start.31 = (bf16[256,512]{1,0:T(8,128)(2,1)S(1)}, bf16[256,512]{1,0:T(8,128)(2,1)}, u32[]{:S(2)}, u32[]{:S(2)}) collective-permute-start(bf16[256,512]{1,0:T(8,128)(2,1)S(1)} %copy-done.73), channel_id=1, source_target_pairs={{0,24},{8,16},{16,8},{24,0},{1,25},{9,17},{17,9},{25,1},{2,26},{10... | collective-permute-start | bytes 786440 | tf_op jit(solution)/shard_map/ppermute | solution.py:978
  97.2 27.4 %collective-permute-start.14 = (bf16[4,512,128]{2,1,0:T(8,128)(2,1)}, bf16[4,512,128]{2,1,0:T(8,128)(2,1)}, u32[]{:S(2)}, u32[]{:S(2)}) collective-permute-start(bf16[4,512,128]{2,1,0:T(8,128)(2,1)} %slice.306), channel_id=1, source_target_pairs={{0,1},{1,0},{2,3},{3,2},{4,5},{5,4},{6,7},{7,6},{8,9},{9,8},{10,11... | collective-permute-start | bytes 1572872 | tf_op jit(solution)/shard_map/ppermute | solution.py:1466
  131.4 28.0 %collective-permute-start.1 = (bf16[2,512,128]{2,1,0:T(8,128)(2,1)}, bf16[2,512,128]{2,1,0:T(8,128)(2,1)S(1)}, u32[]{:S(2)}, u32[]{:S(2)}) collective-permute-start(bf16[2,512,128]{2,1,0:T(8,128)(2,1)} %get-tuple-element.630), channel_id=1, source_target_pairs={{0,2},{1,3},{2,0},{3,1},{4,6},{5,7},{6,4},{7,5},{8,10},{9,11},{10,... | collective-permute-start | bytes 786440 | tf_op jit(solution)/shard_map/while/body/ppermute | solution.py:415
  150.7 12.4 %collective-permute-start.5 = (bf16[2,512,128]{2,1,0:T(8,128)(2,1)}, bf16[2,512,128]{2,1,0:T(8,128)(2,1)S(1)}, u32[]{:S(2)}, u32[]{:S(2)}) collective-permute-start(bf16[2,512,128]{2,1,0:T(8,128)(2,1)} %get-tuple-element.630), channel_id=1, source_target_pairs={{0,6},{1,7},{2,4},{3,5},{4,2},{5,3},{6,0},{7,1},{8,14},{9,15},{10,... | collective-permute-start | bytes 786440 | tf_op jit(solution)/shard_map/while/body/ppermute | solution.py:415
  153.4 11.0 %collective-permute-start.3 = (bf16[2,512,128]{2,1,0:T(8,128)(2,1)}, bf16[2,512,128]{2,1,0:T(8,128)(2,1)S(1)}, u32[]{:S(2)}, u32[]{:S(2)}) collective-permute-start(bf16[2,512,128]{2,1,0:T(8,128)(2,1)} %get-tuple-element.630), channel_id=1, source_target_pairs={{0,4},{1,5},{2,6},{3,7},{4,0},{5,1},{6,2},{7,3},{8,12},{9,13},{10,... | collective-permute-start | bytes 786440 | tf_op jit(solution)/shard_map/while/body/ppermute | solution.py:415
  153.4 11.0 %collective-permute-start = (bf16[2,512,128]{2,1,0:T(8,128)(2,1)}, bf16[2,512,128]{2,1,0:T(8,128)(2,1)S(1)}, u32[]{:S(2)}, u32[]{:S(2)}) collective-permute-start(bf16[2,512,128]{2,1,0:T(8,128)(2,1)} %get-tuple-element.630), channel_id=1, source_target_pairs={{0,1},{1,0},{2,3},{3,2},{4,5},{5,4},{6,7},{7,6},{8,9},{9,8},{10,11... | collective-permute-start | bytes 786440 | tf_op jit(solution)/shard_map/while/body/ppermute | solution.py:415
  159.4 6.5 %collective-permute-start.2 = (bf16[2,512,128]{2,1,0:T(8,128)(2,1)S(1)}, bf16[2,512,128]{2,1,0:T(8,128)(2,1)S(1)}, u32[]{:S(2)}, u32[]{:S(2)}) collective-permute-start(bf16[2,512,128]{2,1,0:T(8,128)(2,1)S(1)} %collective-permute-done.1), channel_id=1, source_target_pairs={{0,1},{1,0},{2,3},{3,2},{4,5},{5,4},{6,7},{7,6},{8,9},{9,8},{10,11... | collective-permute-start | bytes 786440 | tf_op jit(solution)/shard_map/while/body/ppermute | solution.py:415
  163.1 5.7 collective-permute-start.6
  169.7 278.4 %reduce-scatter.4.cloned.1.call-start = ((), (), s32[]{:S(2)}) async-start(), calls=%async_computation.5 | async-start | bytes 18874368 | tf_op jit(solution)/shard_map/reduce_scatter | solution.py:1612
  201.9 21.1 %collective-permute-start.35 = (bf16[2,128,384]{2,1,0:T(8,128)(2,1)}, bf16[2,128,384]{2,1,0:T(8,128)(2,1)}, u32[]{:S(2)}, u32[]{:S(2)}) collective-permute-start(bf16[2,128,384]{2,1,0:T(8,128)(2,1)} %shard_map.348), channel_id=1, source_target_pairs={{0,6},{1,7},{2,4},{3,5},{4,2},{5,3},{6,0},{7,1},{8,14},{9,15},{10,... | collective-permute-start | bytes 589832 | tf_op jit(solution)/shard_map/ppermute | solution.py:415
  204.0 19.0 %collective-permute-start.34 = (bf16[2,128,384]{2,1,0:T(8,128)(2,1)}, bf16[2,128,384]{2,1,0:T(8,128)(2,1)}, u32[]{:S(2)}, u32[]{:S(2)}) collective-permute-start(bf16[2,128,384]{2,1,0:T(8,128)(2,1)} %shard_map.348), channel_id=1, source_target_pairs={{0,4},{1,5},{2,6},{3,7},{4,0},{5,1},{6,2},{7,3},{8,12},{9,13},{10,... | collective-permute-start | bytes 589832 | tf_op jit(solution)/shard_map/ppermute | solution.py:415
  205.4 17.6 %collective-permute-start.33 = (bf16[2,128,384]{2,1,0:T(8,128)(2,1)}, bf16[2,128,384]{2,1,0:T(8,128)(2,1)}, u32[]{:S(2)}, u32[]{:S(2)}) collective-permute-start(bf16[2,128,384]{2,1,0:T(8,128)(2,1)} %shard_map.348), channel_id=1, source_target_pairs={{0,2},{1,3},{2,0},{3,1},{4,6},{5,7},{6,4},{7,5},{8,10},{9,11},{10,... | collective-permute-start | bytes 589832 | tf_op jit(solution)/shard_map/ppermute | solution.py:415
  231.2 16.0 %collective-permute-start.39 = (bf16[256,512]{1,0:T(8,128)(2,1)S(1)}, bf16[256,512]{1,0:T(8,128)(2,1)S(1)}, u32[]{:S(2)}, u32[]{:S(2)}) collective-permute-start(bf16[256,512]{1,0:T(8,128)(2,1)S(1)} %get-tuple-element.276), channel_id=1, source_target_pairs={{0,8},{8,0},{16,24},{24,16},{1,9},{9,1},{17,25},{25,17},{2,10},{10... | collective-permute-start | bytes 786440 | tf_op jit(solution)/shard_map/ppermute | solution.py:978
  236.6 21.3 %collective-permute-start.40 = (bf16[256,512]{1,0:T(8,128)(2,1)S(1)}, bf16[256,512]{1,0:T(8,128)(2,1)S(1)}, u32[]{:S(2)}, u32[]{:S(2)}) collective-permute-start(bf16[256,512]{1,0:T(8,128)(2,1)S(1)} %get-tuple-element.277), channel_id=1, source_target_pairs={{0,16},{8,24},{16,0},{24,8},{1,17},{9,25},{17,1},{25,9},{2,18},{10... | collective-permute-start | bytes 786440 | tf_op jit(solution)/shard_map/ppermute | solution.py:978
  236.6 21.3 %collective-permute-start.41 = (bf16[256,512]{1,0:T(8,128)(2,1)S(1)}, bf16[256,512]{1,0:T(8,128)(2,1)S(1)}, u32[]{:S(2)}, u32[]{:S(2)}) collective-permute-start(bf16[256,512]{1,0:T(8,128)(2,1)S(1)} %get-tuple-element.278), channel_id=1, source_target_pairs={{0,24},{8,16},{16,8},{24,0},{1,25},{9,17},{17,9},{25,1},{2,26},{10... | collective-permute-start | bytes 786440 | tf_op jit(solution)/shard_map/ppermute | solution.py:978
  258.2 32.9 %collective-permute-start.44 = (bf16[256,512]{1,0:T(8,128)(2,1)S(1)}, bf16[256,512]{1,0:T(8,128)(2,1)S(1)}, u32[]{:S(2)}, u32[]{:S(2)}) collective-permute-start(bf16[256,512]{1,0:T(8,128)(2,1)S(1)} %fusion.39), channel_id=1, source_target_pairs={{0,24},{8,16},{16,8},{24,0},{1,25},{9,17},{17,9},{25,1},{2,26},{10... | collective-permute-start | bytes 786440 | tf_op jit(solution)/shard_map/ppermute | solution.py:978
  270.2 20.8 %collective-permute-start.43 = (bf16[256,512]{1,0:T(8,128)(2,1)S(1)}, bf16[256,512]{1,0:T(8,128)(2,1)S(1)}, u32[]{:S(2)}, u32[]{:S(2)}) collective-permute-start(bf16[256,512]{1,0:T(8,128)(2,1)S(1)} %fusion.39), channel_id=1, source_target_pairs={{0,16},{8,24},{16,0},{24,8},{1,17},{9,25},{17,1},{25,9},{2,18},{10... | collective-permute-start | bytes 786440 | tf_op jit(solution)/shard_map/ppermute | solution.py:978
  272.7 18.4 %collective-permute-start.42 = (bf16[256,512]{1,0:T(8,128)(2,1)S(1)}, bf16[256,512]{1,0:T(8,128)(2,1)S(1)}, u32[]{:S(2)}, u32[]{:S(2)}) collective-permute-start(bf16[256,512]{1,0:T(8,128)(2,1)S(1)} %fusion.39), channel_id=1, source_target_pairs={{0,8},{8,0},{16,24},{24,16},{1,9},{9,1},{17,25},{25,17},{2,10},{10... | collective-permute-start | bytes 786440 | tf_op jit(solution)/shard_map/ppermute | solution.py:978
  322.7 265.5 %reduce-scatter.6.cloned.1.call-start = ((), (), s32[]{:S(2)}) async-start(), calls=%async_computation.6 | async-start | bytes 23592960 | tf_op jit(solution)/shard_map/reduce_scatter | solution.py:1677
  331.3 12.2 %collective-permute-start.45 = (bf16[256,512]{1,0:T(8,128)(2,1)S(1)}, bf16[256,512]{1,0:T(8,128)(2,1)S(1)}, u32[]{:S(2)}, u32[]{:S(2)}) collective-permute-start(bf16[256,512]{1,0:T(8,128)(2,1)S(1)} %get-tuple-element.305), channel_id=1, source_target_pairs={{0,8},{8,0},{16,24},{24,16},{1,9},{9,1},{17,25},{25,17},{2,10},{10... | collective-permute-start | bytes 786440 | tf_op jit(solution)/shard_map/ppermute | solution.py:978
  331.5 21.3 %collective-permute-start.46 = (bf16[256,512]{1,0:T(8,128)(2,1)S(1)}, bf16[256,512]{1,0:T(8,128)(2,1)S(1)}, u32[]{:S(2)}, u32[]{:S(2)}) collective-permute-start(bf16[256,512]{1,0:T(8,128)(2,1)S(1)} %get-tuple-element.306), channel_id=1, source_target_pairs={{0,16},{8,24},{16,0},{24,8},{1,17},{9,25},{17,1},{25,9},{2,18},{10... | collective-permute-start | bytes 786440 | tf_op jit(solution)/shard_map/ppermute | solution.py:978
  331.7 21.1 %collective-permute-start.47 = (bf16[256,512]{1,0:T(8,128)(2,1)S(1)}, bf16[256,512]{1,0:T(8,128)(2,1)S(1)}, u32[]{:S(2)}, u32[]{:S(2)}) collective-permute-start(bf16[256,512]{1,0:T(8,128)(2,1)S(1)} %get-tuple-element.307), channel_id=1, source_target_pairs={{0,24},{8,16},{16,8},{24,0},{1,25},{9,17},{17,9},{25,1},{2,26},{10... | collective-permute-start | bytes 786440 | tf_op jit(solution)/shard_map/ppermute | solution.py:978
  353.7 9.5 %collective-permute-start.52 = (f32[2,128]{1,0:T(2,128)S(1)}, f32[2,128]{1,0:T(2,128)S(1)}, u32[]{:S(2)}, u32[]{:S(2)}) collective-permute-start(f32[2,128]{1,0:T(2,128)S(1)} %bitcast.235), channel_id=1, source_target_pairs={{0,16},{8,24},{16,0},{24,8},{1,17},{9,25},{17,1},{25,9},{2,18},{10... | collective-permute-start | bytes 3080 | tf_op jit(solution)/shard_map/ppermute | solution.py:978
  358.5 7.0 %collective-permute-start.53 = (f32[2,128]{1,0:T(2,128)S(1)}, f32[2,128]{1,0:T(2,128)S(1)}, u32[]{:S(2)}, u32[]{:S(2)}) collective-permute-start(f32[2,128]{1,0:T(2,128)S(1)} %bitcast.236), channel_id=1, source_target_pairs={{0,24},{8,16},{16,8},{24,0},{1,25},{9,17},{17,9},{25,1},{2,26},{10... | collective-permute-start | bytes 3080 | tf_op jit(solution)/shard_map/ppermute | solution.py:978
  360.9 4.6 collective-permute-start.51
  361.0 19.9 %collective-permute-start.49 = (bf16[256,512]{1,0:T(8,128)(2,1)S(1)}, bf16[256,512]{1,0:T(8,128)(2,1)S(1)}, u32[]{:S(2)}, u32[]{:S(2)}) collective-permute-start(bf16[256,512]{1,0:T(8,128)(2,1)S(1)} %convert_element_type.217), channel_id=1, source_target_pairs={{0,16},{8,24},{16,0},{24,8},{1,17},{9,25},{17,1},{25,9},{2,18},{10... | collective-permute-start | bytes 786440 | tf_op jit(solution)/shard_map/ppermute | solution.py:978
  363.0 17.9 %collective-permute-start.48 = (bf16[256,512]{1,0:T(8,128)(2,1)S(1)}, bf16[256,512]{1,0:T(8,128)(2,1)S(1)}, u32[]{:S(2)}, u32[]{:S(2)}) collective-permute-start(bf16[256,512]{1,0:T(8,128)(2,1)S(1)} %convert_element_type.217), channel_id=1, source_target_pairs={{0,8},{8,0},{16,24},{24,16},{1,9},{9,1},{17,25},{25,17},{2,10},{10... | collective-permute-start | bytes 786440 | tf_op jit(solution)/shard_map/ppermute | solution.py:978
  363.2 17.8 %collective-permute-start.50 = (bf16[256,512]{1,0:T(8,128)(2,1)S(1)}, bf16[256,512]{1,0:T(8,128)(2,1)S(1)}, u32[]{:S(2)}, u32[]{:S(2)}) collective-permute-start(bf16[256,512]{1,0:T(8,128)(2,1)S(1)} %convert_element_type.217), channel_id=1, source_target_pairs={{0,24},{8,16},{16,8},{24,0},{1,25},{9,17},{17,9},{25,1},{2,26},{10... | collective-permute-start | bytes 786440 | tf_op jit(solution)/shard_map/ppermute | solution.py:978
  389.4 7.0 %collective-permute-start.54 = (bf16[4,128,256]{2,1,0:T(8,128)(2,1)}, bf16[4,128,256]{2,1,0:T(8,128)(2,1)S(1)}, u32[]{:S(2)}, u32[]{:S(2)}) collective-permute-start(bf16[4,128,256]{2,1,0:T(8,128)(2,1)} %get-tuple-element.310.refs_0_), channel_id=1, source_target_pairs={{0,1},{1,0},{2,3},{3,2},{4,5},{5,4},{6,7},{7,6},{8,9},{9,8},{10,11... | collective-permute-start | bytes 786440 | tf_op jit(solution)/shard_map/ppermute | solution.py:415
  397.8 11.5 %collective-permute-start.57 = (bf16[2,128,256]{2,1,0:T(8,128)(2,1)S(1)}, bf16[2,128,256]{2,1,0:T(8,128)(2,1)S(1)}, u32[]{:S(2)}, u32[]{:S(2)}) collective-permute-start(bf16[2,128,256]{2,1,0:T(8,128)(2,1)S(1)} %shard_map.366), channel_id=1, source_target_pairs={{0,6},{1,7},{2,4},{3,5},{4,2},{5,3},{6,0},{7,1},{8,14},{9,15},{10,... | collective-permute-start | bytes 393224 | tf_op jit(solution)/shard_map/ppermute | solution.py:415
  398.1 11.3 %collective-permute-start.56 = (bf16[2,128,256]{2,1,0:T(8,128)(2,1)S(1)}, bf16[2,128,256]{2,1,0:T(8,128)(2,1)S(1)}, u32[]{:S(2)}, u32[]{:S(2)}) collective-permute-start(bf16[2,128,256]{2,1,0:T(8,128)(2,1)S(1)} %shard_map.366), channel_id=1, source_target_pairs={{0,4},{1,5},{2,6},{3,7},{4,0},{5,1},{6,2},{7,3},{8,12},{9,13},{10,... | collective-permute-start | bytes 393224 | tf_op jit(solution)/shard_map/ppermute | solution.py:415
  400.9 8.5 %collective-permute-start.55 = (bf16[2,128,256]{2,1,0:T(8,128)(2,1)S(1)}, bf16[2,128,256]{2,1,0:T(8,128)(2,1)S(1)}, u32[]{:S(2)}, u32[]{:S(2)}) collective-permute-start(bf16[2,128,256]{2,1,0:T(8,128)(2,1)S(1)} %shard_map.366), channel_id=1, source_target_pairs={{0,2},{1,3},{2,0},{3,1},{4,6},{5,7},{6,4},{7,5},{8,10},{9,11},{10,... | collective-permute-start | bytes 393224 | tf_op jit(solution)/shard_map/ppermute | solution.py:415
  409.4 5.8 collective-permute-start.58
  409.5 8.1 %collective-permute-start.59 = (bf16[2,128,256]{2,1,0:T(8,128)(2,1)S(1)}, bf16[2,128,256]{2,1,0:T(8,128)(2,1)S(1)}, u32[]{:S(2)}, u32[]{:S(2)}) collective-permute-start(bf16[2,128,256]{2,1,0:T(8,128)(2,1)S(1)} %collective-permute-done.56.refs_10_), channel_id=1, source_target_pairs={{0,1},{1,0},{2,3},{3,2},{4,5},{5,4},{6,7},{7,6},{8,9},{9,8},{10,11... | collective-permute-start | bytes 393224 | tf_op jit(solution)/shard_map/ppermute | solution.py:415
  410.0 7.6 %collective-permute-start.60 = (bf16[2,128,256]{2,1,0:T(8,128)(2,1)S(1)}, bf16[2,128,256]{2,1,0:T(8,128)(2,1)S(1)}, u32[]{:S(2)}, u32[]{:S(2)}) collective-permute-start(bf16[2,128,256]{2,1,0:T(8,128)(2,1)S(1)} %collective-permute-done.57.refs_12_), channel_id=1, source_target_pairs={{0,1},{1,0},{2,3},{3,2},{4,5},{5,4},{6,7},{7,6},{8,9},{9,8},{10,11... | collective-permute-start | bytes 393224 | tf_op jit(solution)/shard_map/ppermute | solution.py:415
  410.1 36.5 %collective-permute-start.63 = (bf16[256,512]{1,0:T(8,128)(2,1)S(1)}, bf16[256,512]{1,0:T(8,128)(2,1)S(1)}, u32[]{:S(2)}, u32[]{:S(2)}) collective-permute-start(bf16[256,512]{1,0:T(8,128)(2,1)S(1)} %get-tuple-element.343), channel_id=1, source_target_pairs={{0,8},{8,0},{16,24},{24,16},{1,9},{9,1},{17,25},{25,17},{2,10},{10... | collective-permute-start | bytes 786440 | tf_op jit(solution)/shard_map/ppermute | solution.py:978
  415.2 31.4 %collective-permute-start.64 = (bf16[256,512]{1,0:T(8,128)(2,1)S(1)}, bf16[256,512]{1,0:T(8,128)(2,1)S(1)}, u32[]{:S(2)}, u32[]{:S(2)}) collective-permute-start(bf16[256,512]{1,0:T(8,128)(2,1)S(1)} %get-tuple-element.344), channel_id=1, source_target_pairs={{0,16},{8,24},{16,0},{24,8},{1,17},{9,25},{17,1},{25,9},{2,18},{10... | collective-permute-start | bytes 786440 | tf_op jit(solution)/shard_map/ppermute | solution.py:978
  415.2 32.8 %collective-permute-start.65 = (bf16[256,512]{1,0:T(8,128)(2,1)S(1)}, bf16[256,512]{1,0:T(8,128)(2,1)}, u32[]{:S(2)}, u32[]{:S(2)}) collective-permute-start(bf16[256,512]{1,0:T(8,128)(2,1)S(1)} %get-tuple-element.345), channel_id=1, source_target_pairs={{0,24},{8,16},{16,8},{24,0},{1,25},{9,17},{17,9},{25,1},{2,26},{10... | collective-permute-start | bytes 786440 | tf_op jit(solution)/shard_map/ppermute | solution.py:978
  457.9 9.3 %collective-permute-start.66 = (bf16[256,512]{1,0:T(8,128)(2,1)S(1)}, bf16[256,512]{1,0:T(8,128)(2,1)S(1)}, u32[]{:S(2)}, u32[]{:S(2)}) collective-permute-start(bf16[256,512]{1,0:T(8,128)(2,1)S(1)} %get-tuple-element.356), channel_id=1, source_target_pairs={{0,8},{8,0},{16,24},{24,16},{1,9},{9,1},{17,25},{25,17},{2,10},{10... | collective-permute-start | bytes 786440 | tf_op jit(solution)/shard_map/ppermute | solution.py:978
  459.1 10.3 %collective-permute-start.67 = (bf16[256,512]{1,0:T(8,128)(2,1)S(1)}, bf16[256,512]{1,0:T(8,128)(2,1)S(1)}, u32[]{:S(2)}, u32[]{:S(2)}) collective-permute-start(bf16[256,512]{1,0:T(8,128)(2,1)S(1)} %get-tuple-element.357), channel_id=1, source_target_pairs={{0,16},{8,24},{16,0},{24,8},{1,17},{9,25},{17,1},{25,9},{2,18},{10... | collective-permute-start | bytes 786440 | tf_op jit(solution)/shard_map/ppermute | solution.py:978
  460.1 15.9 %collective-permute-start.68 = (bf16[256,512]{1,0:T(8,128)(2,1)S(1)}, bf16[256,512]{1,0:T(8,128)(2,1)S(1)}, u32[]{:S(2)}, u32[]{:S(2)}) collective-permute-start(bf16[256,512]{1,0:T(8,128)(2,1)S(1)} %get-tuple-element.358), channel_id=1, source_target_pairs={{0,24},{8,16},{16,8},{24,0},{1,25},{9,17},{17,9},{25,1},{2,26},{10... | collective-permute-start | bytes 786440 | tf_op jit(solution)/shard_map/ppermute | solution.py:978
  478.7 12.4 %collective-permute-start.70 = (f32[4,128]{1,0:T(4,128)S(1)}, f32[4,128]{1,0:T(4,128)S(1)}, u32[]{:S(2)}, u32[]{:S(2)}) collective-permute-start(f32[4,128]{1,0:T(4,128)S(1)} %pad_maximum_fusion.13), channel_id=1, source_target_pairs={{0,16},{8,24},{16,0},{24,8},{1,17},{9,25},{17,1},{25,9},{2,18},{10... | collective-permute-start | bytes 6152 | tf_op jit(solution)/shard_map/ppermute | solution.py:978
  486.0 5.4 collective-permute-start.71
  494.7 8.8 %collective-permute-start.73 = (f32[208,128]{1,0:T(8,128)S(1)}, f32[208,128]{1,0:T(8,128)S(1)}, u32[]{:S(2)}, u32[]{:S(2)}) collective-permute-start(f32[208,128]{1,0:T(8,128)S(1)} %bitcast_add_fusion), channel_id=1, source_target_pairs={{0,2},{1,3},{2,0},{3,1},{4,6},{5,7},{6,4},{7,5},{8,10},{9,11},{10,... | collective-permute-start | bytes 319496 | tf_op jit(solution)/shard_map/ppermute | solution.py:1726
  503.5 8.5 %collective-permute-start.74 = (f32[208,128]{1,0:T(8,128)S(1)}, f32[208,128]{1,0:T(8,128)S(1)}, u32[]{:S(2)}, u32[]{:S(2)}) collective-permute-start(f32[208,128]{1,0:T(8,128)S(1)} %fusion.103), channel_id=1, source_target_pairs={{0,4},{1,5},{2,6},{3,7},{4,0},{5,1},{6,2},{7,3},{8,12},{9,13},{10,... | collective-permute-start | bytes 319496 | tf_op jit(solution)/shard_map/ppermute | solution.py:1726
  590.3 28.7 %collective-permute-start.75 = (bf16[6,512,128]{2,1,0:T(8,128)(2,1)}, bf16[6,512,128]{2,1,0:T(8,128)(2,1)S(1)}, u32[]{:S(2)}, u32[]{:S(2)}) collective-permute-start(bf16[6,512,128]{2,1,0:T(8,128)(2,1)} %slice.278), channel_id=1, source_target_pairs={{0,1},{1,0},{2,3},{3,2},{4,5},{5,4},{6,7},{7,6},{8,9},{9,8},{10,11... | collective-permute-start | bytes 2359304 | tf_op jit(solution)/shard_map/ppermute | solution.py:415
  592.2 22.3 %collective-permute-start.78 = (bf16[4,512,128]{2,1,0:T(8,128)(2,1)}, bf16[4,512,128]{2,1,0:T(8,128)(2,1)}, u32[]{:S(2)}, u32[]{:S(2)}) collective-permute-start(bf16[4,512,128]{2,1,0:T(8,128)(2,1)} %slice.279), channel_id=1, source_target_pairs={{0,6},{1,7},{2,4},{3,5},{4,2},{5,3},{6,0},{7,1},{8,14},{9,15},{10,... | collective-permute-start | bytes 1572872 | tf_op jit(solution)/shard_map/ppermute | solution.py:415
  593.7 25.3 %collective-permute-start.77 = (bf16[4,512,128]{2,1,0:T(8,128)(2,1)}, bf16[4,512,128]{2,1,0:T(8,128)(2,1)}, u32[]{:S(2)}, u32[]{:S(2)}) collective-permute-start(bf16[4,512,128]{2,1,0:T(8,128)(2,1)} %slice.279), channel_id=1, source_target_pairs={{0,4},{1,5},{2,6},{3,7},{4,0},{5,1},{6,2},{7,3},{8,12},{9,13},{10,... | collective-permute-start | bytes 1572872 | tf_op jit(solution)/shard_map/ppermute | solution.py:415
  595.0 24.0 %collective-permute-start.76 = (bf16[4,512,128]{2,1,0:T(8,128)(2,1)}, bf16[4,512,128]{2,1,0:T(8,128)(2,1)}, u32[]{:S(2)}, u32[]{:S(2)}) collective-permute-start(bf16[4,512,128]{2,1,0:T(8,128)(2,1)} %slice.279), channel_id=1, source_target_pairs={{0,2},{1,3},{2,0},{3,1},{4,6},{5,7},{6,4},{7,5},{8,10},{9,11},{10,... | collective-permute-start | bytes 1572872 | tf_op jit(solution)/shard_map/ppermute | solution.py:415
  (123 other events, 1770.2 us)
Sparse Core Ops, SparseCore 0:
  20.0 137.3 all-gather.2
  169.8 99.9 all-gather.4
  322.8 119.0 reduce-scatter.3
  448.2 139.9 reduce-scatter.5

commit v2 on v1

--- a/solution.py
+++ b/solution.py
@@ -742,8 +742,7 @@
 
 def pack_blocks(master, slot_kinds, kinds_used, first_slot, slot_count):
     piece_size = master.shape[1]
-    chunks = piece_size // CHUNK
-    rows = CHUNK // LANES
+    rows = piece_size // LANES
     first_block = first_slot // 8
     slot_blocks = pl.cdiv(slot_count, 8)
 
@@ -768,9 +767,9 @@
         kernel,
         grid_spec=pltpu.PrefetchScalarGridSpec(
             num_scalar_prefetch=1,
-            grid=(slot_blocks, chunks),
-            in_specs=[pl.BlockSpec((8, CHUNK), lambda i, j, kinds: (first_block + i, j))],
-            out_specs=pl.BlockSpec((8, rows, LANES), lambda i, j, kinds: (i, j, 0)),
+            grid=(slot_blocks,),
+            in_specs=[pl.BlockSpec((8, piece_size), lambda i, kinds: (first_block + i, 0))],
+            out_specs=pl.BlockSpec((8, rows, LANES), lambda i, kinds: (i, 0, 0)),
             scratch_shapes=[pltpu.VMEM((8 * rows, LANES), jnp.float32)],
         ),
         out_shape=jax.ShapeDtypeStruct((slot_count, piece_size // LANES, LANES), jnp.bfloat16),
@@ -1016,7 +1015,7 @@
     return rows, lax.axis_index("seq").astype(jnp.int32).reshape(1)
 
 
-def weight_grad_blocks(left_t, right, right_block, col_count, positions, tables, blocks_a_step):
+def weight_grad_blocks(left_t, rights, col_count, positions, tables, blocks_a_step):
     row_total, depth = left_t.shape
     tiles = col_count // LANES
     piece_rows = 512
@@ -1024,7 +1023,34 @@
     step_rows = blocks_a_step * piece_rows // tiles
     steps = row_total // step_rows
 
-    def kernel(positions_ref, left_ref, right_ref, *refs):
+    total_steps = steps * len(rights)
+
+    def multiply(left, right_ref, product, staged, slot):
+        for c in range(0, tiles, 2):
+            width = min(2, tiles - c)
+            part = jnp.dot(
+                left,
+                right_ref[:, LANES * c : LANES * (c + width)],
+                preferred_element_type=jnp.float32,
+            )
+            for w in range(width):
+                column = part[:, LANES * w : LANES * w + LANES]
+                if not even:
+                    product[pl.ds(c + w, step_rows, stride=tiles), :] = column
+                    continue
+                for row_tile in range(step_rows // TILE):
+                    block, row = divmod(TILE * (row_tile * tiles + c + w), piece_rows)
+                    staged[slot, block, row : row + TILE, :] = column[
+                        TILE * row_tile : TILE * row_tile + TILE
+                    ].astype(jnp.bfloat16)
+        if not even:
+            for block in range(blocks_a_step):
+                staged[slot, block] = product[
+                    piece_rows * block : piece_rows * block + piece_rows, :
+                ].astype(jnp.bfloat16)
+
+    def kernel(positions_ref, left_ref, *refs):
+        right_refs, refs = refs[: len(rights)], refs[len(rights) :]
         table_refs = refs[len(tables) : 2 * len(tables)]
         product, staged, sem = refs[2 * len(tables) :]
         g = pl.program_id(0)
@@ -1037,31 +1063,12 @@
         def _():
             settle(slot)
 
-        left = left_ref[...]
-        if even:
-            product[...] = jnp.dot(left, right_ref[...], preferred_element_type=jnp.float32)
-            for tile in range(step_rows // TILE * tiles):
-                row_tile, column = divmod(tile, tiles)
-                block, row = divmod(TILE * tile, piece_rows)
-                staged[slot, block, row : row + TILE, :] = product[
-                    TILE * row_tile : TILE * row_tile + TILE, LANES * column : LANES * column + LANES
-                ].astype(jnp.bfloat16)
-        else:
-            for c in range(0, tiles, 2):
-                width = min(2, tiles - c)
-                part = jnp.dot(
-                    left,
-                    right_ref[:, LANES * c : LANES * (c + width)],
-                    preferred_element_type=jnp.float32,
-                )
-                for w in range(width):
-                    product[pl.ds(c + w, step_rows, stride=tiles), :] = part[
-                        :, LANES * w : LANES * w + LANES
-                    ]
-            for block in range(blocks_a_step):
-                staged[slot, block] = product[
-                    piece_rows * block : piece_rows * block + piece_rows, :
-                ].astype(jnp.bfloat16)
+        for number, right_ref in enumerate(right_refs):
+
+            @pl.when(g // steps == number)
+            def _():
+                multiply(left_ref[...], right_ref, product, staged, slot)
+
         for block in range(blocks_a_step):
             position = positions_ref[g * blocks_a_step + block]
 
@@ -1075,23 +1082,27 @@
                         sem.at[slot],
                     ).start()
 
-        @pl.when(g == steps - 1)
+        @pl.when(g == total_steps - 1)
         def _():
             settle(slot)
-            if steps > 1:
+            if total_steps > 1:
                 settle(1 - slot)
 
     anywhere = pl.BlockSpec(memory_space=pl.ANY)
     in_specs = [
-        pl.BlockSpec((step_rows, depth), lambda g, positions: (g, 0)),
-        pl.BlockSpec((depth, col_count), lambda g, positions: (0, right_block)),
-    ] + [anywhere for table in tables]
-    product_shape = (step_rows, col_count) if even else (step_rows * tiles, LANES)
+        pl.BlockSpec((step_rows, depth), lambda g, positions: (lax.rem(g, steps), 0)),
+    ]
+    for right, right_block in rights:
+        in_specs.append(
+            pl.BlockSpec((depth, col_count), lambda g, positions, k=right_block: (0, k))
+        )
+    in_specs += [anywhere for table in tables]
+    product_shape = (8, LANES) if even else (step_rows * tiles, LANES)
     return pl.pallas_call(
         kernel,
         grid_spec=pltpu.PrefetchScalarGridSpec(
             num_scalar_prefetch=1,
-            grid=(steps,),
+            grid=(total_steps,),
             in_specs=in_specs,
             out_specs=[anywhere for table in tables],
             scratch_shapes=[
@@ -1101,14 +1112,14 @@
             ],
         ),
         out_shape=[jax.ShapeDtypeStruct(table.shape, table.dtype) for table in tables],
-        input_output_aliases={3 + i: i for i in range(len(tables))},
+        input_output_aliases={2 + len(rights) + i: i for i in range(len(tables))},
         cost_estimate=pl.CostEstimate(
-            flops=2 * row_total * depth * col_count,
-            bytes_accessed=2 * row_total * col_count,
+            flops=2 * len(rights) * row_total * depth * col_count,
+            bytes_accessed=2 * len(rights) * row_total * col_count,
             transcendentals=0,
         ),
         compiler_params=params(),
-    )(positions, left_t, right, *tables)
+    )(positions, left_t, *[right for right, right_block in rights], *tables)
 
 
 def optimizer_update(
@@ -1586,9 +1597,10 @@
         * (1.0 + gate_mlp * (1.0 - logistic_output_multiplier))
     ).astype(jnp.bfloat16)
     d_up_mlp = (d_hidden * silu_gate).astype(jnp.bfloat16)
-    def store_grad(tables, name, left_t, right, right_block, blocks_a_step):
+    def store_grad(tables, names, left_t, rights, blocks_a_step):
+        positions = jnp.concatenate([spots(store, name) for name in names])
         return weight_grad_blocks(
-            left_t, right, right_block, columns[name], spots(store, name), tables, blocks_a_step
+            left_t, rights, columns[names[0]], positions, tables, blocks_a_step
         )
 
     grad_tables = [
@@ -1599,10 +1611,11 @@
             most_reduce * seq_parts * extra_step,
         )
     ]
-    grad_tables = store_grad(grad_tables, "wdown", hidden.T, back_full, 0, 11)
+    grad_tables = store_grad(grad_tables, ["wdown"], hidden.T, [(back_full, 0)], 11)
     hidden_in_t = hidden_in.T
-    grad_tables = store_grad(grad_tables, "wgate", hidden_in_t, d_gate_mlp, 0, 11)
-    grad_tables = store_grad(grad_tables, "wup", hidden_in_t, d_up_mlp, 0, 11)
+    grad_tables = store_grad(
+        grad_tables, ["wgate", "wup"], hidden_in_t, [(d_gate_mlp, 0), (d_up_mlp, 0)], 11
+    )
     grad_tables, d_gate_mlp, d_up_mlp = lax.optimization_barrier(
         (grad_tables, d_gate_mlp, d_up_mlp)
     )
@@ -1637,8 +1650,8 @@
         local_heads, d_gated, recurred, query_gate, norm_row, reach
     )
     normed_t = normed.T
-    grad_tables = store_grad(grad_tables, "wo", gated_low.T, back_mix_full, 0, 8)
-    grad_tables = store_grad(grad_tables, "wg", normed_t, d_gate, 0, 8)
+    grad_tables = store_grad(grad_tables, ["wo"], gated_low.T, [(back_mix_full, 0)], 8)
+    grad_tables = store_grad(grad_tables, ["wg"], normed_t, [(d_gate, 0)], 8)
     d_leaving, (grad_tables, mlp_blocks) = leaving(
         local_heads, my_index_row, d_entering, kept_states, (grad_tables, mlp_blocks)
     )
@@ -1667,9 +1680,10 @@
     d_query, d_value_key = (
         with_rim(*parts) for parts in zip(d_conv, d_tail, d_rims)
     )
-    grad_tables = store_grad(grad_tables, "wv", normed_t, d_value_key, 0, 8)
-    grad_tables = store_grad(grad_tables, "wk", normed_t, d_value_key, 2, 4)
-    grad_tables = store_grad(grad_tables, "wq", normed_t, d_query, 0, 4)
+    grad_tables = store_grad(grad_tables, ["wv"], normed_t, [(d_value_key, 0)], 8)
+    grad_tables = store_grad(
+        grad_tables, ["wk", "wq"], normed_t, [(d_value_key, 2), (d_query, 0)], 4
+    )
     second_table, first_reduced, mlp_parts = lax.optimization_barrier(
         (grad_tables[0], first_reduced, mlp_parts)
     )

time: 638 us -> 630 us (0.987); the launches traced: 636 us -> 620 us
  starting transfers between devices: 116 us -> 90.9 us
  waiting for transfers between devices: 186 us -> 196 us
    all_gather x1, waiting for transfers between devices: 0.01 us -> 23.8 us  [on_device(): early_table = lax.all_gather(early_part, 'seq', axis=0, tiled=True)]
    ppermute x25 -> x18, starting transfers between devices: 34.4 us -> 12.1 us  [moved_by(): lax.ppermute(array, 'seq', [(i, i ^ mask) for i in range(lax.axis_size('s...]
    ppermute x25 -> x18, waiting for transfers between devices: 19.3 us -> 8.48 us  [moved_by(): lax.ppermute(array, 'seq', [(i, i ^ mask) for i in range(lax.axis_size('s...]
    dynamic_update_slice x8 -> x0, local copies, waits for them, and re-layouts: 6.89 us -> none  [more(): table = lax.dynamic_update_slice_in_dim(table, block, place, axis=0)]
    pallas_call x8 -> x6, Pallas kernels: 32.2 us -> 30.4 us  [weight_grad_blocks(): pl.pallas_call(kernel, grid_spec=pltpu.PrefetchScalarGridSpec(num_scalar_...]
    unnamed x240 -> x258, local copies, waits for them, and re-layouts: 16.7 us -> 16 us
  transfers between devices with their start and end apart: 76 -> 69, of which waited for: 31 -> 28; matrix products, arithmetic and copies ran while one was open for 11% -> 12% of each run, Pallas kernels for 26% -> 27%
where the time goes in v2:
time: 630 us; the launch traced here: 620 us
  Pallas kernels  196 us (31%)
  waiting for transfers between devices  196 us (31%)
  starting transfers between devices  90.9 us (14%)
  local copies, waits for them, and re-layouts  60.7 us (10%)
  other arithmetic  36.8 us (6%)
  between operations  25.4 us (4%)
  matrix products  13.6 us (2%)
    ppermute x33, waiting for transfers between devices, exchange(): lax.ppermute(blocks[m], axis, [(i, i ^ m) for i in range(devices)])  80.2 us
    ppermute x33, starting transfers between devices, exchange(): lax.ppermute(blocks[m], axis, [(i, i ^ m) for i in range(devices)])  62 us
    reduce_scatter x1, waiting for transfers between devices, on_device(): lax.psum_scatter(second_table, 'seq', scatter_dimension=0, tiled=True)  53.3 us
    pallas_call x3, Pallas kernels, optimizer_update(): pl.pallas_call(kernel, grid_spec=pltpu.PrefetchScalarGridSpec(num_scalar_...  50.2 us
    pallas_call x5, Pallas kernels, assemble(): pl.pallas_call(kernel, grid_spec=pltpu.PrefetchScalarGridSpec(num_scalar_...  37.6 us
    pallas_call x6, Pallas kernels, weight_grad_blocks(): pl.pallas_call(kernel, grid_spec=pltpu.PrefetchScalarGridSpec(num_scalar_...  30.4 us
    all_gather x1, waiting for transfers between devices, on_device(): early_table = lax.all_gather(early_part, 'seq', axis=0, tiled=True)  23.8 us
    pallas_call x4, Pallas kernels, spread_products(): pl.pallas_call(kernel, in_specs=[pl.BlockSpec(memory_space=pltpu.SMEM)] +...  22.9 us
  transfers between devices with their start and end apart: 69, of which 28 were waited for; matrix products, arithmetic and copies ran while one was open for 12% of the time, Pallas kernels for 27%

profile of v2, /device:TPU:0, one launch (start us, length us, event | category | flops | bytes accessed | tf_op | source)
XLA Modules:
  0.0 619.5 jit_solution(1782509669117226887)
XLA Ops:
  11.4 7.4 %shard_map.342 = bf16[24,512,128]{2,1,0:T(8,128)(2,1)} custom-call(s32[48]{0:T(128)S(1)} %broadcast_add_fusion.1.kinds_ref, f32[44,65536]{1,0:T(8,128)} %refs_10_.1), custom_call_target="tpu_custom_call" | custom-call | tf_op jit(solution)/shard_map/pallas_call | solution.py:766
  23.0 4.0 collective-permute-start.19
  48.8 6.3 %shard_map.344 = bf16[20,512,128]{2,1,0:T(8,128)(2,1)S(1)} custom-call(s32[48]{0:T(128)S(1)} %broadcast_add_fusion.1.kinds_ref, f32[44,65536]{1,0:T(8,128)} %refs_10_.1), custom_call_target="tpu_custom_call" | custom-call | tf_op jit(solution)/shard_map/pallas_call | solution.py:766
  64.0 7.4 %compare_select_fusion.4 = (s32[48]{0:T(128)S(1)}, s32[48]{0:T(128)S(1)}, f32[1,48]{1,0:T(1,128)S(1)}) fusion(s32[48]{0:T(128)S(1)} %get-tuple-element.413, s32[]{:T(128)} %bitcast.54, s32[]{:T(128)} %bitcast.53, s32[]{:T(128)} %bitcast.52, s32[]{:T(128)} %bitcast.51, s32[]{:T(128)} %bitcast.50, s32[]{:T(128)} %bitcast.48, s32[]{:T(128)} %bitcast.46, ...), kind=kLoop, calls=%fused_computation.259 | loop fusion | flops 2256 | bytes 1008 | tf_op jit(solution)/shard_map/jit(_where)/select_n | solution.py:1439
  75.5 2.6 collective-permute-start.15
  81.7 2.6 collective-permute-done.22
  84.3 2.4 collective-permute-start.26
  87.2 4.2 collective-permute-done.26
  95.2 3.2 collective-permute-start.31
  99.6 18.6 %collective-permute-done.30 = bf16[256,512]{1,0:T(8,128)(2,1)S(1)} collective-permute-done((bf16[256,512]{1,0:T(8,128)(2,1)S(1)}, bf16[256,512]{1,0:T(8,128)(2,1)S(1)}, u32[]{:S(2)}, u32[]{:S(2)}) %collective-permute-start.30) | collective-permute-done | bytes 262176 | tf_op jit(solution)/shard_map/ppermute | solution.py:977
  127.3 3.1 slice.303
  130.4 23.8 %all-gather.3.cloned.1.call-done.refs_1_.refs_0_ = bf16[192,512,128]{2,1,0:T(8,128)(2,1)} async-done(((bf16[24,512,128]{2,1,0:T(8,128)(2,1)}), bf16[192,512,128]{2,1,0:T(8,128)(2,1)}) %all-gather.3.cloned.1.call-update) | async-done | bytes 25165840 | tf_op jit(solution)/shard_map/all_gather | solution.py:1473
  155.7 8.0 %shard_map.346 = (bf16[2048,1536]{1,0:T(8,128)(2,1)}, f32[272,1536]{1,0:T(8,128)S(1)}) custom-call(s32[48]{0:T(128)S(1)} %reshape.464.order_ref, bf16[272,2048]{1,0:T(8,128)(2,1)S(1)} %shard_map.345.refs_0_, bf16[192,512,128]{2,1,0:T(8,128)(2,1)} %all-gather.3.cloned.1.call-done.refs_1_.refs_0_, bf16[160,512,128]{2,1,0:T(8,128)(2,1)} %get-tuple-element.246.refs_2_.refs_1_), custom_call_target="tpu_custom_call" | custom-call | flops 1711276032 | bytes 12582912 | tf_op jit(solution)/shard_map/pallas_call | solution.py:894
  163.7 17.1 %shard_map.347 = (f32[4,256,256]{2,1,0:T(8,128)S(1)}, f32[4,256,256]{2,1,0:T(8,128)S(1)}, f32[4,256,128]{2,1,0:T(8,128)S(1)}, bf16[4,128,384]{2,1,0:T(8,128)(2,1)S(1)}) custom-call(f32[272,1536]{1,0:T(8,128)S(1)} %get-tuple-element.247.pv.pk, f32[272,1536]{1,0:T(8,128)S(1)} %get-tuple-element.247.pv.pk, f32[8,1536]{1,0:T(8,128)S(1)} %fusion.34.tv.tk, ...), custom_call_target="tpu_custom_call" | custom-call | tf_op jit(solution)/shard_map/pallas_call | solution.py:245
  190.2 3.8 shard_map.351.refs_1_
  194.2 9.3 %shard_map.349 = (bf16[2048,1536]{1,0:T(8,128)(2,1)}, f32[272,1536]{1,0:T(8,128)S(1)}) custom-call(s32[48]{0:T(128)S(1)} %copy-done.59, bf16[272,2048]{1,0:T(8,128)(2,1)S(1)} %copy-done.10, bf16[192,512,128]{2,1,0:T(8,128)(2,1)} %all-gather.3.cloned.1.call-done.refs_1_.refs_0_, bf16[160,512,128]{2,1,0:T(8,128)(2,1)} %get-tuple-element.246.refs_2_.refs_1_), custom_call_target="tpu_custom_call" | custom-call | flops 1711276032 | bytes 12582912 | tf_op jit(solution)/shard_map/pallas_call | solution.py:894
  203.5 4.5 shard_map.350
  216.8 2.4 collective-permute-start.40
  220.9 8.2 %collective-permute-done.39 = bf16[256,512]{1,0:T(8,128)(2,1)S(1)} collective-permute-done((bf16[256,512]{1,0:T(8,128)(2,1)S(1)}, bf16[256,512]{1,0:T(8,128)(2,1)S(1)}, u32[]{:S(2)}, u32[]{:S(2)}) %collective-permute-start.39) | collective-permute-done | bytes 262176 | tf_op jit(solution)/shard_map/ppermute | solution.py:977
  229.1 9.2 %collective-permute-done.40 = bf16[256,512]{1,0:T(8,128)(2,1)} collective-permute-done((bf16[256,512]{1,0:T(8,128)(2,1)S(1)}, bf16[256,512]{1,0:T(8,128)(2,1)}, u32[]{:S(2)}, u32[]{:S(2)}) %collective-permute-start.40) | collective-permute-done | bytes 262176 | tf_op jit(solution)/shard_map/ppermute | solution.py:977
  240.1 2.4 collective-permute-start.44
  242.5 10.2 %all-gather.5.cloned.1.call-done.refs_0_ = bf16[128,512,128]{2,1,0:T(8,128)(2,1)} async-done(((bf16[16,512,128]{2,1,0:T(8,128)(2,1)}), bf16[128,512,128]{2,1,0:T(8,128)(2,1)}) %all-gather.5.cloned.1.call-update) | async-done | bytes 16777232 | tf_op jit(solution)/shard_map/all_gather | solution.py:1524
  252.7 2.4 collective-permute-start.43
  257.0 4.4 shard_map.356.refs_1_
  261.4 12.0 %shard_map.357.refs_2_ = bf16[2048,2816]{1,0:T(8,128)(2,1)} custom-call(s32[88]{0:T(128)S(1)} %reshape.471.order_ref, bf16[128,512,128]{2,1,0:T(8,128)(2,1)} %all-gather.5.cloned.1.call-done.refs_0_, bf16[192,512,128]{2,1,0:T(8,128)(2,1)} %all-gather.3.cloned.1.call-done.refs_1_.refs_0_, bf16[160,512,128]{2,1,0:T(8,128)(2,1)} %get-tuple-element.280.refs_2_), custom_call_target="tpu_custom_call" | custom-call | bytes 23068672 | tf_op jit(solution)/shard_map/pallas_call | solution.py:894
  277.1 2.4 copy.85.left_ref
  279.5 6.8 %fusion.21 = f32[256,2816]{1,0:T(8,128)S(1)} fusion(bf16[2048,2816]{1,0:T(8,128)(2,1)} %shard_map.357.refs_2_, f32[2048]{0:T(1024)S(1)} %bitcast.214, f32[256]{0:T(256)S(1)} %get-tuple-element.526, bf16[256,512]{1,0:T(8,128)(2,1)} %copy-done.70, bf16[256,512]{1,0:T(8,128)(2,1)} %copy-done.72, bf16[256,512]{1,0:T(8,128)(2,1)} %copy-done.74, ...), kind=kOutput, calls=%fused_computation.80 | convolution fusion | flops 2958557184 | bytes 15475712 | tf_op jit(solution)/shard_map/dot_general | solution.py:1585
  286.3 3.7 multiply_convert_fusion.1
  294.6 4.6 shard_map.361
  299.2 8.5 %shard_map.362 = (bf16[128,512,128]{2,1,0:T(8,128)(2,1)}, bf16[160,512,128]{2,1,0:T(8,128)(2,1)}, bf16[192,512,128]{2,1,0:T(8,128)(2,1)}) custom-call(s32[88]{0:T(128)S(1)} %concatenate.69.positions_ref, bf16[2048,256]{1,0:T(8,128)(2,1)S(1)} %copy-done.19, ...), custom_call_target="tpu_custom_call", output_to_operand_aliasing={{0}: (4, {}), {1}: (5, {}), {2}: (6, {})} | custom-call | flops 2952790016 | bytes 11534336 | tf_op jit(solution)/shard_map/pallas_call | solution.py:1101
  307.9 8.5 %shard_map.363 = (bf16[256,512]{1,0:T(8,128)(2,1)S(1)}, bf16[256,512]{1,0:T(8,128)(2,1)S(1)}, bf16[256,512]{1,0:T(8,128)(2,1)S(1)}, bf16[256,512]{1,0:T(8,128)(2,1)S(1)}) custom-call(s32[1]{0:T(128)} %bitcast.62.part_ref, bf16[256,1408]{1,0:T(8,128)(2,1)S(1)} %copy-done.26, bf16[256,1408]{1,0:T(8,128)(2,1)S(1)} %copy-done.25, ...), custom_call_target="tpu_custom_call" | custom-call | flops 2952790016 | bytes 11534336 | tf_op jit(solution)/shard_map/pallas_call | solution.py:949
  316.8 4.1 collective-permute-start.47
  322.3 6.3 %collective-permute-done.45 = bf16[256,512]{1,0:T(8,128)(2,1)S(1)} collective-permute-done((bf16[256,512]{1,0:T(8,128)(2,1)S(1)}, bf16[256,512]{1,0:T(8,128)(2,1)S(1)}, u32[]{:S(2)}, u32[]{:S(2)}) %collective-permute-start.45) | collective-permute-done | bytes 262176 | tf_op jit(solution)/shard_map/ppermute | solution.py:977
  328.6 9.5 %collective-permute-done.46 = bf16[256,512]{1,0:T(8,128)(2,1)S(1)} collective-permute-done((bf16[256,512]{1,0:T(8,128)(2,1)S(1)}, bf16[256,512]{1,0:T(8,128)(2,1)S(1)}, u32[]{:S(2)}, u32[]{:S(2)}) %collective-permute-start.46) | collective-permute-done | bytes 262176 | tf_op jit(solution)/shard_map/ppermute | solution.py:977
  339.9 4.6 collective-permute-start.52
  344.6 2.5 collective-permute-start.53
  349.3 2.3 collective-permute-start.50
  351.7 15.2 %collective-permute-done.49 = bf16[256,512]{1,0:T(8,128)(2,1)S(1)} collective-permute-done((bf16[256,512]{1,0:T(8,128)(2,1)S(1)}, bf16[256,512]{1,0:T(8,128)(2,1)S(1)}, u32[]{:S(2)}, u32[]{:S(2)}) %collective-permute-start.49) | collective-permute-done | bytes 262176 | tf_op jit(solution)/shard_map/ppermute | solution.py:977
  371.3 2.4 shard_map.364
  376.2 4.7 shard_map.368
  384.7 4.0 shard_map.366
  388.8 4.0 shard_map.367
  394.5 3.9 collective-permute-start.63
  400.9 2.6 shard_map.369.d_leave_ref
  403.5 11.3 %shard_map.370 = (bf16[256,512]{1,0:T(8,128)(2,1)S(1)}, bf16[256,512]{1,0:T(8,128)(2,1)S(1)}, bf16[256,1024]{1,0:T(8,128)(2,1)S(1)}, f32[8,512]{1,0:T(8,128)S(1)...) custom-call(f32[272,1536]{1,0:T(8,128)} %copy-done.3, ...), custom_call_target="tpu_custom_call" | custom-call | tf_op jit(solution)/shard_map/pallas_call | solution.py:673
  419.9 4.0 shard_map.371
  423.9 5.4 shard_map.372
  432.0 8.4 %shard_map.373 = (bf16[256,512]{1,0:T(8,128)(2,1)S(1)}, bf16[256,512]{1,0:T(8,128)(2,1)S(1)}, bf16[256,512]{1,0:T(8,128)(2,1)S(1)}, bf16[256,512]{1,0:T(8,128)(2,1)S(1)}) custom-call(s32[1]{0:T(128)} %bitcast.62.part_ref, bf16[256,1536]{1,0:T(8,128)(2,1)S(1)} %fusion.32.refs_0_, bf16[2048,1536]{1,0:T(8,128)(2,1)} %get-tuple-element.342.refs_1_, ...), custom_call_target="tpu_custom_call" | custom-call | flops 3355443200 | bytes 13107200 | tf_op jit(solution)/shard_map/pallas_call | solution.py:949
  446.3 3.1 collective-permute-done.66
  449.4 2.9 collective-permute-done.67
  452.3 6.4 %collective-permute-done.68 = bf16[256,512]{1,0:T(8,128)(2,1)S(1)} collective-permute-done((bf16[256,512]{1,0:T(8,128)(2,1)S(1)}, bf16[256,512]{1,0:T(8,128)(2,1)S(1)}, u32[]{:S(2)}, u32[]{:S(2)}) %collective-permute-start.68) | collective-permute-done | bytes 262176 | tf_op jit(solution)/shard_map/ppermute | solution.py:977
  458.8 2.7 fusion.19
  461.5 8.2 %collective-permute-start.70 = (f32[4,128]{1,0:T(4,128)S(1)}, f32[4,128]{1,0:T(4,128)S(1)}, u32[]{:S(2)}, u32[]{:S(2)}) collective-permute-start(f32[4,128]{1,0:T(4,128)S(1)} %pad_maximum_fusion.13), channel_id=1, source_target_pairs={{0,16},{8,24},{16,0},{24,8},{1,17},{9,25},{17,1},{25,9},{2,18},{10... | collective-permute-start | bytes 6152 | tf_op jit(solution)/shard_map/ppermute | solution.py:977
  469.8 2.5 collective-permute-start.71
  477.6 2.9 collective-permute-start.73
  480.5 5.9 collective-permute-done.73
  486.5 2.6 collective-permute-start.74
  489.1 2.6 fusion.16
  491.7 3.1 collective-permute-done.74
  494.8 22.8 %shard_map.374 = (f32[44,65536]{1,0:T(8,128)}, f32[44,65536]{1,0:T(8,128)}, f32[44,65536]{1,0:T(8,128)}, f32[44,65536]{1,0:T(8,128)}, bf16[44,65536]{1,0:T(8,128)(2,1)}) custom-call(s32[2]{0:T(128)S(1)} %copy-done.61, s32[48]{0:T(128)S(1)} %copy-done.58, s32[48]{0:T(128)S(1)} %get-tuple-element.239.sources_ref, s32[48]{0:T(128)S(1)} %get-tuple-element.240.rows_ref, ...), custom_call_target="tpu_custom_call" | custom-call | flops 41943040 | bytes 33554432 | tf_op jit(solution)/shard_map/pallas_call | solution.py:1220
  517.6 53.3 %reduce-scatter.6.cloned.1.call-done.refs_2_ = bf16[20,512,128]{2,1,0:T(8,128)(2,1)} async-done(((bf16[160,512,128]{2,1,0:T(8,128)(2,1)}), bf16[20,512,128]{2,1,0:T(8,128)(2,1)}) %reduce-scatter.6.cloned.1.call-update) | async-done | bytes 2621456 | tf_op jit(solution)/shard_map/reduce_scatter | solution.py:1691
  580.2 17.0 %shard_map.375 = (f32[44,65536]{1,0:T(8,128)}, f32[44,65536]{1,0:T(8,128)}, f32[44,65536]{1,0:T(8,128)}, f32[44,65536]{1,0:T(8,128)}, bf16[44,65536]{1,0:T(8,128)(2,1)}) custom-call(s32[2]{0:T(128)S(1)} %copy-done.60, s32[48]{0:T(128)S(1)} %copy-done.58, ...), custom_call_target="tpu_custom_call", output_to_operand_aliasing={{0}: (12, {}), {1}: (13, {}), {2}: (14, {}), {3}: (15, {}),... | custom-call | flops 20971520 | bytes 16777216 | tf_op jit(solution)/shard_map/pallas_call | solution.py:1220
  597.2 4.5 collective-permute-done.77.refs_5_
  602.4 10.4 %shard_map.377 = (f32[44,65536]{1,0:T(8,128)}, f32[44,65536]{1,0:T(8,128)}, f32[44,65536]{1,0:T(8,128)}, f32[44,65536]{1,0:T(8,128)}, bf16[44,65536]{1,0:T(8,128)(2,1)}) custom-call(s32[2]{0:T(128)S(1)} %copy-done.62, s32[48]{0:T(128)S(1)} %copy-done.58, ...), custom_call_target="tpu_custom_call", output_to_operand_aliasing={{0}: (17, {}), {1}: (18, {}), {2}: (19, {}), {3}: (20, {}),... | custom-call | flops 41943040 | bytes 33554432 | tf_op jit(solution)/shard_map/pallas_call | solution.py:1220
  (552 shorter events, 134.2 us)
Async XLA Ops:
  7.2 147.1 %all-gather.3.cloned.1.call-start = ((), (), s32[]{:S(2)}) async-start(), calls=%async_computation.3 | async-start | bytes 28311552 | tf_op jit(solution)/shard_map/all_gather | solution.py:1473
  18.8 233.9 %all-gather.5.cloned.1.call-start = ((), (), s32[]{:S(2)}) async-start(), calls=%async_computation.4 | async-start | bytes 18874368 | tf_op jit(solution)/shard_map/all_gather | solution.py:1524
  23.0 55.0 %collective-permute-start.19 = (bf16[1,1088]{1,0:T(2,128)(2,1)S(1)}, bf16[1,1088]{1,0:T(2,128)(2,1)S(1)}, u32[]{:S(2)}, u32[]{:S(2)}) collective-permute-start(bf16[1,1088]{1,0:T(2,128)(2,1)S(1)} %get-tuple-element.490), channel_id=1, source_target_pairs={{0,16},{8,24},{16,0},{24,8},{1,17},{9,25},{17,1},{25,9},{2,18},{10... | collective-permute-start | bytes 6536 | tf_op jit(solution)/shard_map/ppermute | solution.py:977
  27.1 51.0 %collective-permute-start.18 = (bf16[1,1088]{1,0:T(2,128)(2,1)S(1)}, bf16[1,1088]{1,0:T(2,128)(2,1)S(1)}, u32[]{:S(2)}, u32[]{:S(2)}) collective-permute-start(bf16[1,1088]{1,0:T(2,128)(2,1)S(1)} %get-tuple-element.490), channel_id=1, source_target_pairs={{0,8},{8,0},{16,24},{24,16},{1,9},{9,1},{17,25},{25,17},{2,10},{10... | collective-permute-start | bytes 6536 | tf_op jit(solution)/shard_map/ppermute | solution.py:977
  28.7 49.4 %collective-permute-start.20 = (bf16[1,1088]{1,0:T(2,128)(2,1)S(1)}, bf16[1,1088]{1,0:T(2,128)(2,1)S(1)}, u32[]{:S(2)}, u32[]{:S(2)}) collective-permute-start(bf16[1,1088]{1,0:T(2,128)(2,1)S(1)} %get-tuple-element.490), channel_id=1, source_target_pairs={{0,24},{8,16},{16,8},{24,0},{1,25},{9,17},{17,9},{25,1},{2,26},{10... | collective-permute-start | bytes 6536 | tf_op jit(solution)/shard_map/ppermute | solution.py:977
  28.7 66.6 %collective-permute-start.16 = (bf16[256,512]{1,0:T(8,128)(2,1)S(1)}, bf16[256,512]{1,0:T(8,128)(2,1)S(1)}, u32[]{:S(2)}, u32[]{:S(2)}) collective-permute-start(bf16[256,512]{1,0:T(8,128)(2,1)S(1)} %copy-done.76), channel_id=1, source_target_pairs={{0,16},{8,24},{16,0},{24,8},{1,17},{9,25},{17,1},{25,9},{2,18},{10... | collective-permute-start | bytes 786440 | tf_op jit(solution)/shard_map/ppermute | solution.py:977
  75.5 23.0 %collective-permute-start.15 = (bf16[256,512]{1,0:T(8,128)(2,1)S(1)}, bf16[256,512]{1,0:T(8,128)(2,1)S(1)}, u32[]{:S(2)}, u32[]{:S(2)}) collective-permute-start(bf16[256,512]{1,0:T(8,128)(2,1)S(1)} %copy-done.76), channel_id=1, source_target_pairs={{0,8},{8,0},{16,24},{24,16},{1,9},{9,1},{17,25},{25,17},{2,10},{10... | collective-permute-start | bytes 786440 | tf_op jit(solution)/shard_map/ppermute | solution.py:977
  78.7 5.6 collective-permute-start.22
  80.3 4.0 collective-permute-start.21
  80.3 6.4 %collective-permute-start.24 = (bf16[242,128]{1,0:T(8,128)(2,1)S(1)}, bf16[242,128]{1,0:T(8,128)(2,1)S(1)}, u32[]{:S(2)}, u32[]{:S(2)}) collective-permute-start(bf16[242,128]{1,0:T(8,128)(2,1)S(1)} %bitcast.211), channel_id=1, source_target_pairs={{0,4},{1,5},{2,6},{3,7},{4,0},{5,1},{6,2},{7,3},{8,12},{9,13},{10,... | collective-permute-start | bytes 185864 | tf_op jit(solution)/shard_map/ppermute | solution.py:1010
  84.3 2.6 collective-permute-start.23
  84.3 7.1 %collective-permute-start.26 = (bf16[242,128]{1,0:T(8,128)(2,1)S(1)}, bf16[242,128]{1,0:T(8,128)(2,1)S(1)}, u32[]{:S(2)}, u32[]{:S(2)}) collective-permute-start(bf16[242,128]{1,0:T(8,128)(2,1)S(1)} %bitcast.212), channel_id=1, source_target_pairs={{0,6},{1,7},{2,4},{3,5},{4,2},{5,3},{6,0},{7,1},{8,14},{9,15},{10,... | collective-permute-start | bytes 185864 | tf_op jit(solution)/shard_map/ppermute | solution.py:1010
  86.7 4.7 collective-permute-start.25
  87.0 11.5 %collective-permute-start.17 = (bf16[256,512]{1,0:T(8,128)(2,1)S(1)}, bf16[256,512]{1,0:T(8,128)(2,1)S(1)}, u32[]{:S(2)}, u32[]{:S(2)}) collective-permute-start(bf16[256,512]{1,0:T(8,128)(2,1)S(1)} %copy-done.76), channel_id=1, source_target_pairs={{0,24},{8,16},{16,8},{24,0},{1,25},{9,17},{17,9},{25,1},{2,26},{10... | collective-permute-start | bytes 786440 | tf_op jit(solution)/shard_map/ppermute | solution.py:977
  91.5 26.7 %collective-permute-start.30 = (bf16[256,512]{1,0:T(8,128)(2,1)S(1)}, bf16[256,512]{1,0:T(8,128)(2,1)S(1)}, u32[]{:S(2)}, u32[]{:S(2)}) collective-permute-start(bf16[256,512]{1,0:T(8,128)(2,1)S(1)} %copy-done.79), channel_id=1, source_target_pairs={{0,16},{8,24},{16,0},{24,8},{1,17},{9,25},{17,1},{25,9},{2,18},{10... | collective-permute-start | bytes 786440 | tf_op jit(solution)/shard_map/ppermute | solution.py:977
  95.1 23.0 %collective-permute-start.29 = (bf16[256,512]{1,0:T(8,128)(2,1)S(1)}, bf16[256,512]{1,0:T(8,128)(2,1)}, u32[]{:S(2)}, u32[]{:S(2)}) collective-permute-start(bf16[256,512]{1,0:T(8,128)(2,1)S(1)} %copy-done.79), channel_id=1, source_target_pairs={{0,8},{8,0},{16,24},{24,16},{1,9},{9,1},{17,25},{25,17},{2,10},{10... | collective-permute-start | bytes 786440 | tf_op jit(solution)/shard_map/ppermute | solution.py:977
  95.2 22.9 %collective-permute-start.31 = (bf16[256,512]{1,0:T(8,128)(2,1)S(1)}, bf16[256,512]{1,0:T(8,128)(2,1)}, u32[]{:S(2)}, u32[]{:S(2)}) collective-permute-start(bf16[256,512]{1,0:T(8,128)(2,1)S(1)} %copy-done.79), channel_id=1, source_target_pairs={{0,24},{8,16},{16,8},{24,0},{1,25},{9,17},{17,9},{25,1},{2,26},{10... | collective-permute-start | bytes 786440 | tf_op jit(solution)/shard_map/ppermute | solution.py:977
  98.4 26.6 %collective-permute-start.14 = (bf16[4,512,128]{2,1,0:T(8,128)(2,1)}, bf16[4,512,128]{2,1,0:T(8,128)(2,1)}, u32[]{:S(2)}, u32[]{:S(2)}) collective-permute-start(bf16[4,512,128]{2,1,0:T(8,128)(2,1)} %slice.301), channel_id=1, source_target_pairs={{0,1},{1,0},{2,3},{3,2},{4,5},{5,4},{6,7},{7,6},{8,9},{9,8},{10,11... | collective-permute-start | bytes 1572872 | tf_op jit(solution)/shard_map/ppermute | solution.py:1477
  120.5 3.0 collective-permute-start.28
  155.0 275.8 %reduce-scatter.4.cloned.1.call-start = ((), (), s32[]{:S(2)}) async-start(), calls=%async_computation.5 | async-start | bytes 18874368 | tf_op jit(solution)/shard_map/reduce_scatter | solution.py:1625
  186.2 21.9 %collective-permute-start.35 = (bf16[2,128,384]{2,1,0:T(8,128)(2,1)}, bf16[2,128,384]{2,1,0:T(8,128)(2,1)}, u32[]{:S(2)}, u32[]{:S(2)}) collective-permute-start(bf16[2,128,384]{2,1,0:T(8,128)(2,1)} %shard_map.348), channel_id=1, source_target_pairs={{0,6},{1,7},{2,4},{3,5},{4,2},{5,3},{6,0},{7,1},{8,14},{9,15},{10,... | collective-permute-start | bytes 589832 | tf_op jit(solution)/shard_map/ppermute | solution.py:415
  187.6 20.4 %collective-permute-start.34 = (bf16[2,128,384]{2,1,0:T(8,128)(2,1)}, bf16[2,128,384]{2,1,0:T(8,128)(2,1)}, u32[]{:S(2)}, u32[]{:S(2)}) collective-permute-start(bf16[2,128,384]{2,1,0:T(8,128)(2,1)} %shard_map.348), channel_id=1, source_target_pairs={{0,4},{1,5},{2,6},{3,7},{4,0},{5,1},{6,2},{7,3},{8,12},{9,13},{10,... | collective-permute-start | bytes 589832 | tf_op jit(solution)/shard_map/ppermute | solution.py:415
  187.9 20.1 %collective-permute-start.33 = (bf16[2,128,384]{2,1,0:T(8,128)(2,1)}, bf16[2,128,384]{2,1,0:T(8,128)(2,1)}, u32[]{:S(2)}, u32[]{:S(2)}) collective-permute-start(bf16[2,128,384]{2,1,0:T(8,128)(2,1)} %shard_map.348), channel_id=1, source_target_pairs={{0,2},{1,3},{2,0},{3,1},{4,6},{5,7},{6,4},{7,5},{8,10},{9,11},{10,... | collective-permute-start | bytes 589832 | tf_op jit(solution)/shard_map/ppermute | solution.py:415
  208.2 1.9 collective-permute-start.37
  215.1 14.0 %collective-permute-start.39 = (bf16[256,512]{1,0:T(8,128)(2,1)S(1)}, bf16[256,512]{1,0:T(8,128)(2,1)S(1)}, u32[]{:S(2)}, u32[]{:S(2)}) collective-permute-start(bf16[256,512]{1,0:T(8,128)(2,1)S(1)} %get-tuple-element.271), channel_id=1, source_target_pairs={{0,8},{8,0},{16,24},{24,16},{1,9},{9,1},{17,25},{25,17},{2,10},{10... | collective-permute-start | bytes 786440 | tf_op jit(solution)/shard_map/ppermute | solution.py:977
  216.8 21.4 %collective-permute-start.40 = (bf16[256,512]{1,0:T(8,128)(2,1)S(1)}, bf16[256,512]{1,0:T(8,128)(2,1)}, u32[]{:S(2)}, u32[]{:S(2)}) collective-permute-start(bf16[256,512]{1,0:T(8,128)(2,1)S(1)} %get-tuple-element.272), channel_id=1, source_target_pairs={{0,16},{8,24},{16,0},{24,8},{1,17},{9,25},{17,1},{25,9},{2,18},{10... | collective-permute-start | bytes 786440 | tf_op jit(solution)/shard_map/ppermute | solution.py:977
  219.2 19.0 %collective-permute-start.41 = (bf16[256,512]{1,0:T(8,128)(2,1)S(1)}, bf16[256,512]{1,0:T(8,128)(2,1)}, u32[]{:S(2)}, u32[]{:S(2)}) collective-permute-start(bf16[256,512]{1,0:T(8,128)(2,1)S(1)} %get-tuple-element.273), channel_id=1, source_target_pairs={{0,24},{8,16},{16,8},{24,0},{1,25},{9,17},{17,9},{25,1},{2,26},{10... | collective-permute-start | bytes 786440 | tf_op jit(solution)/shard_map/ppermute | solution.py:977
  240.1 33.3 %collective-permute-start.44 = (bf16[256,512]{1,0:T(8,128)(2,1)}, bf16[256,512]{1,0:T(8,128)(2,1)}, u32[]{:S(2)}, u32[]{:S(2)}) collective-permute-start(bf16[256,512]{1,0:T(8,128)(2,1)} %fusion.39), channel_id=1, source_target_pairs={{0,24},{8,16},{16,8},{24,0},{1,25},{9,17},{17,9},{25,1},{2,26},{10... | collective-permute-start | bytes 786440 | tf_op jit(solution)/shard_map/ppermute | solution.py:977
  252.7 20.8 %collective-permute-start.43 = (bf16[256,512]{1,0:T(8,128)(2,1)}, bf16[256,512]{1,0:T(8,128)(2,1)S(1)}, u32[]{:S(2)}, u32[]{:S(2)}) collective-permute-start(bf16[256,512]{1,0:T(8,128)(2,1)} %fusion.39), channel_id=1, source_target_pairs={{0,16},{8,24},{16,0},{24,8},{1,17},{9,25},{17,1},{25,9},{2,18},{10... | collective-permute-start | bytes 786440 | tf_op jit(solution)/shard_map/ppermute | solution.py:977
  255.1 18.4 %collective-permute-start.42 = (bf16[256,512]{1,0:T(8,128)(2,1)}, bf16[256,512]{1,0:T(8,128)(2,1)S(1)}, u32[]{:S(2)}, u32[]{:S(2)}) collective-permute-start(bf16[256,512]{1,0:T(8,128)(2,1)} %fusion.39), channel_id=1, source_target_pairs={{0,8},{8,0},{16,24},{24,16},{1,9},{9,1},{17,25},{25,17},{2,10},{10... | collective-permute-start | bytes 786440 | tf_op jit(solution)/shard_map/ppermute | solution.py:977
  307.7 263.2 %reduce-scatter.6.cloned.1.call-start = ((), (), s32[]{:S(2)}) async-start(), calls=%async_computation.6 | async-start | bytes 23592960 | tf_op jit(solution)/shard_map/reduce_scatter | solution.py:1691
  316.4 12.2 %collective-permute-start.45 = (bf16[256,512]{1,0:T(8,128)(2,1)S(1)}, bf16[256,512]{1,0:T(8,128)(2,1)S(1)}, u32[]{:S(2)}, u32[]{:S(2)}) collective-permute-start(bf16[256,512]{1,0:T(8,128)(2,1)S(1)} %get-tuple-element.297), channel_id=1, source_target_pairs={{0,8},{8,0},{16,24},{24,16},{1,9},{9,1},{17,25},{25,17},{2,10},{10... | collective-permute-start | bytes 786440 | tf_op jit(solution)/shard_map/ppermute | solution.py:977
  316.7 21.4 %collective-permute-start.46 = (bf16[256,512]{1,0:T(8,128)(2,1)S(1)}, bf16[256,512]{1,0:T(8,128)(2,1)S(1)}, u32[]{:S(2)}, u32[]{:S(2)}) collective-permute-start(bf16[256,512]{1,0:T(8,128)(2,1)S(1)} %get-tuple-element.298), channel_id=1, source_target_pairs={{0,16},{8,24},{16,0},{24,8},{1,17},{9,25},{17,1},{25,9},{2,18},{10... | collective-permute-start | bytes 786440 | tf_op jit(solution)/shard_map/ppermute | solution.py:977
  316.8 21.3 %collective-permute-start.47 = (bf16[256,512]{1,0:T(8,128)(2,1)S(1)}, bf16[256,512]{1,0:T(8,128)(2,1)S(1)}, u32[]{:S(2)}, u32[]{:S(2)}) collective-permute-start(bf16[256,512]{1,0:T(8,128)(2,1)S(1)} %get-tuple-element.299), channel_id=1, source_target_pairs={{0,24},{8,16},{16,8},{24,0},{1,25},{9,17},{17,9},{25,1},{2,26},{10... | collective-permute-start | bytes 786440 | tf_op jit(solution)/shard_map/ppermute | solution.py:977
  339.9 9.4 %collective-permute-start.52 = (f32[2,128]{1,0:T(2,128)S(1)}, f32[2,128]{1,0:T(2,128)S(1)}, u32[]{:S(2)}, u32[]{:S(2)}) collective-permute-start(f32[2,128]{1,0:T(2,128)S(1)} %bitcast.234), channel_id=1, source_target_pairs={{0,16},{8,24},{16,0},{24,8},{1,17},{9,25},{17,1},{25,9},{2,18},{10... | collective-permute-start | bytes 3080 | tf_op jit(solution)/shard_map/ppermute | solution.py:977
  344.6 7.1 %collective-permute-start.53 = (f32[2,128]{1,0:T(2,128)S(1)}, f32[2,128]{1,0:T(2,128)S(1)}, u32[]{:S(2)}, u32[]{:S(2)}) collective-permute-start(f32[2,128]{1,0:T(2,128)S(1)} %bitcast.235), channel_id=1, source_target_pairs={{0,24},{8,16},{16,8},{24,0},{1,25},{9,17},{17,9},{25,1},{2,26},{10... | collective-permute-start | bytes 3080 | tf_op jit(solution)/shard_map/ppermute | solution.py:977
  347.1 4.6 collective-permute-start.51
  347.2 19.7 %collective-permute-start.49 = (bf16[256,512]{1,0:T(8,128)(2,1)S(1)}, bf16[256,512]{1,0:T(8,128)(2,1)S(1)}, u32[]{:S(2)}, u32[]{:S(2)}) collective-permute-start(bf16[256,512]{1,0:T(8,128)(2,1)S(1)} %convert_element_type.217), channel_id=1, source_target_pairs={{0,16},{8,24},{16,0},{24,8},{1,17},{9,25},{17,1},{25,9},{2,18},{10... | collective-permute-start | bytes 786440 | tf_op jit(solution)/shard_map/ppermute | solution.py:977
  349.1 17.8 %collective-permute-start.48 = (bf16[256,512]{1,0:T(8,128)(2,1)S(1)}, bf16[256,512]{1,0:T(8,128)(2,1)S(1)}, u32[]{:S(2)}, u32[]{:S(2)}) collective-permute-start(bf16[256,512]{1,0:T(8,128)(2,1)S(1)} %convert_element_type.217), channel_id=1, source_target_pairs={{0,8},{8,0},{16,24},{24,16},{1,9},{9,1},{17,25},{25,17},{2,10},{10... | collective-permute-start | bytes 786440 | tf_op jit(solution)/shard_map/ppermute | solution.py:977
  349.3 17.6 %collective-permute-start.50 = (bf16[256,512]{1,0:T(8,128)(2,1)S(1)}, bf16[256,512]{1,0:T(8,128)(2,1)S(1)}, u32[]{:S(2)}, u32[]{:S(2)}) collective-permute-start(bf16[256,512]{1,0:T(8,128)(2,1)S(1)} %convert_element_type.217), channel_id=1, source_target_pairs={{0,24},{8,16},{16,8},{24,0},{1,25},{9,17},{17,9},{25,1},{2,26},{10... | collective-permute-start | bytes 786440 | tf_op jit(solution)/shard_map/ppermute | solution.py:977
  374.7 6.2 %collective-permute-start.54 = (bf16[4,128,256]{2,1,0:T(8,128)(2,1)S(1)}, bf16[4,128,256]{2,1,0:T(8,128)(2,1)S(1)}, u32[]{:S(2)}, u32[]{:S(2)}) collective-permute-start(bf16[4,128,256]{2,1,0:T(8,128)(2,1)S(1)} %get-tuple-element.302.refs_0_), channel_id=1, source_target_pairs={{0,1},{1,0},{2,3},{3,2},{4,5},{5,4},{6,7},{7,6},{8,9},{9,8},{10,11... | collective-permute-start | bytes 786440 | tf_op jit(solution)/shard_map/ppermute | solution.py:415
  381.2 11.7 %collective-permute-start.57 = (bf16[2,128,256]{2,1,0:T(8,128)(2,1)S(1)}, bf16[2,128,256]{2,1,0:T(8,128)(2,1)S(1)}, u32[]{:S(2)}, u32[]{:S(2)}) collective-permute-start(bf16[2,128,256]{2,1,0:T(8,128)(2,1)S(1)} %shard_map.365), channel_id=1, source_target_pairs={{0,6},{1,7},{2,4},{3,5},{4,2},{5,3},{6,0},{7,1},{8,14},{9,15},{10,... | collective-permute-start | bytes 393224 | tf_op jit(solution)/shard_map/ppermute | solution.py:415
  382.2 11.5 %collective-permute-start.56 = (bf16[2,128,256]{2,1,0:T(8,128)(2,1)S(1)}, bf16[2,128,256]{2,1,0:T(8,128)(2,1)S(1)}, u32[]{:S(2)}, u32[]{:S(2)}) collective-permute-start(bf16[2,128,256]{2,1,0:T(8,128)(2,1)S(1)} %shard_map.365), channel_id=1, source_target_pairs={{0,4},{1,5},{2,6},{3,7},{4,0},{5,1},{6,2},{7,3},{8,12},{9,13},{10,... | collective-permute-start | bytes 393224 | tf_op jit(solution)/shard_map/ppermute | solution.py:415
  384.1 9.6 %collective-permute-start.55 = (bf16[2,128,256]{2,1,0:T(8,128)(2,1)S(1)}, bf16[2,128,256]{2,1,0:T(8,128)(2,1)S(1)}, u32[]{:S(2)}, u32[]{:S(2)}) collective-permute-start(bf16[2,128,256]{2,1,0:T(8,128)(2,1)S(1)} %shard_map.365), channel_id=1, source_target_pairs={{0,2},{1,3},{2,0},{3,1},{4,6},{5,7},{6,4},{7,5},{8,10},{9,11},{10,... | collective-permute-start | bytes 393224 | tf_op jit(solution)/shard_map/ppermute | solution.py:415
  393.7 5.0 collective-permute-start.58
  393.8 7.0 %collective-permute-start.59 = (bf16[2,128,256]{2,1,0:T(8,128)(2,1)S(1)}, bf16[2,128,256]{2,1,0:T(8,128)(2,1)S(1)}, u32[]{:S(2)}, u32[]{:S(2)}) collective-permute-start(bf16[2,128,256]{2,1,0:T(8,128)(2,1)S(1)} %collective-permute-done.56.refs_10_), channel_id=1, source_target_pairs={{0,1},{1,0},{2,3},{3,2},{4,5},{5,4},{6,7},{7,6},{8,9},{9,8},{10,11... | collective-permute-start | bytes 393224 | tf_op jit(solution)/shard_map/ppermute | solution.py:415
  394.2 6.6 %collective-permute-start.60 = (bf16[2,128,256]{2,1,0:T(8,128)(2,1)S(1)}, bf16[2,128,256]{2,1,0:T(8,128)(2,1)S(1)}, u32[]{:S(2)}, u32[]{:S(2)}) collective-permute-start(bf16[2,128,256]{2,1,0:T(8,128)(2,1)S(1)} %collective-permute-done.57.refs_12_), channel_id=1, source_target_pairs={{0,1},{1,0},{2,3},{3,2},{4,5},{5,4},{6,7},{7,6},{8,9},{9,8},{10,11... | collective-permute-start | bytes 393224 | tf_op jit(solution)/shard_map/ppermute | solution.py:415
  394.5 34.9 %collective-permute-start.63 = (bf16[256,512]{1,0:T(8,128)(2,1)S(1)}, bf16[256,512]{1,0:T(8,128)(2,1)S(1)}, u32[]{:S(2)}, u32[]{:S(2)}) collective-permute-start(bf16[256,512]{1,0:T(8,128)(2,1)S(1)} %get-tuple-element.333), channel_id=1, source_target_pairs={{0,8},{8,0},{16,24},{24,16},{1,9},{9,1},{17,25},{25,17},{2,10},{10... | collective-permute-start | bytes 786440 | tf_op jit(solution)/shard_map/ppermute | solution.py:977
  398.4 31.0 %collective-permute-start.64 = (bf16[256,512]{1,0:T(8,128)(2,1)S(1)}, bf16[256,512]{1,0:T(8,128)(2,1)S(1)}, u32[]{:S(2)}, u32[]{:S(2)}) collective-permute-start(bf16[256,512]{1,0:T(8,128)(2,1)S(1)} %get-tuple-element.334), channel_id=1, source_target_pairs={{0,16},{8,24},{16,0},{24,8},{1,17},{9,25},{17,1},{25,9},{2,18},{10... | collective-permute-start | bytes 786440 | tf_op jit(solution)/shard_map/ppermute | solution.py:977
  398.7 32.1 %collective-permute-start.65 = (bf16[256,512]{1,0:T(8,128)(2,1)S(1)}, bf16[256,512]{1,0:T(8,128)(2,1)}, u32[]{:S(2)}, u32[]{:S(2)}) collective-permute-start(bf16[256,512]{1,0:T(8,128)(2,1)S(1)} %get-tuple-element.335), channel_id=1, source_target_pairs={{0,24},{8,16},{16,8},{24,0},{1,25},{9,17},{17,9},{25,1},{2,26},{10... | collective-permute-start | bytes 786440 | tf_op jit(solution)/shard_map/ppermute | solution.py:977
  414.8 3.1 collective-permute-start.62
  416.2 3.7 collective-permute-start.61
  440.5 8.9 %collective-permute-start.66 = (bf16[256,512]{1,0:T(8,128)(2,1)S(1)}, bf16[256,512]{1,0:T(8,128)(2,1)S(1)}, u32[]{:S(2)}, u32[]{:S(2)}) collective-permute-start(bf16[256,512]{1,0:T(8,128)(2,1)S(1)} %get-tuple-element.346), channel_id=1, source_target_pairs={{0,8},{8,0},{16,24},{24,16},{1,9},{9,1},{17,25},{25,17},{2,10},{10... | collective-permute-start | bytes 786440 | tf_op jit(solution)/shard_map/ppermute | solution.py:977
  441.9 10.4 %collective-permute-start.67 = (bf16[256,512]{1,0:T(8,128)(2,1)S(1)}, bf16[256,512]{1,0:T(8,128)(2,1)S(1)}, u32[]{:S(2)}, u32[]{:S(2)}) collective-permute-start(bf16[256,512]{1,0:T(8,128)(2,1)S(1)} %get-tuple-element.347), channel_id=1, source_target_pairs={{0,16},{8,24},{16,0},{24,8},{1,17},{9,25},{17,1},{25,9},{2,18},{10... | collective-permute-start | bytes 786440 | tf_op jit(solution)/shard_map/ppermute | solution.py:977
  442.8 15.9 %collective-permute-start.68 = (bf16[256,512]{1,0:T(8,128)(2,1)S(1)}, bf16[256,512]{1,0:T(8,128)(2,1)S(1)}, u32[]{:S(2)}, u32[]{:S(2)}) collective-permute-start(bf16[256,512]{1,0:T(8,128)(2,1)S(1)} %get-tuple-element.348), channel_id=1, source_target_pairs={{0,24},{8,16},{16,8},{24,0},{1,25},{9,17},{17,9},{25,1},{2,26},{10... | collective-permute-start | bytes 786440 | tf_op jit(solution)/shard_map/ppermute | solution.py:977
  461.5 13.4 %collective-permute-start.70 = (f32[4,128]{1,0:T(4,128)S(1)}, f32[4,128]{1,0:T(4,128)S(1)}, u32[]{:S(2)}, u32[]{:S(2)}) collective-permute-start(f32[4,128]{1,0:T(4,128)S(1)} %pad_maximum_fusion.13), channel_id=1, source_target_pairs={{0,16},{8,24},{16,0},{24,8},{1,17},{9,25},{17,1},{25,9},{2,18},{10... | collective-permute-start | bytes 6152 | tf_op jit(solution)/shard_map/ppermute | solution.py:977
  469.8 5.4 collective-permute-start.71
  472.2 3.6 collective-permute-start.69
  477.6 8.8 %collective-permute-start.73 = (f32[208,128]{1,0:T(8,128)S(1)}, f32[208,128]{1,0:T(8,128)S(1)}, u32[]{:S(2)}, u32[]{:S(2)}) collective-permute-start(f32[208,128]{1,0:T(8,128)S(1)} %bitcast_add_fusion), channel_id=1, source_target_pairs={{0,2},{1,3},{2,0},{3,1},{4,6},{5,7},{6,4},{7,5},{8,10},{9,11},{10,... | collective-permute-start | bytes 319496 | tf_op jit(solution)/shard_map/ppermute | solution.py:1740
  486.5 8.3 %collective-permute-start.74 = (f32[208,128]{1,0:T(8,128)S(1)}, f32[208,128]{1,0:T(8,128)S(1)}, u32[]{:S(2)}, u32[]{:S(2)}) collective-permute-start(f32[208,128]{1,0:T(8,128)S(1)} %fusion.102), channel_id=1, source_target_pairs={{0,4},{1,5},{2,6},{3,7},{4,0},{5,1},{6,2},{7,3},{8,12},{9,13},{10,... | collective-permute-start | bytes 319496 | tf_op jit(solution)/shard_map/ppermute | solution.py:1740
  573.1 28.7 %collective-permute-start.75 = (bf16[6,512,128]{2,1,0:T(8,128)(2,1)}, bf16[6,512,128]{2,1,0:T(8,128)(2,1)S(1)}, u32[]{:S(2)}, u32[]{:S(2)}) collective-permute-start(bf16[6,512,128]{2,1,0:T(8,128)(2,1)} %slice.273), channel_id=1, source_target_pairs={{0,1},{1,0},{2,3},{3,2},{4,5},{5,4},{6,7},{7,6},{8,9},{9,8},{10,11... | collective-permute-start | bytes 2359304 | tf_op jit(solution)/shard_map/ppermute | solution.py:415
  574.9 22.3 %collective-permute-start.78 = (bf16[4,512,128]{2,1,0:T(8,128)(2,1)}, bf16[4,512,128]{2,1,0:T(8,128)(2,1)}, u32[]{:S(2)}, u32[]{:S(2)}) collective-permute-start(bf16[4,512,128]{2,1,0:T(8,128)(2,1)} %slice.274), channel_id=1, source_target_pairs={{0,6},{1,7},{2,4},{3,5},{4,2},{5,3},{6,0},{7,1},{8,14},{9,15},{10,... | collective-permute-start | bytes 1572872 | tf_op jit(solution)/shard_map/ppermute | solution.py:415
  576.4 25.3 %collective-permute-start.77 = (bf16[4,512,128]{2,1,0:T(8,128)(2,1)}, bf16[4,512,128]{2,1,0:T(8,128)(2,1)}, u32[]{:S(2)}, u32[]{:S(2)}) collective-permute-start(bf16[4,512,128]{2,1,0:T(8,128)(2,1)} %slice.274), channel_id=1, source_target_pairs={{0,4},{1,5},{2,6},{3,7},{4,0},{5,1},{6,2},{7,3},{8,12},{9,13},{10,... | collective-permute-start | bytes 1572872 | tf_op jit(solution)/shard_map/ppermute | solution.py:415
  577.8 24.0 %collective-permute-start.76 = (bf16[4,512,128]{2,1,0:T(8,128)(2,1)}, bf16[4,512,128]{2,1,0:T(8,128)(2,1)}, u32[]{:S(2)}, u32[]{:S(2)}) collective-permute-start(bf16[4,512,128]{2,1,0:T(8,128)(2,1)} %slice.274), channel_id=1, source_target_pairs={{0,2},{1,3},{2,0},{3,1},{4,6},{5,7},{6,4},{7,5},{8,10},{9,11},{10,... | collective-permute-start | bytes 1572872 | tf_op jit(solution)/shard_map/ppermute | solution.py:415
  (125 other events, 1868.6 us)
Sparse Core Ops, SparseCore 0:
  18.9 135.2 all-gather.2
  156.7 95.9 all-gather.4
  307.8 118.9 reduce-scatter.3
  430.9 139.9 reduce-scatter.5
